TPU v7x, 32 devices: a whole 2x2x4 slice. The times are simulated.
32 devices in a mesh: gx: 8 (over z, y), gy: 4 (over x, core).
Axes of the slice: x: 2, y: 2, z: 4, core: 2. Of those that a mesh axis runs over, the one named last changes fastest.
Arguments:
- displacement: float32 [3, 256, 96, 128], P(None, 'gx', 'gy'), may hold values from -6 to 6
- density: float32 [256, 96, 128], P('gx', 'gy'), may hold values from 0.05 to 1
- element_kind: int32 [256, 96, 128], P('gx', 'gy'), may hold values from 0 to 7
- load_x: int32 [1024], replicated, may hold values from 0 to 255
- load_y: int32 [1024], replicated, may hold values from 0 to 95
- load_z: int32 [1024], replicated, may hold values from 0 to 127
- load_force: float32 [3, 1024], replicated, may hold values from -8 to 8
Outputs:
- sensitivity: float32 [256, 96, 128], P('gx', 'gy')
- residual: float32 [3, 256, 96, 128], P(None, 'gx', 'gy')
- compliance: float32 [], replicated
- volume: float32 [], replicated
Inputs may be any that keep to these rules, and one draw needn't show every extreme that they name: `element_kind`: 1 marks a passive void element, 2 a passive solid element, any other value a design element. `load_x`: each load acts on one node; several loads may share a node.
All inputs are finite; a program needn't handle non-finite values.
Results may differ from a plain program's by a relative error of at most 0.0001.
Values sent between devices are 32-bit elements; how exact they have to be, the bound alone decides.
No kernel may reach another device: no remote copies, remote signals or barrier semaphores. Data moves between devices by JAX's collectives and lax.ppermute only.
A program may use at most 128 MiB of HBM per device.

v0:
```python
import functools

import jax
import jax.numpy as jnp
import numpy as np
from jax import lax
from jax.experimental import pallas as pl
from jax.experimental.pallas import tpu as pltpu
from jax.sharding import PartitionSpec as P

RADIUS = 3
PENALTY = 3.0
STIFF_FLOOR = 0.001
POISSON = 0.3
HALO = 8
BOTH = ("gx", "gy")
FULL = jax.ShapeDtypeStruct


def element_matrix():
    lame_first = POISSON / ((1.0 + POISSON) * (1.0 - 2.0 * POISSON))
    shear_modulus = 0.5 / (1.0 + POISSON)
    material = np.zeros((6, 6))
    material[:3, :3] = lame_first
    for diagonal in range(3):
        material[diagonal, diagonal] += 2.0 * shear_modulus
        material[diagonal + 3, diagonal + 3] = shear_modulus
    points = [0.5 - 0.5 / np.sqrt(3.0), 0.5 + 0.5 / np.sqrt(3.0)]
    corners = [(a, b, e) for a in (0, 1) for b in (0, 1) for e in (0, 1)]
    result = np.zeros((24, 24))
    for point_x in points:
        for point_y in points:
            for point_z in points:
                strain = np.zeros((6, 24))
                for corner, (side_x, side_y, side_z) in enumerate(corners):
                    value_x = point_x if side_x else 1.0 - point_x
                    value_y = point_y if side_y else 1.0 - point_y
                    value_z = point_z if side_z else 1.0 - point_z
                    slope_x = (1.0 if side_x else -1.0) * value_y * value_z
                    slope_y = value_x * (1.0 if side_y else -1.0) * value_z
                    slope_z = value_x * value_y * (1.0 if side_z else -1.0)
                    column = 3 * corner
                    strain[0, column] = slope_x
                    strain[1, column + 1] = slope_y
                    strain[2, column + 2] = slope_z
                    strain[3, column] = slope_y
                    strain[3, column + 1] = slope_x
                    strain[4, column + 1] = slope_z
                    strain[4, column + 2] = slope_y
                    strain[5, column + 2] = slope_x
                    strain[5, column] = slope_z
                result += strain.T @ material @ strain / 8.0
    return result


def modal_matrix():
    pair = np.array([[1.0, 1.0], [-1.0, 1.0]])
    turn = np.kron(np.kron(np.kron(pair, pair), pair), np.eye(3))
    return turn @ element_matrix() @ turn.T / 64.0


SHEARS = ((3, 14), (4, 8), (6, 13))
NORMALS = (5, 7, 12)
PAIRS = ((10, 15), (11, 18), (17, 19))
TRIO = (9, 16, 20)
LASTS = (21, 22, 23)


def modal_constants():
    modal = modal_matrix()
    known = np.zeros((24, 24))
    shear = modal[3, 3]
    for first, second in SHEARS:
        known[np.ix_((first, second), (first, second))] = shear
    normal_off = modal[5, 7]
    normal_own = modal[5, 5] - normal_off
    known[np.ix_(NORMALS, NORMALS)] = normal_off
    pair_off = modal[10, 15]
    pair_own = modal[10, 10] - pair_off
    for both in PAIRS:
        known[np.ix_(both, both)] = pair_off
    trio = modal[9, 16]
    known[np.ix_(TRIO, TRIO)] = trio
    last = modal[21, 21]
    for group, own in ((NORMALS, normal_own), (sum(PAIRS, ()), pair_own), (TRIO, trio), (LASTS, last)):
        for degree in group:
            known[degree, degree] += own
    assert np.abs(known - modal).max() < 1e-12
    return tuple(float(v) for v in (shear, normal_off, normal_own, pair_off, pair_own, trio, last))


def weight_of(square):
    return max(0.0, RADIUS + 0.5 - float(np.sqrt(square)))


CLASSES = (0, 1, 2, 4, 5, 8, 9, 10)


def stiffness_of(physical):
    return STIFF_FLOOR + (1.0 - STIFF_FLOOR) * (physical * physical * physical)


def physical_of(density, kind):
    return jnp.where(kind == 1, 0.0, jnp.where(kind == 2, 1.0, density))


def factor_of(physical, kind):
    design = (kind != 1) & (kind != 2)
    return jnp.where(design, (-PENALTY * (1.0 - STIFF_FLOOR)) * (physical * physical), 0.0)


def pack_y(rows, cols, disp, dens, kind, out_a, out_b, vol):
    depth = disp.shape[-1]

    def column(ref, index):
        return ref[pl.ds(index, rows, stride=cols), :]

    def state(index):
        code = column(kind, index)
        physical = physical_of(column(dens, index), code)
        return physical, code

    def fill(low, high):
        slot = 0
        for c in range(3):
            for index in range(RADIUS + 1):
                low[pl.ds(slot * rows, rows), :] = disp[pl.ds(c * rows * cols + index, rows, stride=cols), :]
                slot += 1
        for index in range(RADIUS):
            low[pl.ds(slot * rows, rows), :] = factor_of(*state(index))
            slot += 1
        slot = 0
        for c in range(3):
            for index in range(cols - RADIUS, cols):
                high[pl.ds(slot * rows, rows), :] = disp[pl.ds(c * rows * cols + index, rows, stride=cols), :]
                slot += 1
        for index in range(cols - RADIUS, cols):
            physical, code = state(index)
            high[pl.ds(slot * rows, rows), :] = factor_of(physical, code)
            slot += 1
        high[pl.ds(slot * rows, rows), :] = stiffness_of(physical)

    odd = lax.axis_index("gy") % 2

    @pl.when(odd == 0)
    def _():
        fill(out_b, out_a)

    @pl.when(odd == 1)
    def _():
        fill(out_a, out_b)

    def add(step, total):
        at = pl.ds(pl.multiple_of(step * 32, 32), 32)
        return total + physical_of(dens[at, :], kind[at, :])

    total = lax.fori_loop(0, rows * cols // 32, add, jnp.zeros((32, depth), jnp.float32), unroll=4)
    vol[...] = jnp.sum(total.reshape(4, 8, depth), axis=0)


def unpack_y(rows, cols, count_y, disp, dens, kind, got_a, got_b, edge_u, edge_f, edge_s, out_a, out_b):
    here = lax.axis_index("gy")
    depth = disp.shape[-1]
    has_low = here > 0
    has_high = here < count_y - 1

    def fill(low, high):
        def put(ref, start, sublane, value):
            ref[pl.ds(start + sublane, rows, stride=HALO), :] = value

        zero = jnp.zeros((rows, depth), jnp.float32)
        slot = 0
        for c in range(3):
            for index in range(RADIUS + 1):
                put(edge_u, c * rows * HALO, index, jnp.where(has_high, high[pl.ds(slot * rows, rows), :], 0.0))
                slot += 1
        for index in range(RADIUS):
            put(edge_f, 0, index, jnp.where(has_high, high[pl.ds(slot * rows, rows), :], 0.0))
            slot += 1
        slot = 0
        for c in range(3):
            put(edge_u, c * rows * HALO, RADIUS + 1, zero)
            for index in range(HALO - RADIUS, HALO):
                put(edge_u, c * rows * HALO, index, low[pl.ds(slot * rows, rows), :])
                slot += 1
        for index in range(RADIUS, HALO - RADIUS):
            put(edge_f, 0, index, zero)
        for index in range(HALO - RADIUS, HALO):
            put(edge_f, 0, index, jnp.where(has_low, low[pl.ds(slot * rows, rows), :], 0.0))
            slot += 1
        edge_s[...] = jnp.zeros_like(edge_s)
        put(edge_s, 0, HALO - 1, jnp.where(has_low, low[pl.ds(slot * rows, rows), :], 0.0))

    odd = here % 2

    @pl.when(odd == 0)
    def _():
        fill(got_b, got_a)

    @pl.when(odd == 1)
    def _():
        fill(got_a, got_b)

    def send(out, row, with_stiff):
        for c in range(3):
            out[c, :cols, :] = disp[pl.ds((c * rows + row) * cols, cols), :]
            out[c, cols:, :] = edge_u[pl.ds((c * rows + row) * HALO, HALO), :]
        if with_stiff:
            at = pl.ds(row * cols, cols)
            out[3, :cols, :] = stiffness_of(physical_of(dens[at, :], kind[at, :]))
            out[3, cols:, :] = edge_s[pl.ds(row * HALO, HALO), :]
        else:
            out[3] = jnp.zeros_like(out[3])

    odd_x = lax.axis_index("gx") % 2

    @pl.when(odd_x == 0)
    def _():
        send(out_a, rows - 1, True)
        send(out_b, 0, False)

    @pl.when(odd_x == 1)
    def _():
        send(out_a, 0, False)
        send(out_b, rows - 1, True)


def loads_and_weights(rows, cols, count_x, count_y, after, load_x, load_y, load_z, force, sums, applied, inverse):
    del after
    depth = applied.shape[-1]
    place_x = lax.axis_index("gx") * rows
    place_y = lax.axis_index("gy") * cols
    local_x = load_x[...] - place_x
    local_y = load_y[...] - place_y
    owned = (local_x >= 0) & (local_x < rows) & (local_y >= 0) & (local_y < cols)
    target = jnp.where(owned, local_x * cols + local_y, -1)
    loads = target.shape[1]
    lanes = lax.broadcasted_iota(jnp.int32, (depth, loads), 0)
    hit_z = lanes == load_z[...]
    right = []
    for c in range(3):
        value = force[c : c + 1, :]
        coarse = value.astype(jnp.bfloat16).astype(jnp.float32)
        for part in (coarse, value - coarse):
            right.append(jnp.where(hit_z, part, 0.0).astype(jnp.bfloat16))
    right = jnp.concatenate(right, axis=0)
    block = 128

    def one(step, carry):
        first = pl.multiple_of(step * block, block)
        place = lax.broadcasted_iota(jnp.int32, (block, loads), 0) + first
        left = jnp.where(place == target, 1.0, 0.0).astype(jnp.bfloat16)
        product = lax.dot_general(
            left, right, (((1,), (1,)), ((), ())), preferred_element_type=jnp.float32
        )
        for c in range(3):
            part = product[:, 2 * c * depth : (2 * c + 1) * depth]
            rest = product[:, (2 * c + 1) * depth : (2 * c + 2) * depth]
            applied[c, pl.ds(first, block), :] = part + rest
        return carry

    lax.fori_loop(0, rows * cols // block, one, 0)

    wide = cols + HALO
    total_x, total_y = rows * count_x, cols * count_y
    sublane = lax.broadcasted_iota(jnp.int32, (wide, depth), 0)
    node_y = jnp.where(sublane >= wide - RADIUS, sublane - wide, sublane) + place_y
    inside_y = {
        shift: ((node_y + shift >= 0) & (node_y + shift < total_y)).astype(jnp.float32)
        for shift in range(-RADIUS, RADIUS + 1)
    }
    for kind in range(2 * RADIUS + 1):
        row = kind if kind <= RADIUS else rows - 2 * RADIUS - 1 + kind
        result = jnp.zeros((wide, depth), jnp.float32)
        for shift_y in range(-RADIUS, RADIUS + 1):
            line = jnp.zeros((1, depth), jnp.float32)
            for shift_x in range(-RADIUS, RADIUS + 1):
                square = shift_x * shift_x + shift_y * shift_y
                if square in CLASSES:
                    at = place_x + (row + shift_x)
                    inside = ((at >= 0) & (at < total_x)).astype(jnp.float32)
                    rank = CLASSES.index(square)
                    line = line + inside * sums[rank : rank + 1, :]
            result = result + inside_y[shift_y] * line
        inverse[kind] = 1.0 / jnp.where(result > 0.0, result, 1.0)


def elements(
    rows, cols, count_x, devices,
    disp, dens, kind, edge_u, edge_f, edge_s, got_a, got_b, applied, inverse, vol,
    resid, scaled, out_a, out_b, parts,
    node_u, waves, force,
):
    depth = disp.shape[-1]
    wide = cols + HALO
    blocks = wide // 8
    shear, normal_off, normal_own, pair_off, pair_own, trio, last = modal_constants()
    here = lax.axis_index("gx")
    has_low = here > 0
    has_high = here < count_x - 1
    odd = here % 2
    lane = lax.broadcasted_iota(jnp.int32, (wide, depth), 1)

    def transform(slot, values):
        for c in range(3):
            here_y = values[c]
            next_y = pltpu.roll(here_y, wide - 1, 0)
            for q, along_y in enumerate((here_y + next_y, next_y - here_y)):
                next_z = jnp.where(lane == depth - 1, 0.0, pltpu.roll(along_y, depth - 1, 1))
                waves[slot, (2 * q + 0) * 3 + c] = along_y + next_z
                waves[slot, (2 * q + 1) * 3 + c] = next_z - along_y

    def own_row(row):
        return [
            jnp.concatenate(
                [
                    disp[pl.ds(pl.multiple_of((c * rows + row) * cols, 8), cols), :],
                    edge_u[pl.ds(pl.multiple_of((c * rows + row) * HALO, 8), HALO), :],
                ],
                axis=0,
            )
            for c in range(3)
        ]

    def modal(before, after, block, stiff):
        at = pl.ds(block * 8, 8)
        u = [None] * 24
        for low in range(12):
            first, second = waves[before, low, at, :], waves[after, low, at, :]
            if low >= 3:
                u[low] = first + second
            u[12 + low] = second - first
        f = [None] * 24
        energy = None

        def add(value):
            nonlocal energy
            energy = value if energy is None else energy + value

        for first, second in SHEARS:
            both = u[first] + u[second]
            pull = shear * both
            add(pull * both)
            f[first] = f[second] = pull * stiff
        common = normal_off * (u[5] + u[7] + u[12])
        for degree in NORMALS:
            pull = common + normal_own * u[degree]
            add(pull * u[degree])
            f[degree] = pull * stiff
        for first, second in PAIRS:
            common = pair_off * (u[first] + u[second])
            for degree in (first, second):
                pull = common + pair_own * u[degree]
                add(pull * u[degree])
                f[degree] = pull * stiff
        common = u[9] + u[16] + u[20]
        for degree in TRIO:
            pull = trio * (common + u[degree])
            add(pull * u[degree])
            f[degree] = pull * stiff
        for degree in LASTS:
            pull = last * u[degree]
            add(pull * u[degree])
            f[degree] = pull * stiff
        return energy, f

    def spread(block, f, start, finish):
        at = pl.ds(block * 8, 8)
        for low in range(12):
            near, far = f[low], f[12 + low]
            if start:
                lower = (near - far) if near is not None else -far
                force[1, low, at, :] = force[0, low, at, :] + lower
            if finish:
                force[0, low, at, :] = (near + far) if near is not None else far

    def gather(row):
        for c in range(3):
            along = []
            for r in range(2):
                first = force[1, r * 3 + c]
                second = force[1, (2 + r) * 3 + c]
                along.append((first - second) + pltpu.roll(first + second, 1, 0))
            upper = jnp.where(lane == 0, 0.0, pltpu.roll(along[0] + along[1], 1, 1))
            total = (along[0] - along[1]) + upper
            at = pl.ds(pl.multiple_of(row * cols, 8), cols)
            resid[c, at, :] = applied[c, at, :] - total[:cols]

    def take(low, high):
        transform(0, [low[c] for c in range(3)])
        transform(1, own_row(0))
        for block in range(blocks):
            at = pl.ds(block * 8, 8)
            stiff = jnp.where(has_low, low[3, at, :], 0.0)
            energy, f = modal(0, 1, block, stiff)
            spread(block, f, False, True)
        for c in range(3):
            node_u[c] = jnp.where(has_high, high[c], 0.0)

    @pl.when(odd == 0)
    def _():
        take(got_b, got_a)

    @pl.when(odd == 1)
    def _():
        take(got_a, got_b)

    def element_row(row, total, next_row, before, after):
        transform(after, next_row)
        kind_of_row = jnp.where(
            row < RADIUS, row, jnp.where(row >= rows - RADIUS, row - (rows - 2 * RADIUS - 1), RADIUS)
        )
        for block in range(blocks):
            if block * 8 < cols:
                at = pl.ds(pl.multiple_of(row * cols + block * 8, 8), 8)
                code = kind[at, :]
                physical = physical_of(dens[at, :], code)
                stiff = stiffness_of(physical)
                factor = factor_of(physical, code)
            else:
                at = pl.ds(pl.multiple_of(row * HALO, 8), HALO)
                stiff = edge_s[at, :]
                factor = edge_f[at, :]
            energy, f = modal(before, after, block, stiff)
            spread(block, f, True, True)
            scaled[row, pl.ds(block * 8, 8), :] = factor * energy * inverse[kind_of_row, pl.ds(block * 8, 8), :]
            if block * 8 < cols:
                total = total + stiff * energy
        gather(row)
        return total

    def two_rows(step, total):
        row = 2 * step
        total = element_row(row, total, own_row(row + 1), 1, 0)
        return element_row(row + 1, total, own_row(row + 2), 0, 1)

    total = jnp.zeros((8, depth), jnp.float32)
    total = lax.fori_loop(0, rows // 2 - 1, two_rows, total)
    total = element_row(rows - 2, total, own_row(rows - 1), 1, 0)
    total = element_row(rows - 1, total, [node_u[c] for c in range(3)], 0, 1)

    half = depth // 2
    pieces = []
    for value in (total, vol[...]):
        line = jnp.sum(value, axis=0, keepdims=True)
        pieces.append(line + pltpu.roll(line, half, 1))
    line = jnp.where(lax.broadcasted_iota(jnp.int32, (1, depth), 1) < half, pieces[0], pieces[1])
    parts[...] = jnp.broadcast_to(line, (devices, depth))

    @pl.when(odd == 0)
    def _():
        out_a[...] = scaled[rows - RADIUS :]
        out_b[...] = scaled[:RADIUS]

    @pl.when(odd == 1)
    def _():
        out_a[...] = scaled[:RADIUS]
        out_b[...] = scaled[rows - RADIUS :]


def filter_rows(rows, cols, count_x, cells, scaled, got_a, got_b, parts, sens, comp, vol, near):
    depth = sens.shape[-1]
    wide = cols + HALO
    here = lax.axis_index("gx")
    has_low = here > 0
    has_high = here < count_x - 1
    odd = here % 2
    half = depth // 2
    line = jnp.sum(parts[...], axis=0, keepdims=True)
    first = lax.broadcasted_iota(jnp.int32, (1, depth), 1) < half
    compliance = jnp.sum(jnp.where(first, line, 0.0))
    volume = jnp.sum(jnp.where(first, 0.0, line))
    comp[0, 0] = compliance
    vol[0, 0] = volume / cells
    scale = cells / jnp.broadcast_to(compliance, (8, depth))

    def along_y(row, value):
        near[0, row] = value[:cols]
        for shift in range(1, RADIUS + 1):
            both = pltpu.roll(value, shift, 0) + pltpu.roll(value, wide - shift, 0)
            near[shift, row] = both[:cols]

    def take(low, high):
        for index in range(RADIUS):
            along_y(index, jnp.where(has_low, low[index], 0.0))
            along_y(rows + RADIUS + index, jnp.where(has_high, high[index], 0.0))

    @pl.when(odd == 0)
    def _():
        take(got_b, got_a)

    @pl.when(odd == 1)
    def _():
        take(got_a, got_b)

    def own(row, carry):
        along_y(row + RADIUS, scaled[row])
        return carry

    lax.fori_loop(0, rows, own, 0, unroll=2)
    lane = lax.broadcasted_iota(jnp.int32, (8, depth), 1)

    def out_row(row, carry):
        for block in range(cols // 8):
            at = pl.ds(block * 8, 8)
            classes = {}
            for shift_x in range(RADIUS + 1):
                for shift_y in range(RADIUS + 1):
                    square = shift_x * shift_x + shift_y * shift_y
                    if square not in CLASSES:
                        continue
                    value = near[shift_y, row + (RADIUS + shift_x), at, :]
                    if shift_x:
                        value = value + near[shift_y, row + (RADIUS - shift_x), at, :]
                    classes[square] = value if square not in classes else classes[square] + value
            result = None
            for shift_z in range(RADIUS + 1):
                line = None
                for square, value in classes.items():
                    weight = weight_of(square + shift_z * shift_z)
                    if weight > 0.0:
                        line = weight * value if line is None else line + weight * value
                if shift_z:
                    up = jnp.where(lane < shift_z, 0.0, pltpu.roll(line, shift_z, 1))
                    down = jnp.where(lane >= depth - shift_z, 0.0, pltpu.roll(line, depth - shift_z, 1))
                    line = up + down
                result = line if result is None else result + line
            sens[row, at, :] = result * scale
        return carry

    lax.fori_loop(0, rows, out_row, 0, unroll=2)


def call(body, shapes, inputs, scratch=(), any_first=False, smem_out=(), flops=0, limit=24):
    in_specs = [pl.BlockSpec(memory_space=pltpu.VMEM) for _ in inputs]
    if any_first:
        in_specs[0] = pl.BlockSpec(memory_space=pl.ANY)
    out_specs = [
        pl.BlockSpec(memory_space=pltpu.SMEM if rank in smem_out else pltpu.VMEM)
        for rank in range(len(shapes))
    ]
    moved = sum(int(np.prod(v.shape)) * 4 for v in list(inputs) + list(shapes))
    return pl.pallas_call(
        body,
        out_shape=[FULL(v.shape, v.dtype) for v in shapes],
        in_specs=in_specs,
        out_specs=out_specs,
        scratch_shapes=list(scratch),
        cost_estimate=pl.CostEstimate(flops=flops, bytes_accessed=moved, transcendentals=0),
        compiler_params=pltpu.CompilerParams(vmem_limit_bytes=limit * 1024 * 1024),
    )(*inputs)


def f32(*shape):
    return FULL(shape, jnp.float32)


def on_device(count_x, count_y, displacement, density, element_kind, load_x, load_y, load_z, load_force):
    rows, cols, depth = density.shape
    wide = cols + HALO
    devices = count_x * count_y
    cells = float(rows * cols * depth * devices)

    pairs_ya = [(k, k ^ 1) for k in range(count_y)]
    pairs_yb = [(k, (((k + 1) ^ 1) - 1) % count_y) for k in range(count_y)]
    pairs_xa = [(k, k ^ 1) for k in range(count_x)]
    pairs_xb = []
    for i in range(count_x):
        for j in range(count_y):
            if 0 < i < count_x - 1:
                other = (((i + 1) ^ 1) - 1, j)
            else:
                other = (i, j ^ 1)
            pairs_xb.append((i * count_y + j, other[0] * count_y + other[1]))

    disp = displacement.reshape(3 * rows * cols, depth)
    dens = density.reshape(rows * cols, depth)
    kind = element_kind.reshape(rows * cols, depth)

    slots = 4 * RADIUS + RADIUS
    send_a, send_b, vol = call(
        functools.partial(pack_y, rows, cols),
        [f32(slots * rows, depth), f32(slots * rows, depth), f32(8, depth)],
        [disp, dens, kind],
    )
    got_a = lax.ppermute(send_a, "gy", pairs_ya)
    got_b = lax.ppermute(send_b, "gy", pairs_yb)

    sums = np.zeros((8, depth), np.float32)
    for rank, square in enumerate(CLASSES):
        for z in range(depth):
            sums[rank, z] = sum(
                weight_of(square + s * s) for s in range(-RADIUS, RADIUS + 1) if 0 <= z + s < depth
            )
    count = load_x.shape[0]
    applied, inverse = call(
        functools.partial(loads_and_weights, rows, cols, count_x, count_y),
        [f32(3, rows * cols, depth), f32(2 * RADIUS + 1, wide, depth)],
        [vol, load_x.reshape(1, count), load_y.reshape(1, count), load_z.reshape(1, count), load_force, jnp.asarray(sums)],
        any_first=True,
        flops=2 * rows * cols * count * 6 * depth,
    )

    edge_u, edge_f, edge_s, send_a, send_b = call(
        functools.partial(unpack_y, rows, cols, count_y),
        [f32(3 * rows * HALO, depth), f32(rows * HALO, depth), f32(rows * HALO, depth)] + [f32(4, wide, depth)] * 2,
        [disp, dens, kind, got_a, got_b],
    )
    got_a = lax.ppermute(send_a, "gx", pairs_xa)
    got_b = lax.ppermute(send_b, BOTH, pairs_xb)

    resid, scaled, send_a, send_b, parts = call(
        functools.partial(elements, rows, cols, count_x, devices),
        [f32(3, rows * cols, depth), f32(rows, wide, depth)] + [f32(RADIUS, wide, depth)] * 2 + [f32(devices, depth)],
        [disp, dens, kind, edge_u, edge_f, edge_s, got_a, got_b, applied, inverse, vol],
        scratch=[
            pltpu.VMEM((3, wide, depth), jnp.float32),
            pltpu.VMEM((2, 12, wide, depth), jnp.float32),
            pltpu.VMEM((2, 12, wide, depth), jnp.float32),
        ],
        flops=250 * rows * wide * depth,
    )
    got_a = lax.ppermute(send_a, "gx", pairs_xa)
    got_b = lax.ppermute(send_b, BOTH, pairs_xb)
    parts = lax.all_to_all(parts, BOTH, 0, 0, tiled=True)

    sens, comp, volume = call(
        functools.partial(filter_rows, rows, cols, count_x, cells),
        [f32(rows, cols, depth), f32(1, 1), f32(1, 1)],
        [scaled, got_a, got_b, parts],
        scratch=[pltpu.VMEM((RADIUS + 1, rows + 2 * RADIUS, cols, depth), jnp.float32)],
        smem_out=(1, 2),
        flops=60 * rows * cols * depth,
    )
    return (
        sens,
        resid.reshape(3, rows, cols, depth),
        comp.reshape(()),
        volume.reshape(()),
    )


def solution(mesh):
    placed = (
        P(None, "gx", "gy", None),
        P("gx", "gy", None),
        P("gx", "gy", None),
        P(),
        P(),
        P(),
        P(),
    )
    return jax.shard_map(
        functools.partial(on_device, mesh.shape["gx"], mesh.shape["gy"]),
        mesh=mesh,
        in_specs=placed,
        out_specs=(P("gx", "gy", None), P(None, "gx", "gy", None), P(), P()),
        check_vma=False,
    )
```

profile of v0, /device:TPU:0, one launch (start us, length us, event | category | flops | bytes accessed | tf_op | source)
XLA Modules:
  0.0 45.3 jit_solution(17942341424162919846)
XLA Ops:
  0.6 0.0 copy-start
  0.6 1.3 %copy-done = f32[3,32,24,128]{3,2,1,0:T(8,128)S(1)} copy-done((f32[3,32,24,128]{3,2,1,0:T(8,128)S(1)}, f32[3,32,24,128]{3,2,1,0:T(8,128)}, u32[]{:S(2)}) %copy-start) | copy-done | bytes 1179672
  1.9 1.0 %copy-done.2 = f32[32,24,128]{2,1,0:T(8,128)S(1)} copy-done((f32[32,24,128]{2,1,0:T(8,128)S(1)}, f32[32,24,128]{2,1,0:T(8,128)}, u32[]{:S(2)}) %copy-start.2) | copy-done | bytes 393240
  2.9 1.0 %copy-done.4 = s32[32,24,128]{2,1,0:T(8,128)S(1)} copy-done((s32[32,24,128]{2,1,0:T(8,128)S(1)}, s32[32,24,128]{2,1,0:T(8,128)}, u32[]{:S(2)}) %copy-start.4) | copy-done | bytes 393240
  3.9 0.2 shard_map.111
  4.1 0.5 %collective-permute-start = (f32[480,128]{1,0:T(8,128)S(1)}, f32[480,128]{1,0:T(8,128)S(1)}, u32[]{:S(2)}, u32[]{:S(2)}) collective-permute-start(f32[480,128]{1,0:T(8,128)S(1)} %get-tuple-element.22), channel_id=1, source_target_pairs={{0,1},{1,0},{2,3},{3,2},{4,5},{5,4},{6,7},{7,6},{8,9},{9,8},{10,11... | collective-permute-start | bytes 737288 | tf_op jit(solution)/shard_map/ppermute | solution.py:586
  4.6 0.0 copy-start.9
  4.6 2.7 %collective-permute-start.1 = (f32[480,128]{1,0:T(8,128)S(1)}, f32[480,128]{1,0:T(8,128)S(1)}, u32[]{:S(2)}, u32[]{:S(2)}) collective-permute-start(f32[480,128]{1,0:T(8,128)S(1)} %get-tuple-element.23), channel_id=1, source_target_pairs={{0,3},{1,2},{2,1},{3,0},{4,7},{5,6},{6,5},{7,4},{8,11},{9,10},{10,... | collective-permute-start | bytes 737288 | tf_op jit(solution)/shard_map/ppermute | solution.py:587
  7.3 0.0 collective-permute-done.got_a
  7.3 6.3 %collective-permute-done.1.got_b = f32[480,128]{1,0:T(8,128)S(1)} collective-permute-done((f32[480,128]{1,0:T(8,128)S(1)}, f32[480,128]{1,0:T(8,128)S(1)}, u32[]{:S(2)}, u32[]{:S(2)}) %collective-permute-start.1) | collective-permute-done | bytes 245792 | tf_op jit(solution)/shard_map/ppermute | solution.py:587
  13.6 0.1 shard_map.112
  13.7 1.4 %collective-permute-start.2 = (f32[4,32,128]{2,1,0:T(8,128)S(1)}, f32[4,32,128]{2,1,0:T(8,128)S(1)}, u32[]{:S(2)}, u32[]{:S(2)}) collective-permute-start(f32[4,32,128]{2,1,0:T(8,128)S(1)} %get-tuple-element.27), channel_id=1, source_target_pairs={{0,4},{4,0},{8,12},{12,8},{16,20},{20,16},{24,28},{28,24},{1,5},{5... | collective-permute-start | bytes 196616 | tf_op jit(solution)/shard_map/ppermute | solution.py:609
  15.2 0.1 collective-permute-start.3
  15.3 0.0 copy-start.1
  15.3 0.0 copy-start.3
  15.4 4.1 %shard_map.113 = (f32[3,768,128]{2,1,0:T(8,128)S(1)}, f32[7,32,128]{2,1,0:T(8,128)S(1)}) custom-call(f32[8,128]{1,0:T(8,128)S(1)} %get-tuple-element.29.after.vol, s32[1,1024]{1,0:T(1,128)S(1)} %bitcast.24, s32[1,1024]{1,0:T(1,128)S(1)} %bitcast.25, s32[1,1024]{1,0:T(1,128)S(1)} %bitcast.26, f32[3,1024]{1,0:T(4,128)S(1)} %copy-done.5, f32[8,128]{1,0:T(8,128)S(1)} %copy-done.9), custom_call_target="tpu_custom_call" | custom-call | flops 1207959552 | bytes 1327104 | tf_op jit(solution)/shard_map/pallas_call | solution.py:543
  19.4 0.0 collective-permute-done.2.got_a
  19.4 0.0 collective-permute-done.3.got_b
  19.5 7.4 %shard_map.114 = (f32[3,768,128]{2,1,0:T(8,128)}, f32[32,32,128]{2,1,0:T(8,128)S(1)}, f32[3,32,128]{2,1,0:T(8,128)S(1)}, f32[3,32,128]{2,1,0:T(8,128)S(1)}, f32[32,128]{1,0:T(8,128)S(1)}) custom-call(f32[2304,128]{1,0:T(8,128)S(1)} %bitcast.15, f32[768,128]{1,0:T(8,128)S(1)} %bitcast.18, s32[768,128]{1,0:T(8,128)S(1)} %bitcast.21, ...), custom_call_target="tpu_custom_call" | custom-call | flops 32768000 | bytes 5869568 | tf_op jit(solution)/shard_map/pallas_call | solution.py:543
  26.9 2.9 %collective-permute-start.4 = (f32[3,32,128]{2,1,0:T(8,128)S(1)}, f32[3,32,128]{2,1,0:T(8,128)S(1)}, u32[]{:S(2)}, u32[]{:S(2)}) collective-permute-start(f32[3,32,128]{2,1,0:T(8,128)S(1)} %get-tuple-element.33), channel_id=1, source_target_pairs={{0,4},{4,0},{8,12},{12,8},{16,20},{20,16},{24,28},{28,24},{1,5},{5... | collective-permute-start | bytes 147464 | tf_op jit(solution)/shard_map/ppermute | solution.py:623
  29.8 0.0 collective-permute-start.5
  29.8 12.3 %all_to_all.11 = f32[32,1,128]{2,1,0:T(1,128)S(1)} all-to-all(f32[32,1,128]{2,1,0:T(1,128)S(1)} %bitcast.23), channel_id=1, replica_groups=mesh['gx'=8,'gy'=4] {'gx','gy'}, dimensions={0} | all-to-all | bytes 32768 | tf_op jit(solution)/shard_map/all_to_all | solution.py:625
  42.1 0.0 collective-permute-done.5.got_b
  42.1 3.2 %shard_map.115 = (f32[32,24,128]{2,1,0:T(8,128)}, f32[1,1]{1,0:T(1,128)}, f32[1,1]{1,0:T(1,128)}) custom-call(f32[32,32,128]{2,1,0:T(8,128)S(1)} %get-tuple-element.32.scaled, f32[3,32,128]{2,1,0:T(8,128)S(1)} %collective-permute-done.4.got_a, f32[3,32,128]{2,1,0:T(8,128)S(1)} %collective-permute-done.5.got_b, f32[32,128]{1,0:T(8,128)S(1)} %bitcast.22), custom_call_target="tpu_custom_call" | custom-call | flops 5898240 | bytes 1032200 | tf_op jit(solution)/shard_map/pallas_call | solution.py:543
  (14 shorter events, 0.0 us)
Async XLA Ops:
  0.6 1.3 %copy-start = (f32[3,32,24,128]{3,2,1,0:T(8,128)S(1)}, f32[3,32,24,128]{3,2,1,0:T(8,128)}, u32[]{:S(2)}) copy-start(f32[3,32,24,128]{3,2,1,0:T(8,128)} %param.8) | copy-start | bytes 3538948
  1.9 1.0 %copy-start.2 = (f32[32,24,128]{2,1,0:T(8,128)S(1)}, f32[32,24,128]{2,1,0:T(8,128)}, u32[]{:S(2)}) copy-start(f32[32,24,128]{2,1,0:T(8,128)} %param.9) | copy-start | bytes 1179652
  2.9 1.0 %copy-start.4 = (s32[32,24,128]{2,1,0:T(8,128)S(1)}, s32[32,24,128]{2,1,0:T(8,128)}, u32[]{:S(2)}) copy-start(s32[32,24,128]{2,1,0:T(8,128)} %param.10) | copy-start | bytes 1179652
  4.1 3.2 %collective-permute-start = (f32[480,128]{1,0:T(8,128)S(1)}, f32[480,128]{1,0:T(8,128)S(1)}, u32[]{:S(2)}, u32[]{:S(2)}) collective-permute-start(f32[480,128]{1,0:T(8,128)S(1)} %get-tuple-element.22), channel_id=1, source_target_pairs={{0,1},{1,0},{2,3},{3,2},{4,5},{5,4},{6,7},{7,6},{8,9},{9,8},{10,11... | collective-permute-start | bytes 737288 | tf_op jit(solution)/shard_map/ppermute | solution.py:586
  4.6 10.7 %copy-start.5 = (f32[3,1024]{1,0:T(4,128)S(1)}, f32[3,1024]{1,0:T(4,128)}, u32[]{:S(2)}) copy-start(f32[3,1024]{1,0:T(4,128)} %force.1) | copy-start | bytes 36868
  4.6 10.7 %copy-start.6 = (s32[1024]{0:T(1024)S(1)}, s32[1024]{0:T(1024)}, u32[]{:S(2)}) copy-start(s32[1024]{0:T(1024)} %param.11) | copy-start | bytes 12292
  4.6 10.7 %copy-start.7 = (s32[1024]{0:T(1024)S(1)}, s32[1024]{0:T(1024)}, u32[]{:S(2)}) copy-start(s32[1024]{0:T(1024)} %param.12) | copy-start | bytes 12292
  4.6 10.7 %copy-start.8 = (s32[1024]{0:T(1024)S(1)}, s32[1024]{0:T(1024)}, u32[]{:S(2)}) copy-start(s32[1024]{0:T(1024)} %param.13) | copy-start | bytes 12292
  4.6 10.7 %copy-start.9 = (f32[8,128]{1,0:T(8,128)S(1)}, f32[8,128]{1,0:T(8,128)}, u32[]{:S(2)}) copy-start(f32[8,128]{1,0:T(8,128)} %constant.2.clone.sums) | copy-start | bytes 12292
  4.6 8.9 %collective-permute-start.1 = (f32[480,128]{1,0:T(8,128)S(1)}, f32[480,128]{1,0:T(8,128)S(1)}, u32[]{:S(2)}, u32[]{:S(2)}) collective-permute-start(f32[480,128]{1,0:T(8,128)S(1)} %get-tuple-element.23), channel_id=1, source_target_pairs={{0,3},{1,2},{2,1},{3,0},{4,7},{5,6},{6,5},{7,4},{8,11},{9,10},{10,... | collective-permute-start | bytes 737288 | tf_op jit(solution)/shard_map/ppermute | solution.py:587
  13.7 5.7 %collective-permute-start.2 = (f32[4,32,128]{2,1,0:T(8,128)S(1)}, f32[4,32,128]{2,1,0:T(8,128)S(1)}, u32[]{:S(2)}, u32[]{:S(2)}) collective-permute-start(f32[4,32,128]{2,1,0:T(8,128)S(1)} %get-tuple-element.27), channel_id=1, source_target_pairs={{0,4},{4,0},{8,12},{12,8},{16,20},{20,16},{24,28},{28,24},{1,5},{5... | collective-permute-start | bytes 196616 | tf_op jit(solution)/shard_map/ppermute | solution.py:609
  15.2 4.3 %collective-permute-start.3 = (f32[4,32,128]{2,1,0:T(8,128)S(1)}, f32[4,32,128]{2,1,0:T(8,128)S(1)}, u32[]{:S(2)}, u32[]{:S(2)}) collective-permute-start(f32[4,32,128]{2,1,0:T(8,128)S(1)} %get-tuple-element.28), channel_id=1, source_target_pairs={{0,1},{1,0},{2,3},{3,2},{4,8},{5,9},{6,10},{7,11},{8,4},{9,5},{10,... | collective-permute-start | bytes 196616 | tf_op jit(solution)/shard_map/ppermute | solution.py:610
  15.3 4.1 %copy-start.1 = (f32[3,32,24,128]{3,2,1,0:T(8,128)S(1)}, f32[3,32,24,128]{3,2,1,0:T(8,128)}, u32[]{:S(2)}) copy-start(f32[3,32,24,128]{3,2,1,0:T(8,128)} %param.8) | copy-start | bytes 3538948
  15.3 4.1 %copy-start.3 = (f32[32,24,128]{2,1,0:T(8,128)S(1)}, f32[32,24,128]{2,1,0:T(8,128)}, u32[]{:S(2)}) copy-start(f32[32,24,128]{2,1,0:T(8,128)} %param.9) | copy-start | bytes 1179652
  26.9 15.2 %collective-permute-start.4 = (f32[3,32,128]{2,1,0:T(8,128)S(1)}, f32[3,32,128]{2,1,0:T(8,128)S(1)}, u32[]{:S(2)}, u32[]{:S(2)}) collective-permute-start(f32[3,32,128]{2,1,0:T(8,128)S(1)} %get-tuple-element.33), channel_id=1, source_target_pairs={{0,4},{4,0},{8,12},{12,8},{16,20},{20,16},{24,28},{28,24},{1,5},{5... | collective-permute-start | bytes 147464 | tf_op jit(solution)/shard_map/ppermute | solution.py:623
  29.8 12.3 %collective-permute-start.5 = (f32[3,32,128]{2,1,0:T(8,128)S(1)}, f32[3,32,128]{2,1,0:T(8,128)S(1)}, u32[]{:S(2)}, u32[]{:S(2)}) collective-permute-start(f32[3,32,128]{2,1,0:T(8,128)S(1)} %get-tuple-element.34), channel_id=1, source_target_pairs={{0,1},{1,0},{2,3},{3,2},{4,8},{5,9},{6,10},{7,11},{8,4},{9,5},{10,... | collective-permute-start | bytes 147464 | tf_op jit(solution)/shard_map/ppermute | solution.py:624
where the time goes:
time: 45.6 us; the launch traced here: 45.3 us
  Pallas kernels  15.1 us (33%)
  blocking collectives  12.3 us (27%)
  starting transfers between devices  7.66 us (17%)
  waiting for transfers between devices  6.29 us (14%)
  local copies, waits for them, and re-layouts  3.29 us (7%)
  between operations  0.74 us (2%)
    pallas_call x5, Pallas kernels, call(): pl.pallas_call(body, out_shape=[FULL(v.shape, v.dtype) for v in shapes],...  15.1 us
    all_to_all x1, blocking collectives, on_device(): parts = lax.all_to_all(parts, BOTH, 0, 0, tiled=True)  12.3 us
    ppermute x1, waiting for transfers between devices, on_device(): got_b = lax.ppermute(send_b, 'gy', pairs_yb)  6.28 us
    ppermute x2, starting transfers between devices, on_device(): got_a = lax.ppermute(send_a, 'gx', pairs_xa)  4.32 us
    unnamed x20, local copies, waits for them, and re-layouts  3.29 us
    ppermute x1, starting transfers between devices, on_device(): got_b = lax.ppermute(send_b, 'gy', pairs_yb)  2.67 us
  transfers between devices with their start and end apart: 6, of which 1 were waited for; matrix products, arithmetic and copies ran while one was open for 0% of the time, Pallas kernels for 9%

commit v1 on v0

v1 whole, which is shorter than its diff:
```python
import functools

import jax
import jax.numpy as jnp
import numpy as np
from jax import lax
from jax.experimental import pallas as pl
from jax.experimental.pallas import tpu as pltpu
from jax.sharding import PartitionSpec as P

RADIUS = 3
PENALTY = 3.0
STIFF_FLOOR = 0.001
POISSON = 0.3
HALO = 8
BOTH = ("gx", "gy")
FULL = jax.ShapeDtypeStruct


def element_matrix():
    lame_first = POISSON / ((1.0 + POISSON) * (1.0 - 2.0 * POISSON))
    shear_modulus = 0.5 / (1.0 + POISSON)
    material = np.zeros((6, 6))
    material[:3, :3] = lame_first
    for diagonal in range(3):
        material[diagonal, diagonal] += 2.0 * shear_modulus
        material[diagonal + 3, diagonal + 3] = shear_modulus
    points = [0.5 - 0.5 / np.sqrt(3.0), 0.5 + 0.5 / np.sqrt(3.0)]
    corners = [(a, b, e) for a in (0, 1) for b in (0, 1) for e in (0, 1)]
    result = np.zeros((24, 24))
    for point_x in points:
        for point_y in points:
            for point_z in points:
                strain = np.zeros((6, 24))
                for corner, (side_x, side_y, side_z) in enumerate(corners):
                    value_x = point_x if side_x else 1.0 - point_x
                    value_y = point_y if side_y else 1.0 - point_y
                    value_z = point_z if side_z else 1.0 - point_z
                    slope_x = (1.0 if side_x else -1.0) * value_y * value_z
                    slope_y = value_x * (1.0 if side_y else -1.0) * value_z
                    slope_z = value_x * value_y * (1.0 if side_z else -1.0)
                    column = 3 * corner
                    strain[0, column] = slope_x
                    strain[1, column + 1] = slope_y
                    strain[2, column + 2] = slope_z
                    strain[3, column] = slope_y
                    strain[3, column + 1] = slope_x
                    strain[4, column + 1] = slope_z
                    strain[4, column + 2] = slope_y
                    strain[5, column + 2] = slope_x
                    strain[5, column] = slope_z
                result += strain.T @ material @ strain / 8.0
    return result


def modal_matrix():
    pair = np.array([[1.0, 1.0], [-1.0, 1.0]])
    turn = np.kron(np.kron(np.kron(pair, pair), pair), np.eye(3))
    return turn @ element_matrix() @ turn.T / 64.0


SHEARS = ((3, 14), (4, 8), (6, 13))
NORMALS = (5, 7, 12)
PAIRS = ((10, 15), (11, 18), (17, 19))
TRIO = (9, 16, 20)
LASTS = (21, 22, 23)


def modal_constants():
    modal = modal_matrix()
    known = np.zeros((24, 24))
    shear = modal[3, 3]
    for first, second in SHEARS:
        known[np.ix_((first, second), (first, second))] = shear
    normal_off = modal[5, 7]
    normal_own = modal[5, 5] - normal_off
    known[np.ix_(NORMALS, NORMALS)] = normal_off
    pair_off = modal[10, 15]
    pair_own = modal[10, 10] - pair_off
    for both in PAIRS:
        known[np.ix_(both, both)] = pair_off
    trio = modal[9, 16]
    known[np.ix_(TRIO, TRIO)] = trio
    last = modal[21, 21]
    for group, own in ((NORMALS, normal_own), (sum(PAIRS, ()), pair_own), (TRIO, trio), (LASTS, last)):
        for degree in group:
            known[degree, degree] += own
    assert np.abs(known - modal).max() < 1e-12
    return tuple(float(v) for v in (shear, normal_off, normal_own, pair_off, pair_own, trio, last))


def weight_of(square):
    return max(0.0, RADIUS + 0.5 - float(np.sqrt(square)))


CLASSES = (0, 1, 2, 4, 5, 8, 9, 10)


def stiffness_of(physical):
    return STIFF_FLOOR + (1.0 - STIFF_FLOOR) * (physical * physical * physical)


def physical_of(density, kind):
    return jnp.where(kind == 1, 0.0, jnp.where(kind == 2, 1.0, density))


def factor_of(physical, kind):
    design = (kind != 1) & (kind != 2)
    return jnp.where(design, (-PENALTY * (1.0 - STIFF_FLOOR)) * (physical * physical), 0.0)


def pack_y(rows, cols, disp, dens, kind, out_a, out_b, edge_d, edge_p, edge_k, sems):
    half = HALO // 2
    copies = []
    for side, start in ((0, 0), (half, cols - half)):
        for source, target in ((disp, edge_d), (dens, edge_p), (kind, edge_k)):
            lead = (slice(None),) * (len(source.shape) - 2)
            copies.append(
                pltpu.make_async_copy(
                    source.at[(*lead, pl.ds(start, half), slice(None))],
                    target.at[(*lead, pl.ds(side, half), slice(None))],
                    sems.at[len(copies)],
                )
            )
    for copy in copies:
        copy.start()
    for copy in copies:
        copy.wait()
    depth = disp.shape[-1]
    flat_d = edge_d.reshape(3 * rows * HALO, depth)
    flat_p = edge_p.reshape(rows * HALO, depth)
    flat_k = edge_k.reshape(rows * HALO, depth)

    def state(index):
        code = flat_k[pl.ds(index, rows, stride=HALO), :]
        return physical_of(flat_p[pl.ds(index, rows, stride=HALO), :], code), code

    def fill(low, high):
        slot = 0
        for c in range(3):
            for index in range(RADIUS + 1):
                low[pl.ds(slot * rows, rows), :] = flat_d[pl.ds(c * rows * HALO + index, rows, stride=HALO), :]
                slot += 1
        for index in range(RADIUS):
            low[pl.ds(slot * rows, rows), :] = factor_of(*state(index))
            slot += 1
        slot = 0
        for c in range(3):
            for index in range(HALO - RADIUS, HALO):
                high[pl.ds(slot * rows, rows), :] = flat_d[pl.ds(c * rows * HALO + index, rows, stride=HALO), :]
                slot += 1
        for index in range(HALO - RADIUS, HALO):
            physical, code = state(index)
            high[pl.ds(slot * rows, rows), :] = factor_of(physical, code)
            slot += 1
        high[pl.ds(slot * rows, rows), :] = stiffness_of(physical)

    odd = lax.axis_index("gy") % 2

    @pl.when(odd == 0)
    def _():
        fill(out_b, out_a)

    @pl.when(odd == 1)
    def _():
        fill(out_a, out_b)


def unpack_y(rows, cols, count_y, after, disp, dens, kind, got_a, got_b, edge_u, edge_f, edge_s, out_a, out_b):
    del after
    here = lax.axis_index("gy")
    depth = disp.shape[-1]
    has_low = here > 0
    has_high = here < count_y - 1

    def fill(low, high):
        def put(ref, start, sublane, value):
            ref[pl.ds(start + sublane, rows, stride=HALO), :] = value

        zero = jnp.zeros((rows, depth), jnp.float32)
        slot = 0
        for c in range(3):
            for index in range(RADIUS + 1):
                put(edge_u, c * rows * HALO, index, jnp.where(has_high, high[pl.ds(slot * rows, rows), :], 0.0))
                slot += 1
        for index in range(RADIUS):
            put(edge_f, 0, index, jnp.where(has_high, high[pl.ds(slot * rows, rows), :], 0.0))
            slot += 1
        slot = 0
        for c in range(3):
            put(edge_u, c * rows * HALO, RADIUS + 1, zero)
            for index in range(HALO - RADIUS, HALO):
                put(edge_u, c * rows * HALO, index, low[pl.ds(slot * rows, rows), :])
                slot += 1
        for index in range(RADIUS, HALO - RADIUS):
            put(edge_f, 0, index, zero)
        for index in range(HALO - RADIUS, HALO):
            put(edge_f, 0, index, jnp.where(has_low, low[pl.ds(slot * rows, rows), :], 0.0))
            slot += 1
        edge_s[...] = jnp.zeros_like(edge_s)
        put(edge_s, 0, HALO - 1, jnp.where(has_low, low[pl.ds(slot * rows, rows), :], 0.0))

    odd = here % 2

    @pl.when(odd == 0)
    def _():
        fill(got_b, got_a)

    @pl.when(odd == 1)
    def _():
        fill(got_a, got_b)

    def send(out, row, with_stiff):
        for c in range(3):
            out[c, :cols, :] = disp[pl.ds((c * rows + row) * cols, cols), :]
            out[c, cols:, :] = edge_u[pl.ds((c * rows + row) * HALO, HALO), :]
        if with_stiff:
            at = pl.ds(row * cols, cols)
            out[3, :cols, :] = stiffness_of(physical_of(dens[at, :], kind[at, :]))
            out[3, cols:, :] = edge_s[pl.ds(row * HALO, HALO), :]
        else:
            out[3] = jnp.zeros_like(out[3])

    odd_x = lax.axis_index("gx") % 2

    @pl.when(odd_x == 0)
    def _():
        send(out_a, rows - 1, True)
        send(out_b, 0, False)

    @pl.when(odd_x == 1)
    def _():
        send(out_a, 0, False)
        send(out_b, rows - 1, True)


def loads_and_weights(rows, cols, count_x, count_y, after, load_x, load_y, load_z, force, sums, applied, inverse):
    del after
    depth = applied.shape[-1]
    place_x = lax.axis_index("gx") * rows
    place_y = lax.axis_index("gy") * cols
    local_x = load_x[...] - place_x
    local_y = load_y[...] - place_y
    owned = (local_x >= 0) & (local_x < rows) & (local_y >= 0) & (local_y < cols)
    target = jnp.where(owned, local_x * cols + local_y, -1)
    loads = target.shape[1]
    lanes = lax.broadcasted_iota(jnp.int32, (depth, loads), 0)
    hit_z = lanes == load_z[...]
    right = [[], []]
    for c in range(3):
        value = force[c : c + 1, :]
        coarse = value.astype(jnp.bfloat16).astype(jnp.float32)
        for part, piece in zip(right, (coarse, value - coarse)):
            part.append(jnp.where(hit_z, piece, 0.0).astype(jnp.bfloat16))
    place = lax.broadcasted_iota(jnp.int32, (rows * cols, loads), 0)
    left = jnp.where(place == target, 1.0, 0.0).astype(jnp.bfloat16)
    product = None
    for part in right:
        piece = lax.dot_general(
            left, jnp.concatenate(part, axis=0), (((1,), (1,)), ((), ())), preferred_element_type=jnp.float32
        )
        product = piece if product is None else product + piece
    for c in range(3):
        applied[c] = product[:, c * depth : (c + 1) * depth]

    wide = cols + HALO
    total_x, total_y = rows * count_x, cols * count_y
    sublane = lax.broadcasted_iota(jnp.int32, (wide, depth), 0)
    node_y = jnp.where(sublane >= wide - RADIUS, sublane - wide, sublane) + place_y
    inside_y = {
        shift: ((node_y + shift >= 0) & (node_y + shift < total_y)).astype(jnp.float32)
        for shift in range(-RADIUS, RADIUS + 1)
    }
    for kind in range(2 * RADIUS + 1):
        row = kind if kind <= RADIUS else rows - 2 * RADIUS - 1 + kind
        result = jnp.zeros((wide, depth), jnp.float32)
        for shift_y in range(-RADIUS, RADIUS + 1):
            line = jnp.zeros((1, depth), jnp.float32)
            for shift_x in range(-RADIUS, RADIUS + 1):
                square = shift_x * shift_x + shift_y * shift_y
                if square in CLASSES:
                    at = place_x + (row + shift_x)
                    inside = ((at >= 0) & (at < total_x)).astype(jnp.float32)
                    rank = CLASSES.index(square)
                    line = line + inside * sums[rank : rank + 1, :]
            result = result + inside_y[shift_y] * line
        inverse[kind] = 1.0 / jnp.where(result > 0.0, result, 1.0)


def waves_of(here, there, lane, depth):
    result = [[[None] * 3 for _ in range(2)] for _ in range(2)]
    for c in range(3):
        for q, along in enumerate((here[c] + there[c], there[c] - here[c])):
            beyond = jnp.where(lane == depth - 1, 0.0, pltpu.roll(along, depth - 1, 1))
            result[q][0][c] = along + beyond
            result[q][1][c] = beyond - along
    return tuple(result[q][r][c] for q in range(2) for r in range(2) for c in range(3))


def modal(before, after, stiff, constants):
    shear, normal_off, normal_own, pair_off, pair_own, trio, last = constants
    u = [None] * 24
    for low in range(12):
        if low >= 3:
            u[low] = before[low] + after[low]
        u[12 + low] = after[low] - before[low]
    f = [None] * 24
    terms = []

    def take(degree, pull):
        terms.append(pull * u[degree])
        f[degree] = pull * stiff

    for first, second in SHEARS:
        both = u[first] + u[second]
        pull = shear * both
        terms.append(pull * both)
        f[first] = f[second] = pull * stiff
    common = normal_off * (u[5] + u[7] + u[12])
    for degree in NORMALS:
        take(degree, common + normal_own * u[degree])
    for first, second in PAIRS:
        common = pair_off * (u[first] + u[second])
        take(first, common + pair_own * u[first])
        take(second, common + pair_own * u[second])
    common = u[9] + u[16] + u[20]
    for degree in TRIO:
        take(degree, trio * (common + u[degree]))
    for degree in LASTS:
        take(degree, last * u[degree])
    while len(terms) > 1:
        terms = [sum(terms[k : k + 2][1:], terms[k]) for k in range(0, len(terms), 2)]
    return terms[0], f


def lower_of(f):
    return tuple(f[12 + k] * -1.0 if f[k] is None else f[k] - f[12 + k] for k in range(12))


def upper_of(f):
    return tuple(f[12 + k] if f[k] is None else f[k] + f[12 + k] for k in range(12))


def along_z(g, lane):
    result = []
    for c in range(3):
        lines = []
        for q in range(2):
            first, second = g[6 * q + c], g[6 * q + 3 + c]
            lines.append((first - second) + jnp.where(lane == 0, 0.0, pltpu.roll(first + second, 1, 1)))
        result.append((lines[0] - lines[1], lines[0] + lines[1]))
    return result


def inner_elements(
    rows, cols,
    disp, dens, kind, edge_u, edge_f, edge_s, applied, inverse,
    resid, scaled, sums, ring, carry_y,
):
    depth = disp.shape[-1]
    constants = modal_constants()
    blocks = cols // HALO
    lane = lax.broadcasted_iota(jnp.int32, (HALO, depth), 1)

    def gather(step, nothing):
        for c in range(3):
            at = c * rows + step
            ring[c, step, :HALO, :] = disp[pl.ds(pl.multiple_of(at * cols + cols - HALO, 8), HALO), :]
            ring[c, step, HALO : 2 * HALO, :] = edge_u[pl.ds(pl.multiple_of(at * HALO, 8), HALO), :]
            ring[c, step, 2 * HALO :, :] = disp[pl.ds(pl.multiple_of(at * cols, 8), HALO), :]
        return nothing

    lax.fori_loop(0, rows, gather, 0, unroll=4)
    total = jnp.zeros((HALO, depth), jnp.float32)
    filled = jnp.zeros((HALO, depth), jnp.float32)

    for block in (blocks, *range(blocks)):
        own = block < blocks

        def nodes(row, block=block):
            if block < blocks - 1:
                start = [(c * rows + row) * cols + block * HALO for c in range(3)]
                return waves_of(
                    [disp[pl.ds(v, HALO), :] for v in start], [disp[pl.ds(v + 1, HALO), :] for v in start], lane, depth
                )
            start = (block - (blocks - 1)) * HALO
            return waves_of(
                [ring[c, row, start : start + HALO, :] for c in range(3)],
                [ring[c, row, start + 1 : start + 1 + HALO, :] for c in range(3)],
                lane,
                depth,
            )

        def finish(row, g, block=block, own=own):
            for c, (near, far) in enumerate(along_z(g, lane)):
                if own:
                    carry_y[c, row, 8 * block + 9 : 8 * block + 17, :] = far
                    at = pl.ds(row * cols + 8 * block, HALO)
                    resid[c, at, :] = applied[c, at, :] - (near + carry_y[c, row, 8 * block + 8 : 8 * block + 16, :])
                else:
                    carry_y[c, row, 1:9, :] = far

        def step(row, carry, block=block, own=own, nodes=nodes, finish=finish):
            before, held, total, filled = carry
            after = nodes(row + 1)
            where = jnp.where(
                row < RADIUS, row, jnp.where(row >= rows - RADIUS, row - (rows - 2 * RADIUS - 1), RADIUS)
            )
            if own:
                at = pl.ds(row * cols + block * HALO, HALO)
                code = kind[at, :]
                physical = physical_of(dens[at, :], code)
                stiff, factor = stiffness_of(physical), factor_of(physical, code)
                filled = filled + physical
            else:
                at = pl.ds(row * HALO, HALO)
                stiff, factor = edge_s[at, :], edge_f[at, :]
            energy, f = modal(before, after, stiff, constants)
            value = factor * energy * inverse[where, 8 * block : 8 * block + 8, :]
            if own:
                scaled[row, 8 * block + 8 : 8 * block + 16, :] = value
                total = total + stiff * energy
            else:
                scaled[row, :HALO, :] = value
                scaled[row, cols + HALO :, :] = value
            finish(row, tuple(a + b for a, b in zip(held, lower_of(f))))
            return after, upper_of(f), total, filled

        zero = jnp.zeros((HALO, depth), jnp.float32)
        carry = (nodes(0), (zero,) * 12, total, filled)
        carry = lax.fori_loop(0, rows - 2, step, carry, unroll=2)
        carry = step(rows - 2, carry)
        _, held, total, filled = carry
        finish(rows - 1, held)
        if own:
            at = pl.ds((rows - 1) * cols + block * HALO, HALO)
            filled = filled + physical_of(dens[at, :], kind[at, :])
    sums[0] = total
    sums[1] = filled


def outer_elements(
    rows, cols, count_x, devices,
    disp, dens, kind, edge_u, edge_f, edge_s, got_a, got_b, inner, scaled, sums, inverse,
    resid, final, out_a, out_b, parts, ring, carry_y,
):
    depth = disp.shape[-1]
    constants = modal_constants()
    wide = cols + HALO
    blocks = wide // HALO
    lane = lax.broadcasted_iota(jnp.int32, (HALO, depth), 1)
    here = lax.axis_index("gx")
    has_low = here > 0
    has_high = here < count_x - 1
    odd = here % 2

    def take(low, high):
        for c in range(3):
            ring[0, c, :wide, :] = low[c]
            ring[0, c, wide:, :] = low[c, :HALO, :]
            ring[3, c, :wide, :] = jnp.where(has_high, high[c], 0.0)
            ring[3, c, wide:, :] = jnp.where(has_high, high[c, :HALO, :], 0.0)
        ring[4, 0, :wide, :] = jnp.where(has_low, low[3], 0.0)

    @pl.when(odd == 0)
    def _():
        take(got_b, got_a)

    @pl.when(odd == 1)
    def _():
        take(got_a, got_b)

    for index, row in ((1, 0), (2, rows - 1)):
        for c in range(3):
            at = c * rows + row
            ring[index, c, :cols, :] = disp[pl.ds(at * cols, cols), :]
            ring[index, c, cols:wide, :] = edge_u[pl.ds(at * HALO, HALO), :]
            ring[index, c, wide:, :] = disp[pl.ds(at * cols, HALO), :]

    total = sums[0]
    for block in (blocks - 1, *range(blocks - 1)):
        own = block < blocks - 1
        first = 8 * block
        line = [
            waves_of(
                [ring[index, c, first : first + 8, :] for c in range(3)],
                [ring[index, c, first + 1 : first + 9, :] for c in range(3)],
                lane,
                depth,
            )
            for index in range(4)
        ]
        _, f_low = modal(line[0], line[1], ring[4, 0, first : first + 8, :], constants)
        row = rows - 1
        if own:
            at = pl.ds(row * cols + first, HALO)
            code = kind[at, :]
            physical = physical_of(dens[at, :], code)
            stiff, factor = stiffness_of(physical), factor_of(physical, code)
        else:
            at = pl.ds(row * HALO, HALO)
            stiff, factor = edge_s[at, :], edge_f[at, :]
        energy, f_high = modal(line[2], line[3], stiff, constants)
        value = factor * energy * inverse[2 * RADIUS, first : first + 8, :]
        if own:
            total = total + stiff * energy
            final[first + 8 : first + 16, :] = value
        else:
            final[:HALO, :] = value
            final[wide:, :] = value
        for index, (row, g) in enumerate(((0, upper_of(f_low)), (rows - 1, lower_of(f_high)))):
            for c, (near, far) in enumerate(along_z(g, lane)):
                if own:
                    carry_y[index, c, first + 9 : first + 17, :] = far
                    resid[index, c, first : first + 8, :] = inner[c, pl.ds(row * cols + first, HALO), :] - (
                        near + carry_y[index, c, first + 8 : first + 16, :]
                    )
                else:
                    carry_y[index, c, 1:9, :] = far

    half = depth // 2
    pieces = []
    for value in (total, sums[1]):
        line = jnp.sum(value, axis=0, keepdims=True)
        pieces.append(line + pltpu.roll(line, half, 1))
    line = jnp.where(lax.broadcasted_iota(jnp.int32, (1, depth), 1) < half, pieces[0], pieces[1])
    parts[...] = jnp.broadcast_to(line, (devices, depth))

    def send(up, down):
        for index in range(RADIUS - 1):
            up[index] = scaled[rows - RADIUS + index, :wide, :]
        up[RADIUS - 1] = final[:wide, :]
        for index in range(RADIUS):
            down[index] = scaled[index, :wide, :]

    @pl.when(odd == 0)
    def _():
        send(out_a, out_b)

    @pl.when(odd == 1)
    def _():
        send(out_b, out_a)


def filter_rows(
    rows, cols, count_x, cells,
    scaled, final, got_a, got_b, parts, inner, outer,
    sens, resid, comp, vol, near, ends, result_v, sems,
):
    depth = sens.shape[-1]
    wide = cols + HALO
    copies = [
        pltpu.make_async_copy(
            inner.at[:, pl.ds(cols, (rows - 2) * cols), :], resid.at[:, pl.ds(cols, (rows - 2) * cols), :], sems.at[0]
        )
    ]
    for index, row in enumerate((0, rows - 1)):
        copies.append(
            pltpu.make_async_copy(outer.at[index], resid.at[:, pl.ds(row * cols, cols), :], sems.at[1 + index])
        )
    for copy in copies:
        copy.start()
    here = lax.axis_index("gx")
    has_low = here > 0
    has_high = here < count_x - 1
    odd = here % 2
    half = depth // 2
    line = jnp.sum(parts[...], axis=0, keepdims=True)
    first = lax.broadcasted_iota(jnp.int32, (1, depth), 1) < half
    compliance = jnp.sum(jnp.where(first, line, 0.0))
    volume = jnp.sum(jnp.where(first, 0.0, line))
    comp[0, 0] = compliance
    vol[0, 0] = volume / cells
    scale = cells / jnp.broadcast_to(compliance, (8, depth))

    def along_y(row, load):
        for block in range(cols // 8):
            start = 8 + 8 * block
            near[0, row, 8 * block : 8 * block + 8, :] = load(start)
            for shift in range(1, RADIUS + 1):
                near[shift, row, 8 * block : 8 * block + 8, :] = load(start + shift) + load(start - shift)

    def take(low, high):
        for index in range(RADIUS):
            for source, has, at in ((low, has_low, index), (high, has_high, RADIUS + index)):
                value = jnp.where(has, source[index], 0.0)
                ends[at, :wide, :] = value
                ends[at, wide:, :] = value[:HALO]

    @pl.when(odd == 0)
    def _():
        take(got_b, got_a)

    @pl.when(odd == 1)
    def _():
        take(got_a, got_b)

    for index in range(RADIUS):
        along_y(index, lambda start, at=index: ends[at, start : start + 8, :])
        along_y(rows + RADIUS + index, lambda start, at=RADIUS + index: ends[at, start : start + 8, :])
    along_y(rows + RADIUS - 1, lambda start: final[start : start + 8, :])

    def own(row, carry):
        along_y(row + RADIUS, lambda start: scaled[row, start : start + 8, :])
        return carry

    lax.fori_loop(0, rows - 1, own, 0)
    lane = lax.broadcasted_iota(jnp.int32, (8, depth), 1)

    def out_row(row, carry):
        for block in range(cols // 8):
            at = pl.ds(block * 8, 8)
            classes = {}
            for shift_x in range(RADIUS + 1):
                for shift_y in range(RADIUS + 1):
                    square = shift_x * shift_x + shift_y * shift_y
                    if square not in CLASSES:
                        continue
                    value = near[shift_y, row + (RADIUS + shift_x), at, :]
                    if shift_x:
                        value = value + near[shift_y, row + (RADIUS - shift_x), at, :]
                    classes[square] = value if square not in classes else classes[square] + value
            result = None
            for shift_z in range(RADIUS + 1):
                line = None
                for square, value in classes.items():
                    weight = weight_of(square + shift_z * shift_z)
                    if weight > 0.0:
                        line = weight * value if line is None else line + weight * value
                if shift_z:
                    up = jnp.where(lane < shift_z, 0.0, pltpu.roll(line, shift_z, 1))
                    down = jnp.where(lane >= depth - shift_z, 0.0, pltpu.roll(line, depth - shift_z, 1))
                    line = up + down
                result = line if result is None else result + line
            result_v[row, at, :] = result * scale
        return carry

    pieces = 4
    for piece in range(pieces):
        size = rows // pieces
        lax.fori_loop(piece * size, (piece + 1) * size, out_row, 0, unroll=2)
        at = pl.ds(piece * size, size)
        copies.append(pltpu.make_async_copy(result_v.at[at], sens.at[at], sems.at[3 + piece]))
        copies[-1].start()
    for copy in copies:
        copy.wait()


def call(body, shapes, inputs, scratch=(), places=None, out_places=None, flops=0, limit=24):
    places, out_places = places or {}, out_places or {}
    in_specs = [pl.BlockSpec(memory_space=places.get(rank, pltpu.VMEM)) for rank in range(len(inputs))]
    out_specs = [pl.BlockSpec(memory_space=out_places.get(rank, pltpu.VMEM)) for rank in range(len(shapes))]
    moved = sum(int(np.prod(v.shape)) * 4 for v in list(inputs) + list(shapes))
    return pl.pallas_call(
        body,
        out_shape=[FULL(v.shape, v.dtype) for v in shapes],
        in_specs=in_specs,
        out_specs=out_specs,
        scratch_shapes=list(scratch),
        cost_estimate=pl.CostEstimate(flops=flops, bytes_accessed=moved, transcendentals=0),
        compiler_params=pltpu.CompilerParams(vmem_limit_bytes=limit * 1024 * 1024),
    )(*inputs)


def f32(*shape):
    return FULL(shape, jnp.float32)


def vmem(*shape, dtype=jnp.float32):
    return pltpu.VMEM(shape, dtype)


def on_device(count_x, count_y, displacement, density, element_kind, load_x, load_y, load_z, load_force):
    rows, cols, depth = density.shape
    wide = cols + HALO
    devices = count_x * count_y
    cells = float(rows * cols * depth * devices)

    pairs_ya = [(k, k ^ 1) for k in range(count_y)]
    pairs_xa = [(k, k ^ 1) for k in range(count_x)]
    pairs_yb, pairs_xb = [], []
    for i in range(count_x):
        for j in range(count_y):
            here = i * count_y + j
            inside_y, inside_x = 0 < j < count_y - 1, 0 < i < count_x - 1
            pairs_yb.append((here, i * count_y + ((j + 1) ^ 1) - 1 if inside_y else (i ^ 1) * count_y + j))
            pairs_xb.append((here, (((i + 1) ^ 1) - 1) * count_y + j if inside_x else i * count_y + (j ^ 1)))

    disp = displacement.reshape(3 * rows * cols, depth)
    dens = density.reshape(rows * cols, depth)
    kind = element_kind.reshape(rows * cols, depth)

    slots = 4 * RADIUS + RADIUS
    send_a, send_b = call(
        functools.partial(pack_y, rows, cols),
        [f32(slots * rows, depth)] * 2,
        [displacement, density, element_kind],
        scratch=[
            vmem(3, rows, HALO, depth),
            vmem(rows, HALO, depth),
            vmem(rows, HALO, depth, dtype=jnp.int32),
            pltpu.SemaphoreType.DMA((6,)),
        ],
        places={0: pltpu.HBM, 1: pltpu.HBM, 2: pltpu.HBM},
    )
    got_a = lax.ppermute(send_a, "gy", pairs_ya)
    got_b = lax.ppermute(send_b, BOTH, pairs_yb)

    sums = np.zeros((8, depth), np.float32)
    for rank, square in enumerate(CLASSES):
        for z in range(depth):
            sums[rank, z] = sum(
                weight_of(square + s * s) for s in range(-RADIUS, RADIUS + 1) if 0 <= z + s < depth
            )
    count = load_x.shape[0]
    applied, inverse = call(
        functools.partial(loads_and_weights, rows, cols, count_x, count_y),
        [f32(3, rows * cols, depth), f32(2 * RADIUS + 1, wide, depth)],
        [send_b, load_x.reshape(1, count), load_y.reshape(1, count), load_z.reshape(1, count), load_force, jnp.asarray(sums)],
        places={0: pl.ANY},
        flops=2 * rows * cols * count * 6 * depth,
    )

    edge_u, edge_f, edge_s, send_a, send_b = call(
        functools.partial(unpack_y, rows, cols, count_y),
        [f32(3 * rows * HALO, depth), f32(rows * HALO, depth), f32(rows * HALO, depth)] + [f32(4, wide, depth)] * 2,
        [inverse, disp, dens, kind, got_a, got_b],
        places={0: pl.ANY},
    )
    got_a = lax.ppermute(send_a, "gx", pairs_xa)
    got_b = lax.ppermute(send_b, BOTH, pairs_xb)

    inner, scaled, sums = call(
        functools.partial(inner_elements, rows, cols),
        [f32(3, rows * cols, depth), f32(rows, wide + HALO, depth), f32(2, 8, depth)],
        [disp, dens, kind, edge_u, edge_f, edge_s, applied, inverse],
        scratch=[vmem(3, rows, 3 * HALO, depth), vmem(3, rows, wide + 2 * HALO, depth)],
        flops=250 * rows * wide * depth,
    )
    outer, final, send_a, send_b, parts = call(
        functools.partial(outer_elements, rows, cols, count_x, devices),
        [f32(2, 3, cols, depth), f32(wide + HALO, depth)] + [f32(RADIUS, wide, depth)] * 2 + [f32(devices, depth)],
        [disp, dens, kind, edge_u, edge_f, edge_s, got_a, got_b, inner, scaled, sums, inverse],
        scratch=[vmem(5, 3, wide + HALO, depth), vmem(2, 3, wide + 2 * HALO, depth)],
        flops=500 * wide * depth,
    )
    got_a = lax.ppermute(send_a, "gx", pairs_xa)
    got_b = lax.ppermute(send_b, BOTH, pairs_xb)
    parts = lax.all_to_all(parts, BOTH, 0, 0, tiled=True)

    sens, resid, comp, volume = call(
        functools.partial(filter_rows, rows, cols, count_x, cells),
        [f32(rows, cols, depth), f32(3, rows * cols, depth), f32(1, 1), f32(1, 1)],
        [scaled, final, got_a, got_b, parts, inner, outer],
        scratch=[
            vmem(RADIUS + 1, rows + 2 * RADIUS, cols, depth),
            vmem(2 * RADIUS, wide + HALO, depth),
            vmem(rows, cols, depth),
            pltpu.SemaphoreType.DMA((7,)),
        ],
        out_places={0: pltpu.HBM, 1: pltpu.HBM, 2: pltpu.SMEM, 3: pltpu.SMEM},
        flops=60 * rows * cols * depth,
    )
    return (
        sens,
        resid.reshape(3, rows, cols, depth),
        comp.reshape(()),
        volume.reshape(()),
    )


def solution(mesh):
    placed = (
        P(None, "gx", "gy", None),
        P("gx", "gy", None),
        P("gx", "gy", None),
        P(),
        P(),
        P(),
        P(),
    )
    return jax.shard_map(
        functools.partial(on_device, mesh.shape["gx"], mesh.shape["gy"]),
        mesh=mesh,
        in_specs=placed,
        out_specs=(P("gx", "gy", None), P(None, "gx", "gy", None), P(), P()),
        check_vma=False,
    )
```

time: 45.6 us -> 46.4 us (1.018)
  Pallas kernels: 15.1 us -> 19.8 us
  waiting for transfers between devices: 6.29 us -> 2.2 us
  starting transfers between devices: 7.66 us -> 8.31 us
  blocking collectives: 12.3 us -> 11.7 us
    pallas_call x5 -> x6, Pallas kernels: 15.1 us -> 19.8 us  [call(): pl.pallas_call(body, out_shape=[FULL(v.shape, v.dtype) for v in shapes],...]
    ppermute x1, waiting for transfers between devices: 6.28 us -> 2.19 us  [on_device(): got_b = lax.ppermute(send_b, BOTH, pairs_yb)]
    ppermute x2, starting transfers between devices: 4.32 us -> 5.19 us  [on_device(): got_a = lax.ppermute(send_a, 'gx', pairs_xa)]
    all_to_all x1, blocking collectives: 12.3 us -> 11.7 us  [on_device(): parts = lax.all_to_all(parts, BOTH, 0, 0, tiled=True)]
  transfers between devices with their start and end apart: 6 -> 6, of which waited for: 1 -> 1; matrix products, arithmetic and copies ran while one was open for 0% -> 0% of each run, Pallas kernels for 9% -> 33%
where the time goes in v1:
time: 46.4 us; the launch traced here: 46.1 us
  Pallas kernels  19.8 us (43%)
  blocking collectives  11.7 us (25%)
  starting transfers between devices  8.31 us (18%)
  local copies, waits for them, and re-layouts  3.29 us (7%)
  waiting for transfers between devices  2.2 us (5%)
  between operations  0.74 us (2%)
    pallas_call x6, Pallas kernels, call(): pl.pallas_call(body, out_shape=[FULL(v.shape, v.dtype) for v in shapes],...  19.8 us
    all_to_all x1, blocking collectives, on_device(): parts = lax.all_to_all(parts, BOTH, 0, 0, tiled=True)  11.7 us
    ppermute x2, starting transfers between devices, on_device(): got_a = lax.ppermute(send_a, 'gx', pairs_xa)  5.19 us
    unnamed x20, local copies, waits for them, and re-layouts  3.29 us
    ppermute x1, starting transfers between devices, on_device(): got_b = lax.ppermute(send_b, BOTH, pairs_yb)  2.59 us
    ppermute x1, waiting for transfers between devices, on_device(): got_b = lax.ppermute(send_b, BOTH, pairs_yb)  2.19 us
  transfers between devices with their start and end apart: 6, of which 1 were waited for; matrix products, arithmetic and copies ran while one was open for 0% of the time, Pallas kernels for 33%

profile of v1, /device:TPU:0, one launch (start us, length us, event | category | flops | bytes accessed | tf_op | source)
XLA Modules:
  0.0 46.1 jit_solution(14189373274340808336)
XLA Ops:
  0.6 0.0 copy-start
  0.6 1.3 %copy-done = f32[3,32,24,128]{3,2,1,0:T(8,128)S(1)} copy-done((f32[3,32,24,128]{3,2,1,0:T(8,128)S(1)}, f32[3,32,24,128]{3,2,1,0:T(8,128)}, u32[]{:S(2)}) %copy-start) | copy-done | bytes 1179672
  1.9 1.0 %copy-done.2 = f32[32,24,128]{2,1,0:T(8,128)S(1)} copy-done((f32[32,24,128]{2,1,0:T(8,128)S(1)}, f32[32,24,128]{2,1,0:T(8,128)}, u32[]{:S(2)}) %copy-start.2) | copy-done | bytes 393240
  2.9 1.0 %copy-done.4 = s32[32,24,128]{2,1,0:T(8,128)S(1)} copy-done((s32[32,24,128]{2,1,0:T(8,128)S(1)}, s32[32,24,128]{2,1,0:T(8,128)}, u32[]{:S(2)}) %copy-start.4) | copy-done | bytes 393240
  3.9 0.0 copy-start.9
  3.9 0.3 shard_map.111
  4.2 0.5 %collective-permute-start = (f32[480,128]{1,0:T(8,128)S(1)}, f32[480,128]{1,0:T(8,128)S(1)}, u32[]{:S(2)}, u32[]{:S(2)}) collective-permute-start(f32[480,128]{1,0:T(8,128)S(1)} %get-tuple-element.27), channel_id=1, source_target_pairs={{0,1},{1,0},{2,3},{3,2},{4,5},{5,4},{6,7},{7,6},{8,9},{9,8},{10,11... | collective-permute-start | bytes 737288 | tf_op jit(solution)/shard_map/ppermute | solution.py:706
  4.8 2.6 %collective-permute-start.1 = (f32[480,128]{1,0:T(8,128)S(1)}, f32[480,128]{1,0:T(8,128)S(1)}, u32[]{:S(2)}, u32[]{:S(2)}) collective-permute-start(f32[480,128]{1,0:T(8,128)S(1)} %get-tuple-element.25.after), channel_id=1, source_target_pairs={{0,4},{1,2},{2,1},{3,7},{4,0},{5,6},{6,5},{7,3},{8,12},{9,10},{10,... | collective-permute-start | bytes 737288 | tf_op jit(solution)/shard_map/ppermute | solution.py:707
  7.4 0.0 copy-start.1
  7.4 0.0 copy-start.3
  7.4 1.9 %shard_map.112 = (f32[3,768,128]{2,1,0:T(8,128)S(1)}, f32[7,32,128]{2,1,0:T(8,128)S(1)}) custom-call(f32[480,128]{1,0:T(8,128)S(1)} %get-tuple-element.25.after, s32[1,1024]{1,0:T(1,128)S(1)} %bitcast.24, s32[1,1024]{1,0:T(1,128)S(1)} %bitcast.25, s32[1,1024]{1,0:T(1,128)S(1)} %bitcast.26, f32[3,1024]{1,0:T(4,128)S(1)} %copy-done.5, f32[8,128]{1,0:T(8,128)S(1)} %copy-done.9), custom_call_target="tpu_custom_call" | custom-call | flops 1207959552 | bytes 1568768 | tf_op jit(solution)/shard_map/pallas_call | solution.py:654
  9.3 0.0 collective-permute-done.got_a
  9.3 2.2 %collective-permute-done.1.got_b = f32[480,128]{1,0:T(8,128)S(1)} collective-permute-done((f32[480,128]{1,0:T(8,128)S(1)}, f32[480,128]{1,0:T(8,128)S(1)}, u32[]{:S(2)}, u32[]{:S(2)}) %collective-permute-start.1) | collective-permute-done | bytes 245792 | tf_op jit(solution)/shard_map/ppermute | solution.py:707
  11.5 0.1 shard_map.113
  11.7 2.1 %collective-permute-start.2 = (f32[4,32,128]{2,1,0:T(8,128)S(1)}, f32[4,32,128]{2,1,0:T(8,128)S(1)}, u32[]{:S(2)}, u32[]{:S(2)}) collective-permute-start(f32[4,32,128]{2,1,0:T(8,128)S(1)} %get-tuple-element.33), channel_id=1, source_target_pairs={{0,4},{4,0},{8,12},{12,8},{16,20},{20,16},{24,28},{28,24},{1,5},{5... | collective-permute-start | bytes 196616 | tf_op jit(solution)/shard_map/ppermute | solution.py:730
  13.8 0.0 collective-permute-start.3
  13.8 13.4 %shard_map.114 = (f32[3,768,128]{2,1,0:T(8,128)S(1)}, f32[32,40,128]{2,1,0:T(8,128)S(1)}, f32[2,8,128]{2,1,0:T(8,128)S(1)}) custom-call(f32[2304,128]{1,0:T(8,128)S(1)} %bitcast.14, f32[768,128]{1,0:T(8,128)S(1)} %bitcast.17, s32[768,128]{1,0:T(8,128)S(1)} %bitcast.20, f32[768,128]{1,0:T(8,128)S(1)} %get-tuple-element.28.edge_u, ...), custom_call_target="tpu_custom_call" | custom-call | flops 32768000 | bytes 5758976 | tf_op jit(solution)/shard_map/pallas_call | solution.py:654
  27.1 0.0 collective-permute-done.2.got_a
  27.1 0.0 collective-permute-done.3.got_b
  27.2 0.4 shard_map.115
  27.6 3.1 %collective-permute-start.4 = (f32[3,32,128]{2,1,0:T(8,128)S(1)}, f32[3,32,128]{2,1,0:T(8,128)S(1)}, u32[]{:S(2)}, u32[]{:S(2)}) collective-permute-start(f32[3,32,128]{2,1,0:T(8,128)S(1)} %get-tuple-element.38), channel_id=1, source_target_pairs={{0,4},{4,0},{8,12},{12,8},{16,20},{20,16},{24,28},{28,24},{1,5},{5... | collective-permute-start | bytes 147464 | tf_op jit(solution)/shard_map/ppermute | solution.py:747
  30.7 0.0 collective-permute-start.5
  30.7 11.7 %all_to_all.11 = f32[32,1,128]{2,1,0:T(1,128)S(1)} all-to-all(f32[32,1,128]{2,1,0:T(1,128)S(1)} %bitcast.23), channel_id=1, replica_groups=mesh['gx'=8,'gy'=4] {'gx','gy'}, dimensions={0} | all-to-all | bytes 32768 | tf_op jit(solution)/shard_map/all_to_all | solution.py:749
  42.4 3.7 %shard_map.116 = (f32[32,24,128]{2,1,0:T(8,128)}, f32[3,768,128]{2,1,0:T(8,128)}, f32[1,1]{1,0:T(1,128)}, f32[1,1]{1,0:T(1,128)}) custom-call(f32[32,40,128]{2,1,0:T(8,128)S(1)} %get-tuple-element.32.scaled, f32[40,128]{1,0:T(8,128)S(1)} %get-tuple-element.37.final, f32[3,32,128]{2,1,0:T(8,128)S(1)} %collective-permute-done.4.got_a, ...), custom_call_target="tpu_custom_call" | custom-call | flops 5898240 | bytes 3616776 | tf_op jit(solution)/shard_map/pallas_call | solution.py:654
  (15 shorter events, 0.0 us)
Async XLA Ops:
  0.6 1.3 %copy-start = (f32[3,32,24,128]{3,2,1,0:T(8,128)S(1)}, f32[3,32,24,128]{3,2,1,0:T(8,128)}, u32[]{:S(2)}) copy-start(f32[3,32,24,128]{3,2,1,0:T(8,128)} %disp.1) | copy-start | bytes 3538948
  1.9 1.0 %copy-start.2 = (f32[32,24,128]{2,1,0:T(8,128)S(1)}, f32[32,24,128]{2,1,0:T(8,128)}, u32[]{:S(2)}) copy-start(f32[32,24,128]{2,1,0:T(8,128)} %dens.1) | copy-start | bytes 1179652
  2.9 1.0 %copy-start.4 = (s32[32,24,128]{2,1,0:T(8,128)S(1)}, s32[32,24,128]{2,1,0:T(8,128)}, u32[]{:S(2)}) copy-start(s32[32,24,128]{2,1,0:T(8,128)} %kind.1) | copy-start | bytes 1179652
  3.9 3.5 %copy-start.5 = (f32[3,1024]{1,0:T(4,128)S(1)}, f32[3,1024]{1,0:T(4,128)}, u32[]{:S(2)}) copy-start(f32[3,1024]{1,0:T(4,128)} %force.1) | copy-start | bytes 36868
  3.9 3.5 %copy-start.6 = (s32[1024]{0:T(1024)S(1)}, s32[1024]{0:T(1024)}, u32[]{:S(2)}) copy-start(s32[1024]{0:T(1024)} %param.11) | copy-start | bytes 12292
  3.9 3.5 %copy-start.7 = (s32[1024]{0:T(1024)S(1)}, s32[1024]{0:T(1024)}, u32[]{:S(2)}) copy-start(s32[1024]{0:T(1024)} %param.12) | copy-start | bytes 12292
  3.9 3.5 %copy-start.8 = (s32[1024]{0:T(1024)S(1)}, s32[1024]{0:T(1024)}, u32[]{:S(2)}) copy-start(s32[1024]{0:T(1024)} %param.13) | copy-start | bytes 12292
  3.9 3.5 %copy-start.9 = (f32[8,128]{1,0:T(8,128)S(1)}, f32[8,128]{1,0:T(8,128)}, u32[]{:S(2)}) copy-start(f32[8,128]{1,0:T(8,128)} %constant.2.clone.sums) | copy-start | bytes 12292
  4.2 5.1 %collective-permute-start = (f32[480,128]{1,0:T(8,128)S(1)}, f32[480,128]{1,0:T(8,128)S(1)}, u32[]{:S(2)}, u32[]{:S(2)}) collective-permute-start(f32[480,128]{1,0:T(8,128)S(1)} %get-tuple-element.27), channel_id=1, source_target_pairs={{0,1},{1,0},{2,3},{3,2},{4,5},{5,4},{6,7},{7,6},{8,9},{9,8},{10,11... | collective-permute-start | bytes 737288 | tf_op jit(solution)/shard_map/ppermute | solution.py:706
  4.8 6.8 %collective-permute-start.1 = (f32[480,128]{1,0:T(8,128)S(1)}, f32[480,128]{1,0:T(8,128)S(1)}, u32[]{:S(2)}, u32[]{:S(2)}) collective-permute-start(f32[480,128]{1,0:T(8,128)S(1)} %get-tuple-element.25.after), channel_id=1, source_target_pairs={{0,4},{1,2},{2,1},{3,7},{4,0},{5,6},{6,5},{7,3},{8,12},{9,10},{10,... | collective-permute-start | bytes 737288 | tf_op jit(solution)/shard_map/ppermute | solution.py:707
  7.4 4.2 %copy-start.1 = (f32[3,32,24,128]{3,2,1,0:T(8,128)S(1)}, f32[3,32,24,128]{3,2,1,0:T(8,128)}, u32[]{:S(2)}) copy-start(f32[3,32,24,128]{3,2,1,0:T(8,128)} %disp.1) | copy-start | bytes 3538948
  7.4 4.1 %copy-start.3 = (f32[32,24,128]{2,1,0:T(8,128)S(1)}, f32[32,24,128]{2,1,0:T(8,128)}, u32[]{:S(2)}) copy-start(f32[32,24,128]{2,1,0:T(8,128)} %dens.1) | copy-start | bytes 1179652
  11.7 15.5 %collective-permute-start.2 = (f32[4,32,128]{2,1,0:T(8,128)S(1)}, f32[4,32,128]{2,1,0:T(8,128)S(1)}, u32[]{:S(2)}, u32[]{:S(2)}) collective-permute-start(f32[4,32,128]{2,1,0:T(8,128)S(1)} %get-tuple-element.33), channel_id=1, source_target_pairs={{0,4},{4,0},{8,12},{12,8},{16,20},{20,16},{24,28},{28,24},{1,5},{5... | collective-permute-start | bytes 196616 | tf_op jit(solution)/shard_map/ppermute | solution.py:730
  13.8 13.4 %collective-permute-start.3 = (f32[4,32,128]{2,1,0:T(8,128)S(1)}, f32[4,32,128]{2,1,0:T(8,128)S(1)}, u32[]{:S(2)}, u32[]{:S(2)}) collective-permute-start(f32[4,32,128]{2,1,0:T(8,128)S(1)} %get-tuple-element.34), channel_id=1, source_target_pairs={{0,1},{1,0},{2,3},{3,2},{4,8},{5,9},{6,10},{7,11},{8,4},{9,5},{10,... | collective-permute-start | bytes 196616 | tf_op jit(solution)/shard_map/ppermute | solution.py:731
  27.6 14.8 %collective-permute-start.4 = (f32[3,32,128]{2,1,0:T(8,128)S(1)}, f32[3,32,128]{2,1,0:T(8,128)S(1)}, u32[]{:S(2)}, u32[]{:S(2)}) collective-permute-start(f32[3,32,128]{2,1,0:T(8,128)S(1)} %get-tuple-element.38), channel_id=1, source_target_pairs={{0,4},{4,0},{8,12},{12,8},{16,20},{20,16},{24,28},{28,24},{1,5},{5... | collective-permute-start | bytes 147464 | tf_op jit(solution)/shard_map/ppermute | solution.py:747
  30.7 11.7 %collective-permute-start.5 = (f32[3,32,128]{2,1,0:T(8,128)S(1)}, f32[3,32,128]{2,1,0:T(8,128)S(1)}, u32[]{:S(2)}, u32[]{:S(2)}) collective-permute-start(f32[3,32,128]{2,1,0:T(8,128)S(1)} %get-tuple-element.39), channel_id=1, source_target_pairs={{0,1},{1,0},{2,3},{3,2},{4,8},{5,9},{6,10},{7,11},{8,4},{9,5},{10,... | collective-permute-start | bytes 147464 | tf_op jit(solution)/shard_map/ppermute | solution.py:748

commit v2 on v1

--- a/solution.py
+++ b/solution.py
@@ -15,6 +15,7 @@
 HALO = 8
 BOTH = ("gx", "gy")
 FULL = jax.ShapeDtypeStruct
+UNROLL = 5
 
 
 def element_matrix():
@@ -109,7 +110,7 @@
     return jnp.where(design, (-PENALTY * (1.0 - STIFF_FLOOR)) * (physical * physical), 0.0)
 
 
-def pack_y(rows, cols, disp, dens, kind, out_a, out_b, edge_d, edge_p, edge_k, sems):
+def pack_y(rows, cols, disp, dens, kind, out_a, out_b, mark, edge_d, edge_p, edge_k, sems):
     half = HALO // 2
     copies = []
     for side, start in ((0, 0), (half, cols - half)):
@@ -155,6 +156,7 @@
             slot += 1
         high[pl.ds(slot * rows, rows), :] = stiffness_of(physical)
 
+    mark[...] = jnp.zeros_like(mark)
     odd = lax.axis_index("gy") % 2
 
     @pl.when(odd == 0)
@@ -287,14 +289,13 @@
         inverse[kind] = 1.0 / jnp.where(result > 0.0, result, 1.0)
 
 
-def waves_of(here, there, lane, depth):
-    result = [[[None] * 3 for _ in range(2)] for _ in range(2)]
-    for c in range(3):
-        for q, along in enumerate((here[c] + there[c], there[c] - here[c])):
-            beyond = jnp.where(lane == depth - 1, 0.0, pltpu.roll(along, depth - 1, 1))
-            result[q][0][c] = along + beyond
-            result[q][1][c] = beyond - along
-    return tuple(result[q][r][c] for q in range(2) for r in range(2) for c in range(3))
+def shifted_z(value, lane, depth):
+    beyond = jnp.where(lane == depth - 1, 0.0, pltpu.roll(value, depth - 1, 1))
+    return value + beyond, beyond - value
+
+
+def waves_of(here, there):
+    return tuple(a + b for a, b in zip(here, there)) + tuple(b - a for a, b in zip(here, there))
 
 
 def modal(before, after, stiff, constants):
@@ -341,110 +342,182 @@
     return tuple(f[12 + k] if f[k] is None else f[k] + f[12 + k] for k in range(12))
 
 
+def along_y(g):
+    return tuple(g[k] - g[6 + k] for k in range(6)), tuple(g[k] + g[6 + k] for k in range(6))
+
+
 def along_z(g, lane):
-    result = []
-    for c in range(3):
-        lines = []
-        for q in range(2):
-            first, second = g[6 * q + c], g[6 * q + 3 + c]
-            lines.append((first - second) + jnp.where(lane == 0, 0.0, pltpu.roll(first + second, 1, 1)))
-        result.append((lines[0] - lines[1], lines[0] + lines[1]))
-    return result
-
-
-def inner_elements(
-    rows, cols,
-    disp, dens, kind, edge_u, edge_f, edge_s, applied, inverse,
-    resid, scaled, sums, ring, carry_y,
-):
+    return [
+        (g[c] - g[3 + c]) + jnp.where(lane == 0, 0.0, pltpu.roll(g[c] + g[3 + c], 1, 1)) for c in range(3)
+    ]
+
+
+def class_of(row, rows):
+    return jnp.where(row < RADIUS, row, jnp.where(row >= rows - RADIUS, row - (rows - 2 * RADIUS - 1), RADIUS))
+
+
+def march(rows, block, waves, state, inverse, near, far, put, own):
+    constants = modal_constants()
+    depth = waves.shape[-1]
+    first = 8 * block
+    zero = jnp.zeros((HALO, depth), jnp.float32)
+
+    def nodes(row):
+        return waves_of(
+            [waves[k, row, first : first + 8, :] for k in range(6)],
+            [waves[k, row, first + 1 : first + 9, :] for k in range(6)],
+        )
+
+    def finish(row, g):
+        low, high = along_y(g)
+        for k in range(6):
+            if near is not None:
+                near(k, row, low[k])
+            far(k, row, high[k])
+
+    def step(row, carry):
+        before, held, total, filled = carry
+        after = nodes(row + 1)
+        physical, stiff, factor = state(row)
+        energy, f = modal(before, after, stiff, constants)
+        put(row, factor * energy * inverse[class_of(row, rows), first : first + 8, :])
+        if own:
+            total = total + stiff * energy
+            filled = filled + physical
+        finish(row, tuple(a + b for a, b in zip(held, lower_of(f))))
+        return after, upper_of(f), total, filled
+
+    carry = (nodes(0), (zero,) * 12, zero, zero)
+    carry = lax.fori_loop(0, rows - 2, step, carry, unroll=UNROLL)
+    _, held, total, filled = step(rows - 2, carry)
+    finish(rows - 1, held)
+    if own:
+        filled = filled + state(rows - 1)[0]
+    return total, filled
+
+
+def own_state(dens, kind, cols, first):
+    def state(row):
+        at = pl.ds(pl.multiple_of(row * cols + first, 8), HALO)
+        code = kind[at, :]
+        physical = physical_of(dens[at, :], code)
+        return physical, stiffness_of(physical), factor_of(physical, code)
+
+    return state
+
+
+def early_elements(rows, cols, disp, dens, kind, inverse, waves, near, far, scaled, sums):
     depth = disp.shape[-1]
-    constants = modal_constants()
-    blocks = cols // HALO
     lane = lax.broadcasted_iota(jnp.int32, (HALO, depth), 1)
 
-    def gather(step, nothing):
+    def turn(row, nothing):
         for c in range(3):
-            at = c * rows + step
-            ring[c, step, :HALO, :] = disp[pl.ds(pl.multiple_of(at * cols + cols - HALO, 8), HALO), :]
-            ring[c, step, HALO : 2 * HALO, :] = edge_u[pl.ds(pl.multiple_of(at * HALO, 8), HALO), :]
-            ring[c, step, 2 * HALO :, :] = disp[pl.ds(pl.multiple_of(at * cols, 8), HALO), :]
+            for block in range(cols // 8):
+                at = pl.ds(pl.multiple_of((c * rows + row) * cols + 8 * block, 8), HALO)
+                for r, value in enumerate(shifted_z(disp[at, :], lane, depth)):
+                    waves[3 * r + c, row, 8 * block : 8 * block + 8, :] = value
+                    if block == 0:
+                        waves[3 * r + c, row, cols + HALO :, :] = value
         return nothing
 
-    lax.fori_loop(0, rows, gather, 0, unroll=4)
-    total = jnp.zeros((HALO, depth), jnp.float32)
-    filled = jnp.zeros((HALO, depth), jnp.float32)
-
-    for block in (blocks, *range(blocks)):
-        own = block < blocks
-
-        def nodes(row, block=block):
-            if block < blocks - 1:
-                start = [(c * rows + row) * cols + block * HALO for c in range(3)]
-                return waves_of(
-                    [disp[pl.ds(v, HALO), :] for v in start], [disp[pl.ds(v + 1, HALO), :] for v in start], lane, depth
-                )
-            start = (block - (blocks - 1)) * HALO
-            return waves_of(
-                [ring[c, row, start : start + HALO, :] for c in range(3)],
-                [ring[c, row, start + 1 : start + 1 + HALO, :] for c in range(3)],
-                lane,
-                depth,
-            )
-
-        def finish(row, g, block=block, own=own):
-            for c, (near, far) in enumerate(along_z(g, lane)):
-                if own:
-                    carry_y[c, row, 8 * block + 9 : 8 * block + 17, :] = far
-                    at = pl.ds(row * cols + 8 * block, HALO)
-                    resid[c, at, :] = applied[c, at, :] - (near + carry_y[c, row, 8 * block + 8 : 8 * block + 16, :])
-                else:
-                    carry_y[c, row, 1:9, :] = far
-
-        def step(row, carry, block=block, own=own, nodes=nodes, finish=finish):
-            before, held, total, filled = carry
-            after = nodes(row + 1)
-            where = jnp.where(
-                row < RADIUS, row, jnp.where(row >= rows - RADIUS, row - (rows - 2 * RADIUS - 1), RADIUS)
-            )
-            if own:
-                at = pl.ds(row * cols + block * HALO, HALO)
-                code = kind[at, :]
-                physical = physical_of(dens[at, :], code)
-                stiff, factor = stiffness_of(physical), factor_of(physical, code)
-                filled = filled + physical
-            else:
-                at = pl.ds(row * HALO, HALO)
-                stiff, factor = edge_s[at, :], edge_f[at, :]
-            energy, f = modal(before, after, stiff, constants)
-            value = factor * energy * inverse[where, 8 * block : 8 * block + 8, :]
-            if own:
-                scaled[row, 8 * block + 8 : 8 * block + 16, :] = value
-                total = total + stiff * energy
-            else:
-                scaled[row, :HALO, :] = value
-                scaled[row, cols + HALO :, :] = value
-            finish(row, tuple(a + b for a, b in zip(held, lower_of(f))))
-            return after, upper_of(f), total, filled
-
-        zero = jnp.zeros((HALO, depth), jnp.float32)
-        carry = (nodes(0), (zero,) * 12, total, filled)
-        carry = lax.fori_loop(0, rows - 2, step, carry, unroll=2)
-        carry = step(rows - 2, carry)
-        _, held, total, filled = carry
-        finish(rows - 1, held)
-        if own:
-            at = pl.ds((rows - 1) * cols + block * HALO, HALO)
-            filled = filled + physical_of(dens[at, :], kind[at, :])
+    lax.fori_loop(0, rows, turn, 0, unroll=4)
+    total = filled = jnp.zeros((HALO, depth), jnp.float32)
+    for block in range(cols // 8 - 1):
+        first = 8 * block
+
+        def put_near(k, row, value, first=first):
+            near[k, row, first : first + 8, :] = value
+
+        def put_far(k, row, value, first=first):
+            far[k, row, first + 1 : first + 9, :] = value
+
+        def put(row, value, first=first):
+            scaled[row, first : first + 8, :] = value
+
+        state = own_state(dens, kind, cols, first)
+        more = march(rows, block, waves, state, inverse, put_near, put_far, put, True)
+        total, filled = total + more[0], filled + more[1]
     sums[0] = total
     sums[1] = filled
 
 
+def late_elements(
+    rows, cols,
+    waves_in, dens, kind, edge_u, edge_f, edge_s, applied, inverse, near_a, far_a, scaled_a, sums_a,
+    waves, resid, scaled, sums, near, far_h, far,
+):
+    depth = dens.shape[-1]
+    del waves_in
+    wide = cols + HALO
+    lane = lax.broadcasted_iota(jnp.int32, (HALO, depth), 1)
+    sublane = lax.broadcasted_iota(jnp.int32, (HALO, depth), 0)
+
+    def turn(row, nothing):
+        for c in range(3):
+            at = pl.ds(pl.multiple_of((c * rows + row) * HALO, 8), HALO)
+            for r, value in enumerate(shifted_z(edge_u[at, :], lane, depth)):
+                waves[3 * r + c, row, cols:wide, :] = value
+        return nothing
+
+    lax.fori_loop(0, rows, turn, 0, unroll=8)
+
+    def edge_state(row):
+        at = pl.ds(pl.multiple_of(row * HALO, 8), HALO)
+        return None, edge_s[at, :], edge_f[at, :]
+
+    def put_edge(row, value):
+        scaled[row, :HALO, :] = value
+        scaled[row, wide:, :] = value
+
+    def far_edge(k, row, value):
+        far_h[k, row, 1:9, :] = value
+
+    march(rows, cols // 8, waves, edge_state, inverse, None, far_edge, put_edge, False)
+    last = cols // 8 - 1
+
+    def put_near(k, row, value):
+        near[k, row] = value
+
+    def put_far(k, row, value):
+        far[k, row, 1:9, :] = value
+
+    def put(row, value):
+        scaled[row, cols:wide, :] = value
+
+    state = own_state(dens, kind, cols, 8 * last)
+    total, filled = march(rows, last, waves, state, inverse, put_near, put_far, put, True)
+    sums[0] = sums_a[0] + total
+    sums[1] = sums_a[1] + filled
+
+    def join(row, nothing):
+        for block in range(last + 1):
+            first = 8 * block
+            parts = []
+            for k in range(6):
+                if block < last:
+                    low, high = near_a[k, row, first : first + 8, :], far_a[k, row, first : first + 8, :]
+                    if block == 0:
+                        high = jnp.where(sublane == 0, far_h[k, row, 8:16, :], high)
+                else:
+                    low = near[k, row]
+                    high = jnp.where(sublane == 0, far_a[k, row, first : first + 8, :], far[k, row, :8, :])
+                parts.append(low + high)
+            at = pl.ds(pl.multiple_of(row * cols + first, 8), HALO)
+            for c, value in enumerate(along_z(parts, lane)):
+                resid[c, at, :] = applied[c, at, :] - value
+            if block < last:
+                scaled[row, first + 8 : first + 16, :] = scaled_a[row, first : first + 8, :]
+        return nothing
+
+    lax.fori_loop(0, rows, join, 0, unroll=4)
+
+
 def outer_elements(
     rows, cols, count_x, devices,
-    disp, dens, kind, edge_u, edge_f, edge_s, got_a, got_b, inner, scaled, sums, inverse,
-    resid, final, out_a, out_b, parts, ring, carry_y,
+    waves, dens, kind, edge_f, edge_s, got_a, got_b, inner, scaled, sums, inverse,
+    resid, final, out_a, out_b, parts, ring, stiff_low, carry_y,
 ):
-    depth = disp.shape[-1]
+    depth = dens.shape[-1]
     constants = modal_constants()
     wide = cols + HALO
     blocks = wide // HALO
@@ -455,12 +528,17 @@
     odd = here % 2
 
     def take(low, high):
-        for c in range(3):
-            ring[0, c, :wide, :] = low[c]
-            ring[0, c, wide:, :] = low[c, :HALO, :]
-            ring[3, c, :wide, :] = jnp.where(has_high, high[c], 0.0)
-            ring[3, c, wide:, :] = jnp.where(has_high, high[c, :HALO, :], 0.0)
-        ring[4, 0, :wide, :] = jnp.where(has_low, low[3], 0.0)
+        for block in range(blocks):
+            first = 8 * block
+            for c in range(3):
+                for side, value in enumerate((low[c, first : first + 8, :], high[c, first : first + 8, :])):
+                    if side:
+                        value = jnp.where(has_high, value, 0.0)
+                    for r, wave in enumerate(shifted_z(value, lane, depth)):
+                        ring[side, 3 * r + c, first : first + 8, :] = wave
+                        if block == 0:
+                            ring[side, 3 * r + c, wide:, :] = wave
+        stiff_low[...] = jnp.where(has_low, low[3], 0.0)
 
     @pl.when(odd == 0)
     def _():
@@ -469,36 +547,28 @@
     @pl.when(odd == 1)
     def _():
         take(got_a, got_b)
-
-    for index, row in ((1, 0), (2, rows - 1)):
-        for c in range(3):
-            at = c * rows + row
-            ring[index, c, :cols, :] = disp[pl.ds(at * cols, cols), :]
-            ring[index, c, cols:wide, :] = edge_u[pl.ds(at * HALO, HALO), :]
-            ring[index, c, wide:, :] = disp[pl.ds(at * cols, HALO), :]
 
     total = sums[0]
     for block in (blocks - 1, *range(blocks - 1)):
         own = block < blocks - 1
         first = 8 * block
+
+        def nodes(load):
+            return waves_of(
+                [load(k)[first : first + 8, :] for k in range(6)], [load(k)[first + 1 : first + 9, :] for k in range(6)]
+            )
+
         line = [
-            waves_of(
-                [ring[index, c, first : first + 8, :] for c in range(3)],
-                [ring[index, c, first + 1 : first + 9, :] for c in range(3)],
-                lane,
-                depth,
-            )
-            for index in range(4)
+            nodes(lambda k: ring.at[0, k]),
+            nodes(lambda k: waves.at[k, 0]),
+            nodes(lambda k: waves.at[k, rows - 1]),
+            nodes(lambda k: ring.at[1, k]),
         ]
-        _, f_low = modal(line[0], line[1], ring[4, 0, first : first + 8, :], constants)
-        row = rows - 1
+        _, f_low = modal(line[0], line[1], stiff_low[first : first + 8, :], constants)
         if own:
-            at = pl.ds(row * cols + first, HALO)
-            code = kind[at, :]
-            physical = physical_of(dens[at, :], code)
-            stiff, factor = stiffness_of(physical), factor_of(physical, code)
+            _, stiff, factor = own_state(dens, kind, cols, first)(rows - 1)
         else:
-            at = pl.ds(row * HALO, HALO)
+            at = pl.ds((rows - 1) * HALO, HALO)
             stiff, factor = edge_s[at, :], edge_f[at, :]
         energy, f_high = modal(line[2], line[3], stiff, constants)
         value = factor * energy * inverse[2 * RADIUS, first : first + 8, :]
@@ -509,14 +579,17 @@
             final[:HALO, :] = value
             final[wide:, :] = value
         for index, (row, g) in enumerate(((0, upper_of(f_low)), (rows - 1, lower_of(f_high)))):
-            for c, (near, far) in enumerate(along_z(g, lane)):
-                if own:
-                    carry_y[index, c, first + 9 : first + 17, :] = far
-                    resid[index, c, first : first + 8, :] = inner[c, pl.ds(row * cols + first, HALO), :] - (
-                        near + carry_y[index, c, first + 8 : first + 16, :]
-                    )
-                else:
-                    carry_y[index, c, 1:9, :] = far
+            low, high = along_y(g)
+            if own:
+                joined = []
+                for k in range(6):
+                    carry_y[index, k, first + 9 : first + 17, :] = high[k]
+                    joined.append(low[k] + carry_y[index, k, first + 8 : first + 16, :])
+                for c, value in enumerate(along_z(joined, lane)):
+                    resid[index, c, first : first + 8, :] = inner[c, pl.ds(row * cols + first, HALO), :] - value
+            else:
+                for k in range(6):
+                    carry_y[index, k, 1:9, :] = high[k]
 
     half = depth // 2
     pieces = []
@@ -573,7 +646,7 @@
     vol[0, 0] = volume / cells
     scale = cells / jnp.broadcast_to(compliance, (8, depth))
 
-    def along_y(row, load):
+    def lines_y(row, load):
         for block in range(cols // 8):
             start = 8 + 8 * block
             near[0, row, 8 * block : 8 * block + 8, :] = load(start)
@@ -596,19 +669,21 @@
         take(got_a, got_b)
 
     for index in range(RADIUS):
-        along_y(index, lambda start, at=index: ends[at, start : start + 8, :])
-        along_y(rows + RADIUS + index, lambda start, at=RADIUS + index: ends[at, start : start + 8, :])
-    along_y(rows + RADIUS - 1, lambda start: final[start : start + 8, :])
+        lines_y(index, lambda start, at=index: ends[at, start : start + 8, :])
+        lines_y(rows + RADIUS + index, lambda start, at=RADIUS + index: ends[at, start : start + 8, :])
+    lines_y(rows + RADIUS - 1, lambda start: final[start : start + 8, :])
 
     def own(row, carry):
-        along_y(row + RADIUS, lambda start: scaled[row, start : start + 8, :])
+        lines_y(row + RADIUS, lambda start: scaled[row, start : start + 8, :])
         return carry
 
     lax.fori_loop(0, rows - 1, own, 0)
     lane = lax.broadcasted_iota(jnp.int32, (8, depth), 1)
-
-    def out_row(row, carry):
-        for block in range(cols // 8):
+    blocks = cols // 8
+
+    def lines_of(row):
+        lines = []
+        for block in range(blocks):
             at = pl.ds(block * 8, 8)
             classes = {}
             for shift_x in range(RADIUS + 1):
@@ -620,25 +695,37 @@
                     if shift_x:
                         value = value + near[shift_y, row + (RADIUS - shift_x), at, :]
                     classes[square] = value if square not in classes else classes[square] + value
-            result = None
             for shift_z in range(RADIUS + 1):
                 line = None
                 for square, value in classes.items():
                     weight = weight_of(square + shift_z * shift_z)
                     if weight > 0.0:
                         line = weight * value if line is None else line + weight * value
-                if shift_z:
-                    up = jnp.where(lane < shift_z, 0.0, pltpu.roll(line, shift_z, 1))
-                    down = jnp.where(lane >= depth - shift_z, 0.0, pltpu.roll(line, depth - shift_z, 1))
-                    line = up + down
-                result = line if result is None else result + line
-            result_v[row, at, :] = result * scale
-        return carry
+                lines.append(line)
+        return tuple(lines)
+
+    def write(row, lines):
+        for block in range(blocks):
+            result, *rest = lines[(RADIUS + 1) * block : (RADIUS + 1) * (block + 1)]
+            for shift_z, line in enumerate(rest, 1):
+                up = jnp.where(lane < shift_z, 0.0, pltpu.roll(line, shift_z, 1))
+                down = jnp.where(lane >= depth - shift_z, 0.0, pltpu.roll(line, depth - shift_z, 1))
+                result = result + (up + down)
+            result_v[row, 8 * block : 8 * block + 8, :] = result * scale
+
+    def out_row(row, lines):
+        more = lines_of(row + 1)
+        write(row, lines)
+        return more
 
     pieces = 4
+    size = rows // pieces
+    lines = lines_of(0)
     for piece in range(pieces):
-        size = rows // pieces
-        lax.fori_loop(piece * size, (piece + 1) * size, out_row, 0, unroll=2)
+        last = piece == pieces - 1
+        lines = lax.fori_loop(piece * size, (piece + 1) * size - (1 if last else 0), out_row, lines)
+        if last:
+            write(rows - 1, lines)
         at = pl.ds(piece * size, size)
         copies.append(pltpu.make_async_copy(result_v.at[at], sens.at[at], sems.at[3 + piece]))
         copies[-1].start()
@@ -646,7 +733,7 @@
         copy.wait()
 
 
-def call(body, shapes, inputs, scratch=(), places=None, out_places=None, flops=0, limit=24):
+def call(body, shapes, inputs, scratch=(), places=None, out_places=None, flops=0, limit=24, aliases=None):
     places, out_places = places or {}, out_places or {}
     in_specs = [pl.BlockSpec(memory_space=places.get(rank, pltpu.VMEM)) for rank in range(len(inputs))]
     out_specs = [pl.BlockSpec(memory_space=out_places.get(rank, pltpu.VMEM)) for rank in range(len(shapes))]
@@ -657,8 +744,9 @@
         in_specs=in_specs,
         out_specs=out_specs,
         scratch_shapes=list(scratch),
+        input_output_aliases=aliases or {},
         cost_estimate=pl.CostEstimate(flops=flops, bytes_accessed=moved, transcendentals=0),
-        compiler_params=pltpu.CompilerParams(vmem_limit_bytes=limit * 1024 * 1024),
+        compiler_params=pltpu.CompilerParams(vmem_limit_bytes=int(limit * 1024 * 1024)),
     )(*inputs)
 
 
@@ -691,9 +779,9 @@
     kind = element_kind.reshape(rows * cols, depth)
 
     slots = 4 * RADIUS + RADIUS
-    send_a, send_b = call(
+    send_a, send_b, mark = call(
         functools.partial(pack_y, rows, cols),
-        [f32(slots * rows, depth)] * 2,
+        [f32(slots * rows, depth)] * 2 + [f32(8, depth)],
         [displacement, density, element_kind],
         scratch=[
             vmem(3, rows, HALO, depth),
@@ -702,6 +790,7 @@
             pltpu.SemaphoreType.DMA((6,)),
         ],
         places={0: pltpu.HBM, 1: pltpu.HBM, 2: pltpu.HBM},
+        limit=53.25,
     )
     got_a = lax.ppermute(send_a, "gy", pairs_ya)
     got_b = lax.ppermute(send_b, BOTH, pairs_yb)
@@ -716,32 +805,47 @@
     applied, inverse = call(
         functools.partial(loads_and_weights, rows, cols, count_x, count_y),
         [f32(3, rows * cols, depth), f32(2 * RADIUS + 1, wide, depth)],
-        [send_b, load_x.reshape(1, count), load_y.reshape(1, count), load_z.reshape(1, count), load_force, jnp.asarray(sums)],
+        [mark, load_x.reshape(1, count), load_y.reshape(1, count), load_z.reshape(1, count), load_force, jnp.asarray(sums)],
         places={0: pl.ANY},
         flops=2 * rows * cols * count * 6 * depth,
+    )
+
+    early = cols - HALO
+    waves, near_a, far_a, scaled_a, sums_a = call(
+        functools.partial(early_elements, rows, cols),
+        [
+            f32(6, rows, wide + HALO, depth),
+            f32(6, rows, early, depth),
+            f32(6, rows, cols, depth),
+            f32(rows, early, depth),
+            f32(2, 8, depth),
+        ],
+        [disp, dens, kind, inverse],
+        flops=250 * rows * early * depth,
     )
 
     edge_u, edge_f, edge_s, send_a, send_b = call(
         functools.partial(unpack_y, rows, cols, count_y),
         [f32(3 * rows * HALO, depth), f32(rows * HALO, depth), f32(rows * HALO, depth)] + [f32(4, wide, depth)] * 2,
-        [inverse, disp, dens, kind, got_a, got_b],
+        [sums_a, disp, dens, kind, got_a, got_b],
         places={0: pl.ANY},
     )
     got_a = lax.ppermute(send_a, "gx", pairs_xa)
     got_b = lax.ppermute(send_b, BOTH, pairs_xb)
 
-    inner, scaled, sums = call(
-        functools.partial(inner_elements, rows, cols),
-        [f32(3, rows * cols, depth), f32(rows, wide + HALO, depth), f32(2, 8, depth)],
-        [disp, dens, kind, edge_u, edge_f, edge_s, applied, inverse],
-        scratch=[vmem(3, rows, 3 * HALO, depth), vmem(3, rows, wide + 2 * HALO, depth)],
-        flops=250 * rows * wide * depth,
+    waves, inner, scaled, sums = call(
+        functools.partial(late_elements, rows, cols),
+        [f32(6, rows, wide + HALO, depth), f32(3, rows * cols, depth), f32(rows, wide + HALO, depth), f32(2, 8, depth)],
+        [waves, dens, kind, edge_u, edge_f, edge_s, applied, inverse, near_a, far_a, scaled_a, sums_a],
+        scratch=[vmem(6, rows, HALO, depth), vmem(6, rows, 2 * HALO, depth), vmem(6, rows, 2 * HALO, depth)],
+        flops=250 * rows * 2 * HALO * depth,
+        aliases={0: 0},
     )
     outer, final, send_a, send_b, parts = call(
         functools.partial(outer_elements, rows, cols, count_x, devices),
         [f32(2, 3, cols, depth), f32(wide + HALO, depth)] + [f32(RADIUS, wide, depth)] * 2 + [f32(devices, depth)],
-        [disp, dens, kind, edge_u, edge_f, edge_s, got_a, got_b, inner, scaled, sums, inverse],
-        scratch=[vmem(5, 3, wide + HALO, depth), vmem(2, 3, wide + 2 * HALO, depth)],
+        [waves, dens, kind, edge_f, edge_s, got_a, got_b, inner, scaled, sums, inverse],
+        scratch=[vmem(2, 6, wide + HALO, depth), vmem(wide, depth), vmem(2, 6, wide + 2 * HALO, depth)],
         flops=500 * wide * depth,
     )
     got_a = lax.ppermute(send_a, "gx", pairs_xa)

time: 46.4 us -> 35 us (0.75)
  Pallas kernels: 19.8 us -> 14.1 us
  local copies, waits for them, and re-layouts: 3.29 us -> 0.04 us
  waiting for transfers between devices: 2.2 us -> 0.02 us
  starting transfers between devices: 8.31 us -> 7.75 us
    pallas_call x6 -> x7, Pallas kernels: 19.8 us -> 14.1 us  [call(): pl.pallas_call(body, out_shape=[FULL(v.shape, v.dtype) for v in shapes],...]
    unnamed x20 -> x16, local copies, waits for them, and re-layouts: 3.29 us -> 0.04 us
    ppermute x1, waiting for transfers between devices: 2.19 us -> 0.01 us  [on_device(): got_b = lax.ppermute(send_b, BOTH, pairs_yb)]
    ppermute x2, starting transfers between devices: 5.19 us -> 4.63 us  [on_device(): got_a = lax.ppermute(send_a, 'gx', pairs_xa)]
  transfers between devices with their start and end apart: 6 -> 6, of which waited for: 1 -> 0; matrix products, arithmetic and copies ran while one was open for 0% -> 0% of each run, Pallas kernels for 33% -> 22%
where the time goes in v2:
time: 35 us; the launch traced here: 34.8 us
  Pallas kernels  14.1 us (40%)
  blocking collectives  12.1 us (35%)
  starting transfers between devices  7.75 us (22%)
  between operations  0.8 us (2%)
    pallas_call x7, Pallas kernels, call(): pl.pallas_call(body, out_shape=[FULL(v.shape, v.dtype) for v in shapes],...  14.1 us
    all_to_all x1, blocking collectives, on_device(): parts = lax.all_to_all(parts, BOTH, 0, 0, tiled=True)  12.1 us
    ppermute x2, starting transfers between devices, on_device(): got_a = lax.ppermute(send_a, 'gx', pairs_xa)  4.63 us
    ppermute x1, starting transfers between devices, on_device(): got_b = lax.ppermute(send_b, BOTH, pairs_yb)  2.59 us
  transfers between devices with their start and end apart: 6, of which 0 were waited for; matrix products, arithmetic and copies ran while one was open for 0% of the time, Pallas kernels for 22%

profile of v2, /device:TPU:0, one launch (start us, length us, event | category | flops | bytes accessed | tf_op | source)
XLA Modules:
  0.0 34.8 jit_solution(2686903731563687726)
XLA Ops:
  0.6 0.0 copy-start.7
  0.7 1.3 %shard_map.111 = (f32[480,128]{1,0:T(8,128)S(1)}, f32[480,128]{1,0:T(8,128)S(1)}, f32[8,128]{1,0:T(8,128)S(1)}) custom-call(f32[3,32,24,128]{3,2,1,0:T(8,128)} %disp.1, f32[32,24,128]{2,1,0:T(8,128)} %dens.1, s32[32,24,128]{2,1,0:T(8,128)} %kind.1), custom_call_target="tpu_custom_call" | custom-call | bytes 2461696 | tf_op jit(solution)/shard_map/pallas_call | solution.py:741
  2.0 0.5 %collective-permute-start = (f32[480,128]{1,0:T(8,128)S(1)}, f32[480,128]{1,0:T(8,128)S(1)}, u32[]{:S(2)}, u32[]{:S(2)}) collective-permute-start(f32[480,128]{1,0:T(8,128)S(1)} %get-tuple-element.36), channel_id=1, source_target_pairs={{0,1},{1,0},{2,3},{3,2},{4,5},{5,4},{6,7},{7,6},{8,9},{9,8},{10,11... | collective-permute-start | bytes 737288 | tf_op jit(solution)/shard_map/ppermute | solution.py:795
  2.5 2.6 %collective-permute-start.1 = (f32[480,128]{1,0:T(8,128)S(1)}, f32[480,128]{1,0:T(8,128)S(1)}, u32[]{:S(2)}, u32[]{:S(2)}) collective-permute-start(f32[480,128]{1,0:T(8,128)S(1)} %get-tuple-element.37), channel_id=1, source_target_pairs={{0,4},{1,2},{2,1},{3,7},{4,0},{5,6},{6,5},{7,3},{8,12},{9,10},{10,... | collective-permute-start | bytes 737288 | tf_op jit(solution)/shard_map/ppermute | solution.py:796
  5.2 0.0 copy-start
  5.2 0.0 copy-start.1
  5.2 0.0 copy-start.2
  5.2 1.9 %shard_map.112 = (f32[3,768,128]{2,1,0:T(8,128)S(1)}, f32[7,32,128]{2,1,0:T(8,128)S(1)}) custom-call(f32[8,128]{1,0:T(8,128)S(1)} %get-tuple-element.32.after, s32[1,1024]{1,0:T(1,128)S(1)} %bitcast.25, s32[1,1024]{1,0:T(1,128)S(1)} %bitcast.26, s32[1,1024]{1,0:T(1,128)S(1)} %bitcast.27, f32[3,1024]{1,0:T(4,128)S(1)} %copy-done.3, f32[8,128]{1,0:T(8,128)S(1)} %copy-done.7), custom_call_target="tpu_custom_call" | custom-call | flops 1207959552 | bytes 1327104 | tf_op jit(solution)/shard_map/pallas_call | solution.py:741
  7.2 2.7 %shard_map.113 = (f32[6,32,40,128]{3,2,1,0:T(8,128)S(1)}, f32[6,32,16,128]{3,2,1,0:T(8,128)S(1)}, f32[6,32,24,128]{3,2,1,0:T(8,128)S(1)}, f32[32,16,128]{2,1,0:T(8,128)S(1)}, f32[2,8,128]{2,1,0:T(8,128)S(1)}) custom-call(f32[2304,128]{1,0:T(8,128)S(1)} %bitcast.13, f32[768,128]{1,0:T(8,128)S(1)} %bitcast.15, s32[768,128]{1,0:T(8,128)S(1)} %bitcast.19, ...), custom_call_target="tpu_custom_call" | custom-call | flops 16384000 | bytes 10215424 | tf_op jit(solution)/shard_map/pallas_call | solution.py:741
  9.9 0.0 collective-permute-done.got_a
  9.9 0.0 collective-permute-done.1.got_b
  9.9 0.1 shard_map.114
  10.0 1.5 %collective-permute-start.2 = (f32[4,32,128]{2,1,0:T(8,128)S(1)}, f32[4,32,128]{2,1,0:T(8,128)S(1)}, u32[]{:S(2)}, u32[]{:S(2)}) collective-permute-start(f32[4,32,128]{2,1,0:T(8,128)S(1)} %get-tuple-element.47), channel_id=1, source_target_pairs={{0,4},{4,0},{8,12},{12,8},{16,20},{20,16},{24,28},{28,24},{1,5},{5... | collective-permute-start | bytes 196616 | tf_op jit(solution)/shard_map/ppermute | solution.py:833
  11.5 0.0 collective-permute-start.3
  11.5 3.1 %shard_map.115 = (f32[6,32,40,128]{3,2,1,0:T(8,128)S(1)}, f32[3,768,128]{2,1,0:T(8,128)S(1)}, f32[32,40,128]{2,1,0:T(8,128)S(1)}, f32[2,8,128]{2,1,0:T(8,128)S(1)}) custom-call(f32[6,32,40,128]{3,2,1,0:T(8,128)S(1)} %get-tuple-element.34.waves_in, f32[768,128]{1,0:T(8,128)S(1)} %bitcast.17, ...), custom_call_target="tpu_custom_call", output_to_operand_aliasing={{0}: (0, {})} | custom-call | flops 16384000 | bytes 16646144 | tf_op jit(solution)/shard_map/pallas_call | solution.py:741
  14.7 0.0 collective-permute-done.2.got_a
  14.7 0.0 collective-permute-done.3.got_b
  14.7 0.4 %shard_map.116 = (f32[2,3,24,128]{3,2,1,0:T(8,128)S(1)}, f32[40,128]{1,0:T(8,128)S(1)}, f32[3,32,128]{2,1,0:T(8,128)S(1)}, f32[3,32,128]{2,1,0:T(8,128)S(1)}, f32[32,128]{1,0:T(8,128)S(1)}) custom-call(f32[6,32,40,128]{3,2,1,0:T(8,128)S(1)} %get-tuple-element.46.waves, f32[768,128]{1,0:T(8,128)S(1)} %bitcast.18, s32[768,128]{1,0:T(8,128)S(1)} %bitcast.22, ...), custom_call_target="tpu_custom_call" | custom-call | flops 2048000 | bytes 7278592 | tf_op jit(solution)/shard_map/pallas_call | solution.py:741
  15.1 3.1 %collective-permute-start.4 = (f32[3,32,128]{2,1,0:T(8,128)S(1)}, f32[3,32,128]{2,1,0:T(8,128)S(1)}, u32[]{:S(2)}, u32[]{:S(2)}) collective-permute-start(f32[3,32,128]{2,1,0:T(8,128)S(1)} %get-tuple-element.52), channel_id=1, source_target_pairs={{0,4},{4,0},{8,12},{12,8},{16,20},{20,16},{24,28},{28,24},{1,5},{5... | collective-permute-start | bytes 147464 | tf_op jit(solution)/shard_map/ppermute | solution.py:851
  18.2 0.0 collective-permute-start.5
  18.3 12.1 %all_to_all.11 = f32[32,1,128]{2,1,0:T(1,128)S(1)} all-to-all(f32[32,1,128]{2,1,0:T(1,128)S(1)} %bitcast.24), channel_id=1, replica_groups=mesh['gx'=8,'gy'=4] {'gx','gy'}, dimensions={0} | all-to-all | bytes 32768 | tf_op jit(solution)/shard_map/all_to_all | solution.py:853
  30.3 0.0 collective-permute-done.4.got_a
  30.3 0.0 collective-permute-done.5.got_b
  30.3 4.5 %shard_map.117 = (f32[32,24,128]{2,1,0:T(8,128)}, f32[3,768,128]{2,1,0:T(8,128)}, f32[1,1]{1,0:T(1,128)}, f32[1,1]{1,0:T(1,128)}) custom-call(f32[32,40,128]{2,1,0:T(8,128)S(1)} %get-tuple-element.45.scaled, f32[40,128]{1,0:T(8,128)S(1)} %get-tuple-element.51.final, f32[3,32,128]{2,1,0:T(8,128)S(1)} %collective-permute-done.4.got_a, ...), custom_call_target="tpu_custom_call" | custom-call | flops 5898240 | bytes 3616776 | tf_op jit(solution)/shard_map/pallas_call | solution.py:741
  (12 shorter events, 0.0 us)
Async XLA Ops:
  0.6 4.5 %copy-start.7 = (f32[8,128]{1,0:T(8,128)S(1)}, f32[8,128]{1,0:T(8,128)}, u32[]{:S(2)}) copy-start(f32[8,128]{1,0:T(8,128)} %constant.2.clone.sums) | copy-start | bytes 12292
  0.6 4.5 %copy-start.3 = (f32[3,1024]{1,0:T(4,128)S(1)}, f32[3,1024]{1,0:T(4,128)}, u32[]{:S(2)}) copy-start(f32[3,1024]{1,0:T(4,128)} %force.1) | copy-start | bytes 36868
  0.7 4.5 %copy-start.6 = (s32[1024]{0:T(1024)S(1)}, s32[1024]{0:T(1024)}, u32[]{:S(2)}) copy-start(s32[1024]{0:T(1024)} %param.13) | copy-start | bytes 12292
  0.7 4.5 %copy-start.5 = (s32[1024]{0:T(1024)S(1)}, s32[1024]{0:T(1024)}, u32[]{:S(2)}) copy-start(s32[1024]{0:T(1024)} %param.12) | copy-start | bytes 12292
  0.7 4.5 %copy-start.4 = (s32[1024]{0:T(1024)S(1)}, s32[1024]{0:T(1024)}, u32[]{:S(2)}) copy-start(s32[1024]{0:T(1024)} %param.11) | copy-start | bytes 12292
  2.0 7.8 %collective-permute-start = (f32[480,128]{1,0:T(8,128)S(1)}, f32[480,128]{1,0:T(8,128)S(1)}, u32[]{:S(2)}, u32[]{:S(2)}) collective-permute-start(f32[480,128]{1,0:T(8,128)S(1)} %get-tuple-element.36), channel_id=1, source_target_pairs={{0,1},{1,0},{2,3},{3,2},{4,5},{5,4},{6,7},{7,6},{8,9},{9,8},{10,11... | collective-permute-start | bytes 737288 | tf_op jit(solution)/shard_map/ppermute | solution.py:795
  2.5 7.3 %collective-permute-start.1 = (f32[480,128]{1,0:T(8,128)S(1)}, f32[480,128]{1,0:T(8,128)S(1)}, u32[]{:S(2)}, u32[]{:S(2)}) collective-permute-start(f32[480,128]{1,0:T(8,128)S(1)} %get-tuple-element.37), channel_id=1, source_target_pairs={{0,4},{1,2},{2,1},{3,7},{4,0},{5,6},{6,5},{7,3},{8,12},{9,10},{10,... | collective-permute-start | bytes 737288 | tf_op jit(solution)/shard_map/ppermute | solution.py:796
  5.2 2.0 %copy-start = (f32[3,32,24,128]{3,2,1,0:T(8,128)S(1)}, f32[3,32,24,128]{3,2,1,0:T(8,128)}, u32[]{:S(2)}) copy-start(f32[3,32,24,128]{3,2,1,0:T(8,128)} %disp.1) | copy-start | bytes 3538948
  5.2 2.0 %copy-start.1 = (f32[32,24,128]{2,1,0:T(8,128)S(1)}, f32[32,24,128]{2,1,0:T(8,128)}, u32[]{:S(2)}) copy-start(f32[32,24,128]{2,1,0:T(8,128)} %dens.1) | copy-start | bytes 1179652
  5.2 2.0 %copy-start.2 = (s32[32,24,128]{2,1,0:T(8,128)S(1)}, s32[32,24,128]{2,1,0:T(8,128)}, u32[]{:S(2)}) copy-start(s32[32,24,128]{2,1,0:T(8,128)} %kind.1) | copy-start | bytes 1179652
  10.0 4.7 %collective-permute-start.2 = (f32[4,32,128]{2,1,0:T(8,128)S(1)}, f32[4,32,128]{2,1,0:T(8,128)S(1)}, u32[]{:S(2)}, u32[]{:S(2)}) collective-permute-start(f32[4,32,128]{2,1,0:T(8,128)S(1)} %get-tuple-element.47), channel_id=1, source_target_pairs={{0,4},{4,0},{8,12},{12,8},{16,20},{20,16},{24,28},{28,24},{1,5},{5... | collective-permute-start | bytes 196616 | tf_op jit(solution)/shard_map/ppermute | solution.py:833
  11.5 3.2 %collective-permute-start.3 = (f32[4,32,128]{2,1,0:T(8,128)S(1)}, f32[4,32,128]{2,1,0:T(8,128)S(1)}, u32[]{:S(2)}, u32[]{:S(2)}) collective-permute-start(f32[4,32,128]{2,1,0:T(8,128)S(1)} %get-tuple-element.48), channel_id=1, source_target_pairs={{0,1},{1,0},{2,3},{3,2},{4,8},{5,9},{6,10},{7,11},{8,4},{9,5},{10,... | collective-permute-start | bytes 196616 | tf_op jit(solution)/shard_map/ppermute | solution.py:834
  15.1 15.2 %collective-permute-start.4 = (f32[3,32,128]{2,1,0:T(8,128)S(1)}, f32[3,32,128]{2,1,0:T(8,128)S(1)}, u32[]{:S(2)}, u32[]{:S(2)}) collective-permute-start(f32[3,32,128]{2,1,0:T(8,128)S(1)} %get-tuple-element.52), channel_id=1, source_target_pairs={{0,4},{4,0},{8,12},{12,8},{16,20},{20,16},{24,28},{28,24},{1,5},{5... | collective-permute-start | bytes 147464 | tf_op jit(solution)/shard_map/ppermute | solution.py:851
  18.2 12.1 %collective-permute-start.5 = (f32[3,32,128]{2,1,0:T(8,128)S(1)}, f32[3,32,128]{2,1,0:T(8,128)S(1)}, u32[]{:S(2)}, u32[]{:S(2)}) collective-permute-start(f32[3,32,128]{2,1,0:T(8,128)S(1)} %get-tuple-element.53), channel_id=1, source_target_pairs={{0,1},{1,0},{2,3},{3,2},{4,8},{5,9},{6,10},{7,11},{8,4},{9,5},{10,... | collective-permute-start | bytes 147464 | tf_op jit(solution)/shard_map/ppermute | solution.py:852

commit v3 on v2

--- a/solution.py
+++ b/solution.py
@@ -356,7 +356,7 @@
     return jnp.where(row < RADIUS, row, jnp.where(row >= rows - RADIUS, row - (rows - 2 * RADIUS - 1), RADIUS))
 
 
-def march(rows, block, waves, state, inverse, near, far, put, own):
+def march(rows, block, waves, state, inverse, near, far, put, own, beside=None):
     constants = modal_constants()
     depth = waves.shape[-1]
     first = 8 * block
@@ -377,6 +377,8 @@
 
     def step(row, carry):
         before, held, total, filled = carry
+        if beside is not None:
+            beside(row)
         after = nodes(row + 1)
         physical, stiff, factor = state(row)
         energy, f = modal(before, after, stiff, constants)
@@ -406,7 +408,31 @@
     return state
 
 
-def early_elements(rows, cols, disp, dens, kind, inverse, waves, near, far, scaled, sums):
+def joiner(rows, cols, block, near, far, applied, resid, lane):
+    first = 8 * block
+
+    def put_near(k, row, value):
+        near[k, row] = value
+
+    def put_far(k, row, value):
+        far[k, row, first + 1 : first + 9, :] = value
+
+    def join(row):
+        parts = [near[k, row] + far[k, row, first : first + 8, :] for k in range(6)]
+        at = pl.ds(pl.multiple_of(row * cols + first, 8), HALO)
+        for c, value in enumerate(along_z(parts, lane)):
+            resid[c, at, :] = applied[c, at, :] - value
+
+    def finish():
+        join(rows - 2)
+        join(rows - 1)
+
+    return put_near, put_far, lambda row: join(jnp.maximum(row - 1, 0)), finish
+
+
+def early_elements(
+    rows, cols, disp, dens, kind, inverse, applied, waves, far, resid, scaled, sums, near
+):
     depth = disp.shape[-1]
     lane = lax.broadcasted_iota(jnp.int32, (HALO, depth), 1)
 
@@ -418,24 +444,22 @@
                     waves[3 * r + c, row, 8 * block : 8 * block + 8, :] = value
                     if block == 0:
                         waves[3 * r + c, row, cols + HALO :, :] = value
+        for k in range(6):
+            far[k, row, :8, :] = jnp.zeros((HALO, depth), jnp.float32)
         return nothing
 
-    lax.fori_loop(0, rows, turn, 0, unroll=4)
+    lax.fori_loop(0, rows, turn, 0, unroll=8)
     total = filled = jnp.zeros((HALO, depth), jnp.float32)
     for block in range(cols // 8 - 1):
         first = 8 * block
 
-        def put_near(k, row, value, first=first):
-            near[k, row, first : first + 8, :] = value
-
-        def put_far(k, row, value, first=first):
-            far[k, row, first + 1 : first + 9, :] = value
-
         def put(row, value, first=first):
-            scaled[row, first : first + 8, :] = value
-
+            scaled[row, first + 8 : first + 16, :] = value
+
+        put_near, put_far, beside, finish = joiner(rows, cols, block, near, far, applied, resid, lane)
         state = own_state(dens, kind, cols, first)
-        more = march(rows, block, waves, state, inverse, put_near, put_far, put, True)
+        more = march(rows, block, waves, state, inverse, put_near, put_far, put, True, beside=beside)
+        finish()
         total, filled = total + more[0], filled + more[1]
     sums[0] = total
     sums[1] = filled
@@ -443,14 +467,13 @@
 
 def late_elements(
     rows, cols,
-    waves_in, dens, kind, edge_u, edge_f, edge_s, applied, inverse, near_a, far_a, scaled_a, sums_a,
-    waves, resid, scaled, sums, near, far_h, far,
+    waves_in, far_in, resid_in, scaled_in, dens, kind, edge_u, edge_f, edge_s, applied, inverse, sums_a,
+    waves, far, resid, scaled, sums, near, far_h,
 ):
     depth = dens.shape[-1]
-    del waves_in
+    del waves_in, far_in, resid_in, scaled_in
     wide = cols + HALO
     lane = lax.broadcasted_iota(jnp.int32, (HALO, depth), 1)
-    sublane = lax.broadcasted_iota(jnp.int32, (HALO, depth), 0)
 
     def turn(row, nothing):
         for c in range(3):
@@ -459,7 +482,7 @@
                 waves[3 * r + c, row, cols:wide, :] = value
         return nothing
 
-    lax.fori_loop(0, rows, turn, 0, unroll=8)
+    lax.fori_loop(0, rows, turn, 0, unroll=16)
 
     def edge_state(row):
         at = pl.ds(pl.multiple_of(row * HALO, 8), HALO)
@@ -470,46 +493,25 @@
         scaled[row, wide:, :] = value
 
     def far_edge(k, row, value):
-        far_h[k, row, 1:9, :] = value
+        far_h[pl.ds(pl.multiple_of((k * rows + row) * HALO, 8), HALO), :] = value
 
     march(rows, cols // 8, waves, edge_state, inverse, None, far_edge, put_edge, False)
     last = cols // 8 - 1
 
-    def put_near(k, row, value):
-        near[k, row] = value
-
-    def put_far(k, row, value):
-        far[k, row, 1:9, :] = value
-
     def put(row, value):
         scaled[row, cols:wide, :] = value
 
+    put_near, put_far, beside, finish = joiner(rows, cols, last, near, far, applied, resid, lane)
     state = own_state(dens, kind, cols, 8 * last)
-    total, filled = march(rows, last, waves, state, inverse, put_near, put_far, put, True)
+    total, filled = march(rows, last, waves, state, inverse, put_near, put_far, put, True, beside=beside)
+    finish()
     sums[0] = sums_a[0] + total
     sums[1] = sums_a[1] + filled
 
-    def join(row, nothing):
-        for block in range(last + 1):
-            first = 8 * block
-            parts = []
-            for k in range(6):
-                if block < last:
-                    low, high = near_a[k, row, first : first + 8, :], far_a[k, row, first : first + 8, :]
-                    if block == 0:
-                        high = jnp.where(sublane == 0, far_h[k, row, 8:16, :], high)
-                else:
-                    low = near[k, row]
-                    high = jnp.where(sublane == 0, far_a[k, row, first : first + 8, :], far[k, row, :8, :])
-                parts.append(low + high)
-            at = pl.ds(pl.multiple_of(row * cols + first, 8), HALO)
-            for c, value in enumerate(along_z(parts, lane)):
-                resid[c, at, :] = applied[c, at, :] - value
-            if block < last:
-                scaled[row, first + 8 : first + 16, :] = scaled_a[row, first : first + 8, :]
-        return nothing
-
-    lax.fori_loop(0, rows, join, 0, unroll=4)
+    parts = [far_h[pl.ds(k * rows * HALO + HALO - 1, rows, stride=HALO), :] for k in range(6)]
+    at = pl.ds(0, rows, stride=cols)
+    for c, value in enumerate(along_z(parts, lax.broadcasted_iota(jnp.int32, (rows, depth), 1))):
+        resid[c, at, :] = resid[c, at, :] - value
 
 
 def outer_elements(
@@ -677,7 +679,7 @@
         lines_y(row + RADIUS, lambda start: scaled[row, start : start + 8, :])
         return carry
 
-    lax.fori_loop(0, rows - 1, own, 0)
+    lax.fori_loop(0, rows - 1, own, 0, unroll=True)
     lane = lax.broadcasted_iota(jnp.int32, (8, depth), 1)
     blocks = cols // 8
 
@@ -713,19 +715,14 @@
                 result = result + (up + down)
             result_v[row, 8 * block : 8 * block + 8, :] = result * scale
 
-    def out_row(row, lines):
-        more = lines_of(row + 1)
-        write(row, lines)
-        return more
+    def out_row(row, nothing):
+        write(row, lines_of(row))
+        return nothing
 
     pieces = 4
     size = rows // pieces
-    lines = lines_of(0)
     for piece in range(pieces):
-        last = piece == pieces - 1
-        lines = lax.fori_loop(piece * size, (piece + 1) * size - (1 if last else 0), out_row, lines)
-        if last:
-            write(rows - 1, lines)
+        lax.fori_loop(piece * size, (piece + 1) * size, out_row, 0, unroll=size)
         at = pl.ds(piece * size, size)
         copies.append(pltpu.make_async_copy(result_v.at[at], sens.at[at], sems.at[3 + piece]))
         copies[-1].start()
@@ -811,35 +808,36 @@
     )
 
     early = cols - HALO
-    waves, near_a, far_a, scaled_a, sums_a = call(
+    waves, far, inner, scaled, sums = call(
         functools.partial(early_elements, rows, cols),
         [
             f32(6, rows, wide + HALO, depth),
-            f32(6, rows, early, depth),
-            f32(6, rows, cols, depth),
-            f32(rows, early, depth),
+            f32(6, rows, wide, depth),
+            f32(3, rows * cols, depth),
+            f32(rows, wide + HALO, depth),
             f32(2, 8, depth),
         ],
-        [disp, dens, kind, inverse],
+        [disp, dens, kind, inverse, applied],
+        scratch=[vmem(6, rows, HALO, depth)],
         flops=250 * rows * early * depth,
     )
 
     edge_u, edge_f, edge_s, send_a, send_b = call(
         functools.partial(unpack_y, rows, cols, count_y),
         [f32(3 * rows * HALO, depth), f32(rows * HALO, depth), f32(rows * HALO, depth)] + [f32(4, wide, depth)] * 2,
-        [sums_a, disp, dens, kind, got_a, got_b],
+        [sums, disp, dens, kind, got_a, got_b],
         places={0: pl.ANY},
     )
     got_a = lax.ppermute(send_a, "gx", pairs_xa)
     got_b = lax.ppermute(send_b, BOTH, pairs_xb)
 
-    waves, inner, scaled, sums = call(
+    waves, far, inner, scaled, sums = call(
         functools.partial(late_elements, rows, cols),
-        [f32(6, rows, wide + HALO, depth), f32(3, rows * cols, depth), f32(rows, wide + HALO, depth), f32(2, 8, depth)],
-        [waves, dens, kind, edge_u, edge_f, edge_s, applied, inverse, near_a, far_a, scaled_a, sums_a],
-        scratch=[vmem(6, rows, HALO, depth), vmem(6, rows, 2 * HALO, depth), vmem(6, rows, 2 * HALO, depth)],
+        [f32(*v.shape) for v in (waves, far, inner, scaled, sums)],
+        [waves, far, inner, scaled, dens, kind, edge_u, edge_f, edge_s, applied, inverse, sums],
+        scratch=[vmem(6, rows, HALO, depth), vmem(6 * rows * HALO, depth)],
         flops=250 * rows * 2 * HALO * depth,
-        aliases={0: 0},
+        aliases={0: 0, 1: 1, 2: 2, 3: 3},
     )
     outer, final, send_a, send_b, parts = call(
         functools.partial(outer_elements, rows, cols, count_x, devices),

time: 35 us -> 33.7 us (0.963)
  Pallas kernels: 14.1 us -> 12.6 us
    pallas_call x7, Pallas kernels: 14.1 us -> 12.6 us  [call(): pl.pallas_call(body, out_shape=[FULL(v.shape, v.dtype) for v in shapes],...]
    ppermute x2, starting transfers between devices: 4.63 us -> 3.47 us  [on_device(): got_a = lax.ppermute(send_a, 'gx', pairs_xa)]
    ppermute x2, starting transfers between devices: 0.01 us -> 0.92 us  [on_device(): got_b = lax.ppermute(send_b, BOTH, pairs_xb)]
  transfers between devices with their start and end apart: 6 -> 6, of which waited for: 0 -> 1; matrix products, arithmetic and copies ran while one was open for 0% -> 0% of each run, Pallas kernels for 22% -> 25%
where the time goes in v3:
time: 33.7 us; the launch traced here: 33.5 us
  Pallas kernels  12.6 us (37%)
  blocking collectives  12.3 us (36%)
  starting transfers between devices  7.51 us (22%)
  between operations  0.77 us (2%)
    pallas_call x7, Pallas kernels, call(): pl.pallas_call(body, out_shape=[FULL(v.shape, v.dtype) for v in shapes],...  12.6 us
    all_to_all x1, blocking collectives, on_device(): parts = lax.all_to_all(parts, BOTH, 0, 0, tiled=True)  12.3 us
    ppermute x2, starting transfers between devices, on_device(): got_a = lax.ppermute(send_a, 'gx', pairs_xa)  3.47 us
    ppermute x1, starting transfers between devices, on_device(): got_b = lax.ppermute(send_b, BOTH, pairs_yb)  2.59 us
    ppermute x2, starting transfers between devices, on_device(): got_b = lax.ppermute(send_b, BOTH, pairs_xb)  0.92 us
  transfers between devices with their start and end apart: 6, of which 1 were waited for; matrix products, arithmetic and copies ran while one was open for 0% of the time, Pallas kernels for 25%

profile of v3, /device:TPU:0, one launch (start us, length us, event | category | flops | bytes accessed | tf_op | source)
XLA Modules:
  0.0 33.5 jit_solution(3445440291799778339)
XLA Ops:
  0.6 0.0 copy-start.7
  0.7 1.3 %shard_map.111 = (f32[480,128]{1,0:T(8,128)S(1)}, f32[480,128]{1,0:T(8,128)S(1)}, f32[8,128]{1,0:T(8,128)S(1)}) custom-call(f32[3,32,24,128]{3,2,1,0:T(8,128)} %disp.1, f32[32,24,128]{2,1,0:T(8,128)} %dens.1, s32[32,24,128]{2,1,0:T(8,128)} %kind.1), custom_call_target="tpu_custom_call" | custom-call | bytes 2461696 | tf_op jit(solution)/shard_map/pallas_call | solution.py:738
  2.0 0.5 %collective-permute-start = (f32[480,128]{1,0:T(8,128)S(1)}, f32[480,128]{1,0:T(8,128)S(1)}, u32[]{:S(2)}, u32[]{:S(2)}) collective-permute-start(f32[480,128]{1,0:T(8,128)S(1)} %get-tuple-element.40), channel_id=1, source_target_pairs={{0,1},{1,0},{2,3},{3,2},{4,5},{5,4},{6,7},{7,6},{8,9},{9,8},{10,11... | collective-permute-start | bytes 737288 | tf_op jit(solution)/shard_map/ppermute | solution.py:792
  2.5 2.6 %collective-permute-start.1 = (f32[480,128]{1,0:T(8,128)S(1)}, f32[480,128]{1,0:T(8,128)S(1)}, u32[]{:S(2)}, u32[]{:S(2)}) collective-permute-start(f32[480,128]{1,0:T(8,128)S(1)} %get-tuple-element.41), channel_id=1, source_target_pairs={{0,4},{1,2},{2,1},{3,7},{4,0},{5,6},{6,5},{7,3},{8,12},{9,10},{10,... | collective-permute-start | bytes 737288 | tf_op jit(solution)/shard_map/ppermute | solution.py:793
  5.2 0.0 copy-start
  5.2 0.0 copy-start.1
  5.2 0.0 copy-start.2
  5.2 1.9 %shard_map.112 = (f32[3,768,128]{2,1,0:T(8,128)S(1)}, f32[7,32,128]{2,1,0:T(8,128)S(1)}) custom-call(f32[8,128]{1,0:T(8,128)S(1)} %get-tuple-element.32.after, s32[1,1024]{1,0:T(1,128)S(1)} %bitcast.25, s32[1,1024]{1,0:T(1,128)S(1)} %bitcast.26, s32[1,1024]{1,0:T(1,128)S(1)} %bitcast.27, f32[3,1024]{1,0:T(4,128)S(1)} %copy-done.3, f32[8,128]{1,0:T(8,128)S(1)} %copy-done.7), custom_call_target="tpu_custom_call" | custom-call | flops 1207959552 | bytes 1327104 | tf_op jit(solution)/shard_map/pallas_call | solution.py:738
  7.2 3.7 %shard_map.113 = (f32[6,32,40,128]{3,2,1,0:T(8,128)S(1)}, f32[6,32,32,128]{3,2,1,0:T(8,128)S(1)}, f32[3,768,128]{2,1,0:T(8,128)S(1)}, f32[32,40,128]{2,1,0:T(8,128)S(1)}, f32[2,8,128]{2,1,0:T(8,128)S(1)}) custom-call(f32[2304,128]{1,0:T(8,128)S(1)} %bitcast.13, f32[768,128]{1,0:T(8,128)S(1)} %bitcast.15, s32[768,128]{1,0:T(8,128)S(1)} %bitcast.19, ...), custom_call_target="tpu_custom_call" | custom-call | flops 16384000 | bytes 12181504 | tf_op jit(solution)/shard_map/pallas_call | solution.py:738
  10.9 0.0 collective-permute-done.got_a
  10.9 0.0 collective-permute-done.1.got_b
  10.9 0.1 shard_map.114
  11.1 0.5 %collective-permute-start.2 = (f32[4,32,128]{2,1,0:T(8,128)S(1)}, f32[4,32,128]{2,1,0:T(8,128)S(1)}, u32[]{:S(2)}, u32[]{:S(2)}) collective-permute-start(f32[4,32,128]{2,1,0:T(8,128)S(1)} %get-tuple-element.47), channel_id=1, source_target_pairs={{0,4},{4,0},{8,12},{12,8},{16,20},{20,16},{24,28},{28,24},{1,5},{5... | collective-permute-start | bytes 196616 | tf_op jit(solution)/shard_map/ppermute | solution.py:831
  11.5 0.9 %collective-permute-start.3 = (f32[4,32,128]{2,1,0:T(8,128)S(1)}, f32[4,32,128]{2,1,0:T(8,128)S(1)}, u32[]{:S(2)}, u32[]{:S(2)}) collective-permute-start(f32[4,32,128]{2,1,0:T(8,128)S(1)} %get-tuple-element.48), channel_id=1, source_target_pairs={{0,1},{1,0},{2,3},{3,2},{4,8},{5,9},{6,10},{7,11},{8,4},{9,5},{10,... | collective-permute-start | bytes 196616 | tf_op jit(solution)/shard_map/ppermute | solution.py:832
  12.5 2.6 %shard_map.115 = (f32[6,32,40,128]{3,2,1,0:T(8,128)S(1)}, f32[6,32,32,128]{3,2,1,0:T(8,128)S(1)}, f32[3,768,128]{2,1,0:T(8,128)S(1)}, f32[32,40,128]{2,1,0:T(8,128)S(1)}, f32[2,8,128]{2,1,0:T(8,128)S(1)}) custom-call(f32[6,32,40,128]{3,2,1,0:T(8,128)S(1)} %get-tuple-element.35.waves_in, ...), custom_call_target="tpu_custom_call", output_to_operand_aliasing={{0}: (0, {}), {1}: (1, {}), {2}: (2, {}), {3}: (3, {})} | custom-call | flops 16384000 | bytes 20578304 | tf_op jit(solution)/shard_map/pallas_call | solution.py:738
  15.1 0.3 collective-permute-done.2.got_a
  15.4 0.0 collective-permute-done.3.got_b
  15.4 0.4 %shard_map.116 = (f32[2,3,24,128]{3,2,1,0:T(8,128)S(1)}, f32[40,128]{1,0:T(8,128)S(1)}, f32[3,32,128]{2,1,0:T(8,128)S(1)}, f32[3,32,128]{2,1,0:T(8,128)S(1)}, f32[32,128]{1,0:T(8,128)S(1)}) custom-call(f32[6,32,40,128]{3,2,1,0:T(8,128)S(1)} %get-tuple-element.46.waves, f32[768,128]{1,0:T(8,128)S(1)} %bitcast.18, s32[768,128]{1,0:T(8,128)S(1)} %bitcast.22, ...), custom_call_target="tpu_custom_call" | custom-call | flops 2048000 | bytes 7278592 | tf_op jit(solution)/shard_map/pallas_call | solution.py:738
  15.8 3.0 %collective-permute-start.4 = (f32[3,32,128]{2,1,0:T(8,128)S(1)}, f32[3,32,128]{2,1,0:T(8,128)S(1)}, u32[]{:S(2)}, u32[]{:S(2)}) collective-permute-start(f32[3,32,128]{2,1,0:T(8,128)S(1)} %get-tuple-element.52), channel_id=1, source_target_pairs={{0,4},{4,0},{8,12},{12,8},{16,20},{20,16},{24,28},{28,24},{1,5},{5... | collective-permute-start | bytes 147464 | tf_op jit(solution)/shard_map/ppermute | solution.py:849
  18.8 0.0 collective-permute-start.5
  18.8 12.3 %all_to_all.11 = f32[32,1,128]{2,1,0:T(1,128)S(1)} all-to-all(f32[32,1,128]{2,1,0:T(1,128)S(1)} %bitcast.24), channel_id=1, replica_groups=mesh['gx'=8,'gy'=4] {'gx','gy'}, dimensions={0} | all-to-all | bytes 32768 | tf_op jit(solution)/shard_map/all_to_all | solution.py:851
  31.1 0.0 collective-permute-done.4.got_a
  31.1 0.0 collective-permute-done.5.got_b
  31.1 2.4 %shard_map.117 = (f32[32,24,128]{2,1,0:T(8,128)}, f32[3,768,128]{2,1,0:T(8,128)}, f32[1,1]{1,0:T(1,128)}, f32[1,1]{1,0:T(1,128)}) custom-call(f32[32,40,128]{2,1,0:T(8,128)S(1)} %get-tuple-element.45.scaled, f32[40,128]{1,0:T(8,128)S(1)} %get-tuple-element.51.final, f32[3,32,128]{2,1,0:T(8,128)S(1)} %collective-permute-done.4.got_a, ...), custom_call_target="tpu_custom_call" | custom-call | flops 5898240 | bytes 3616776 | tf_op jit(solution)/shard_map/pallas_call | solution.py:738
  (12 shorter events, 0.0 us)
Async XLA Ops:
  0.6 4.5 %copy-start.7 = (f32[8,128]{1,0:T(8,128)S(1)}, f32[8,128]{1,0:T(8,128)}, u32[]{:S(2)}) copy-start(f32[8,128]{1,0:T(8,128)} %constant.2.clone.sums) | copy-start | bytes 12292
  0.6 4.5 %copy-start.3 = (f32[3,1024]{1,0:T(4,128)S(1)}, f32[3,1024]{1,0:T(4,128)}, u32[]{:S(2)}) copy-start(f32[3,1024]{1,0:T(4,128)} %force.1) | copy-start | bytes 36868
  0.7 4.5 %copy-start.6 = (s32[1024]{0:T(1024)S(1)}, s32[1024]{0:T(1024)}, u32[]{:S(2)}) copy-start(s32[1024]{0:T(1024)} %param.13) | copy-start | bytes 12292
  0.7 4.5 %copy-start.5 = (s32[1024]{0:T(1024)S(1)}, s32[1024]{0:T(1024)}, u32[]{:S(2)}) copy-start(s32[1024]{0:T(1024)} %param.12) | copy-start | bytes 12292
  0.7 4.5 %copy-start.4 = (s32[1024]{0:T(1024)S(1)}, s32[1024]{0:T(1024)}, u32[]{:S(2)}) copy-start(s32[1024]{0:T(1024)} %param.11) | copy-start | bytes 12292
  2.0 8.9 %collective-permute-start = (f32[480,128]{1,0:T(8,128)S(1)}, f32[480,128]{1,0:T(8,128)S(1)}, u32[]{:S(2)}, u32[]{:S(2)}) collective-permute-start(f32[480,128]{1,0:T(8,128)S(1)} %get-tuple-element.40), channel_id=1, source_target_pairs={{0,1},{1,0},{2,3},{3,2},{4,5},{5,4},{6,7},{7,6},{8,9},{9,8},{10,11... | collective-permute-start | bytes 737288 | tf_op jit(solution)/shard_map/ppermute | solution.py:792
  2.5 8.4 %collective-permute-start.1 = (f32[480,128]{1,0:T(8,128)S(1)}, f32[480,128]{1,0:T(8,128)S(1)}, u32[]{:S(2)}, u32[]{:S(2)}) collective-permute-start(f32[480,128]{1,0:T(8,128)S(1)} %get-tuple-element.41), channel_id=1, source_target_pairs={{0,4},{1,2},{2,1},{3,7},{4,0},{5,6},{6,5},{7,3},{8,12},{9,10},{10,... | collective-permute-start | bytes 737288 | tf_op jit(solution)/shard_map/ppermute | solution.py:793
  5.2 2.0 %copy-start = (f32[3,32,24,128]{3,2,1,0:T(8,128)S(1)}, f32[3,32,24,128]{3,2,1,0:T(8,128)}, u32[]{:S(2)}) copy-start(f32[3,32,24,128]{3,2,1,0:T(8,128)} %disp.1) | copy-start | bytes 3538948
  5.2 2.0 %copy-start.1 = (f32[32,24,128]{2,1,0:T(8,128)S(1)}, f32[32,24,128]{2,1,0:T(8,128)}, u32[]{:S(2)}) copy-start(f32[32,24,128]{2,1,0:T(8,128)} %dens.1) | copy-start | bytes 1179652
  5.2 2.0 %copy-start.2 = (s32[32,24,128]{2,1,0:T(8,128)S(1)}, s32[32,24,128]{2,1,0:T(8,128)}, u32[]{:S(2)}) copy-start(s32[32,24,128]{2,1,0:T(8,128)} %kind.1) | copy-start | bytes 1179652
  11.1 4.3 %collective-permute-start.2 = (f32[4,32,128]{2,1,0:T(8,128)S(1)}, f32[4,32,128]{2,1,0:T(8,128)S(1)}, u32[]{:S(2)}, u32[]{:S(2)}) collective-permute-start(f32[4,32,128]{2,1,0:T(8,128)S(1)} %get-tuple-element.47), channel_id=1, source_target_pairs={{0,4},{4,0},{8,12},{12,8},{16,20},{20,16},{24,28},{28,24},{1,5},{5... | collective-permute-start | bytes 196616 | tf_op jit(solution)/shard_map/ppermute | solution.py:831
  11.5 3.9 %collective-permute-start.3 = (f32[4,32,128]{2,1,0:T(8,128)S(1)}, f32[4,32,128]{2,1,0:T(8,128)S(1)}, u32[]{:S(2)}, u32[]{:S(2)}) collective-permute-start(f32[4,32,128]{2,1,0:T(8,128)S(1)} %get-tuple-element.48), channel_id=1, source_target_pairs={{0,1},{1,0},{2,3},{3,2},{4,8},{5,9},{6,10},{7,11},{8,4},{9,5},{10,... | collective-permute-start | bytes 196616 | tf_op jit(solution)/shard_map/ppermute | solution.py:832
  15.8 15.3 %collective-permute-start.4 = (f32[3,32,128]{2,1,0:T(8,128)S(1)}, f32[3,32,128]{2,1,0:T(8,128)S(1)}, u32[]{:S(2)}, u32[]{:S(2)}) collective-permute-start(f32[3,32,128]{2,1,0:T(8,128)S(1)} %get-tuple-element.52), channel_id=1, source_target_pairs={{0,4},{4,0},{8,12},{12,8},{16,20},{20,16},{24,28},{28,24},{1,5},{5... | collective-permute-start | bytes 147464 | tf_op jit(solution)/shard_map/ppermute | solution.py:849
  18.8 12.3 %collective-permute-start.5 = (f32[3,32,128]{2,1,0:T(8,128)S(1)}, f32[3,32,128]{2,1,0:T(8,128)S(1)}, u32[]{:S(2)}, u32[]{:S(2)}) collective-permute-start(f32[3,32,128]{2,1,0:T(8,128)S(1)} %get-tuple-element.53), channel_id=1, source_target_pairs={{0,1},{1,0},{2,3},{3,2},{4,8},{5,9},{6,10},{7,11},{8,4},{9,5},{10,... | collective-permute-start | bytes 147464 | tf_op jit(solution)/shard_map/ppermute | solution.py:850

commit v4 on v3

--- a/solution.py
+++ b/solution.py
@@ -15,7 +15,6 @@
 HALO = 8
 BOTH = ("gx", "gy")
 FULL = jax.ShapeDtypeStruct
-UNROLL = 5
 
 
 def element_matrix():
@@ -356,7 +355,7 @@
     return jnp.where(row < RADIUS, row, jnp.where(row >= rows - RADIUS, row - (rows - 2 * RADIUS - 1), RADIUS))
 
 
-def march(rows, block, waves, state, inverse, near, far, put, own, beside=None):
+def march(rows, block, waves, state, inverse, emit, put, own):
     constants = modal_constants()
     depth = waves.shape[-1]
     first = 8 * block
@@ -368,17 +367,8 @@
             [waves[k, row, first + 1 : first + 9, :] for k in range(6)],
         )
 
-    def finish(row, g):
-        low, high = along_y(g)
-        for k in range(6):
-            if near is not None:
-                near(k, row, low[k])
-            far(k, row, high[k])
-
     def step(row, carry):
         before, held, total, filled = carry
-        if beside is not None:
-            beside(row)
         after = nodes(row + 1)
         physical, stiff, factor = state(row)
         energy, f = modal(before, after, stiff, constants)
@@ -386,13 +376,13 @@
         if own:
             total = total + stiff * energy
             filled = filled + physical
-        finish(row, tuple(a + b for a, b in zip(held, lower_of(f))))
+        emit(row, *along_y(tuple(a + b for a, b in zip(held, lower_of(f)))))
         return after, upper_of(f), total, filled
 
     carry = (nodes(0), (zero,) * 12, zero, zero)
-    carry = lax.fori_loop(0, rows - 2, step, carry, unroll=UNROLL)
+    carry = lax.fori_loop(0, rows - 2, step, carry, unroll=True)
     _, held, total, filled = step(rows - 2, carry)
-    finish(rows - 1, held)
+    emit(rows - 1, *along_y(held))
     if own:
         filled = filled + state(rows - 1)[0]
     return total, filled
@@ -408,30 +398,29 @@
     return state
 
 
-def joiner(rows, cols, block, near, far, applied, resid, lane):
+def joiner(cols, block, tail_in, tail_out, applied, resid):
     first = 8 * block
-
-    def put_near(k, row, value):
-        near[k, row] = value
-
-    def put_far(k, row, value):
-        far[k, row, first + 1 : first + 9, :] = value
-
-    def join(row):
-        parts = [near[k, row] + far[k, row, first : first + 8, :] for k in range(6)]
+    depth = resid.shape[-1]
+    lane = lax.broadcasted_iota(jnp.int32, (HALO, depth), 1)
+    sublane = lax.broadcasted_iota(jnp.int32, (HALO, depth), 0)
+
+    def emit(row, low, high):
+        parts = []
+        for k in range(6):
+            turned = pltpu.roll(high[k], 1, 0)
+            if tail_out is not None:
+                tail_out[k, row] = turned
+            before = 0.0 if tail_in is None else tail_in[k, row]
+            parts.append(low[k] + jnp.where(sublane == 0, before, turned))
         at = pl.ds(pl.multiple_of(row * cols + first, 8), HALO)
         for c, value in enumerate(along_z(parts, lane)):
             resid[c, at, :] = applied[c, at, :] - value
 
-    def finish():
-        join(rows - 2)
-        join(rows - 1)
-
-    return put_near, put_far, lambda row: join(jnp.maximum(row - 1, 0)), finish
+    return emit
 
 
 def early_elements(
-    rows, cols, disp, dens, kind, inverse, applied, waves, far, resid, scaled, sums, near
+    rows, cols, disp, dens, kind, inverse, applied, waves, tail, resid, scaled, sums, *tails
 ):
     depth = disp.shape[-1]
     lane = lax.broadcasted_iota(jnp.int32, (HALO, depth), 1)
@@ -444,22 +433,20 @@
                     waves[3 * r + c, row, 8 * block : 8 * block + 8, :] = value
                     if block == 0:
                         waves[3 * r + c, row, cols + HALO :, :] = value
-        for k in range(6):
-            far[k, row, :8, :] = jnp.zeros((HALO, depth), jnp.float32)
         return nothing
 
     lax.fori_loop(0, rows, turn, 0, unroll=8)
     total = filled = jnp.zeros((HALO, depth), jnp.float32)
+    chain = (None, *tails, tail)
     for block in range(cols // 8 - 1):
         first = 8 * block
 
         def put(row, value, first=first):
             scaled[row, first + 8 : first + 16, :] = value
 
-        put_near, put_far, beside, finish = joiner(rows, cols, block, near, far, applied, resid, lane)
+        emit = joiner(cols, block, chain[block], chain[block + 1], applied, resid)
         state = own_state(dens, kind, cols, first)
-        more = march(rows, block, waves, state, inverse, put_near, put_far, put, True, beside=beside)
-        finish()
+        more = march(rows, block, waves, state, inverse, emit, put, True)
         total, filled = total + more[0], filled + more[1]
     sums[0] = total
     sums[1] = filled
@@ -467,11 +454,11 @@
 
 def late_elements(
     rows, cols,
-    waves_in, far_in, resid_in, scaled_in, dens, kind, edge_u, edge_f, edge_s, applied, inverse, sums_a,
-    waves, far, resid, scaled, sums, near, far_h,
+    waves_in, resid_in, scaled_in, tail, dens, kind, edge_u, edge_f, edge_s, applied, inverse, sums_a,
+    waves, resid, scaled, sums, resid_out, near, filtered, far_h, sem,
 ):
     depth = dens.shape[-1]
-    del waves_in, far_in, resid_in, scaled_in
+    del waves_in, resid_in, scaled_in
     wide = cols + HALO
     lane = lax.broadcasted_iota(jnp.int32, (HALO, depth), 1)
 
@@ -492,19 +479,19 @@
         scaled[row, :HALO, :] = value
         scaled[row, wide:, :] = value
 
-    def far_edge(k, row, value):
-        far_h[pl.ds(pl.multiple_of((k * rows + row) * HALO, 8), HALO), :] = value
-
-    march(rows, cols // 8, waves, edge_state, inverse, None, far_edge, put_edge, False)
+    def emit_edge(row, low, high):
+        for k in range(6):
+            far_h[pl.ds(pl.multiple_of((k * rows + row) * HALO, 8), HALO), :] = high[k]
+
+    march(rows, cols // 8, waves, edge_state, inverse, emit_edge, put_edge, False)
     last = cols // 8 - 1
 
     def put(row, value):
         scaled[row, cols:wide, :] = value
 
-    put_near, put_far, beside, finish = joiner(rows, cols, last, near, far, applied, resid, lane)
+    emit = joiner(cols, last, tail, None, applied, resid)
     state = own_state(dens, kind, cols, 8 * last)
-    total, filled = march(rows, last, waves, state, inverse, put_near, put_far, put, True, beside=beside)
-    finish()
+    total, filled = march(rows, last, waves, state, inverse, emit, put, True)
     sums[0] = sums_a[0] + total
     sums[1] = sums_a[1] + filled
 
@@ -512,6 +499,19 @@
     at = pl.ds(0, rows, stride=cols)
     for c, value in enumerate(along_z(parts, lax.broadcasted_iota(jnp.int32, (rows, depth), 1))):
         resid[c, at, :] = resid[c, at, :] - value
+    middle = pl.ds(cols, (rows - 2) * cols)
+    copy = pltpu.make_async_copy(resid.at[:, middle, :], resid_out.at[:, middle, :], sem)
+    copy.start()
+
+    def own(row, nothing):
+        lines_y(near, row + RADIUS, cols, lambda start: scaled[row, start : start + 8, :])
+        return nothing
+
+    lax.fori_loop(0, rows - 1, own, 0, unroll=True)
+    for row in range(RADIUS, rows - RADIUS - 1):
+        for block in range(last + 1):
+            filtered[row, 8 * block : 8 * block + 8, :] = filter_row(near, row, block, lane)
+    copy.wait()
 
 
 def outer_elements(
@@ -617,22 +617,54 @@
         send(out_b, out_a)
 
 
-def filter_rows(
+def lines_y(near, row, cols, load):
+    for block in range(cols // 8):
+        start = HALO + 8 * block
+        near[0, row, 8 * block : 8 * block + 8, :] = load(start)
+        for shift in range(1, RADIUS + 1):
+            near[shift, row, 8 * block : 8 * block + 8, :] = load(start + shift) + load(start - shift)
+
+
+def filter_row(near, row, block, lane):
+    depth = near.shape[-1]
+    at = pl.ds(block * 8, 8)
+    classes = {}
+    for shift_x in range(RADIUS + 1):
+        for shift_y in range(RADIUS + 1):
+            square = shift_x * shift_x + shift_y * shift_y
+            if square not in CLASSES:
+                continue
+            value = near[shift_y, row + (RADIUS + shift_x), at, :]
+            if shift_x:
+                value = value + near[shift_y, row + (RADIUS - shift_x), at, :]
+            classes[square] = value if square not in classes else classes[square] + value
+    result = None
+    for shift_z in range(RADIUS + 1):
+        line = None
+        for square, value in classes.items():
+            weight = weight_of(square + shift_z * shift_z)
+            if weight > 0.0:
+                line = weight * value if line is None else line + weight * value
+        if shift_z:
+            up = jnp.where(lane < shift_z, 0.0, pltpu.roll(line, shift_z, 1))
+            down = jnp.where(lane >= depth - shift_z, 0.0, pltpu.roll(line, depth - shift_z, 1))
+            line = up + down
+        result = line if result is None else result + line
+    return result
+
+
+def filter_rest(
     rows, cols, count_x, cells,
-    scaled, final, got_a, got_b, parts, inner, outer,
+    near_in, inner, final, got_a, got_b, parts, outer, resid_in,
     sens, resid, comp, vol, near, ends, result_v, sems,
 ):
     depth = sens.shape[-1]
+    del near_in, resid_in
     wide = cols + HALO
     copies = [
-        pltpu.make_async_copy(
-            inner.at[:, pl.ds(cols, (rows - 2) * cols), :], resid.at[:, pl.ds(cols, (rows - 2) * cols), :], sems.at[0]
-        )
+        pltpu.make_async_copy(outer.at[index], resid.at[:, pl.ds(row * cols, cols), :], sems.at[index])
+        for index, row in enumerate((0, rows - 1))
     ]
-    for index, row in enumerate((0, rows - 1)):
-        copies.append(
-            pltpu.make_async_copy(outer.at[index], resid.at[:, pl.ds(row * cols, cols), :], sems.at[1 + index])
-        )
     for copy in copies:
         copy.start()
     here = lax.axis_index("gx")
@@ -648,12 +680,17 @@
     vol[0, 0] = volume / cells
     scale = cells / jnp.broadcast_to(compliance, (8, depth))
 
-    def lines_y(row, load):
+    def send(start, size):
+        at = pl.ds(start, size)
+        copies.append(pltpu.make_async_copy(result_v.at[at], sens.at[at], sems.at[len(copies)]))
+        copies[-1].start()
+
+    low_end, high_start = RADIUS, rows - RADIUS - 1
+    for row in range(low_end, high_start):
         for block in range(cols // 8):
-            start = 8 + 8 * block
-            near[0, row, 8 * block : 8 * block + 8, :] = load(start)
-            for shift in range(1, RADIUS + 1):
-                near[shift, row, 8 * block : 8 * block + 8, :] = load(start + shift) + load(start - shift)
+            at = pl.ds(block * 8, 8)
+            result_v[row, at, :] = inner[row, at, :] * scale
+    send(low_end, high_start - low_end)
 
     def take(low, high):
         for index in range(RADIUS):
@@ -671,61 +708,15 @@
         take(got_a, got_b)
 
     for index in range(RADIUS):
-        lines_y(index, lambda start, at=index: ends[at, start : start + 8, :])
-        lines_y(rows + RADIUS + index, lambda start, at=RADIUS + index: ends[at, start : start + 8, :])
-    lines_y(rows + RADIUS - 1, lambda start: final[start : start + 8, :])
-
-    def own(row, carry):
-        lines_y(row + RADIUS, lambda start: scaled[row, start : start + 8, :])
-        return carry
-
-    lax.fori_loop(0, rows - 1, own, 0, unroll=True)
+        lines_y(near, index, cols, lambda start, at=index: ends[at, start : start + 8, :])
+        lines_y(near, rows + RADIUS + index, cols, lambda start, at=RADIUS + index: ends[at, start : start + 8, :])
+    lines_y(near, rows + RADIUS - 1, cols, lambda start: final[start : start + 8, :])
     lane = lax.broadcasted_iota(jnp.int32, (8, depth), 1)
-    blocks = cols // 8
-
-    def lines_of(row):
-        lines = []
-        for block in range(blocks):
-            at = pl.ds(block * 8, 8)
-            classes = {}
-            for shift_x in range(RADIUS + 1):
-                for shift_y in range(RADIUS + 1):
-                    square = shift_x * shift_x + shift_y * shift_y
-                    if square not in CLASSES:
-                        continue
-                    value = near[shift_y, row + (RADIUS + shift_x), at, :]
-                    if shift_x:
-                        value = value + near[shift_y, row + (RADIUS - shift_x), at, :]
-                    classes[square] = value if square not in classes else classes[square] + value
-            for shift_z in range(RADIUS + 1):
-                line = None
-                for square, value in classes.items():
-                    weight = weight_of(square + shift_z * shift_z)
-                    if weight > 0.0:
-                        line = weight * value if line is None else line + weight * value
-                lines.append(line)
-        return tuple(lines)
-
-    def write(row, lines):
-        for block in range(blocks):
-            result, *rest = lines[(RADIUS + 1) * block : (RADIUS + 1) * (block + 1)]
-            for shift_z, line in enumerate(rest, 1):
-                up = jnp.where(lane < shift_z, 0.0, pltpu.roll(line, shift_z, 1))
-                down = jnp.where(lane >= depth - shift_z, 0.0, pltpu.roll(line, depth - shift_z, 1))
-                result = result + (up + down)
-            result_v[row, 8 * block : 8 * block + 8, :] = result * scale
-
-    def out_row(row, nothing):
-        write(row, lines_of(row))
-        return nothing
-
-    pieces = 4
-    size = rows // pieces
-    for piece in range(pieces):
-        lax.fori_loop(piece * size, (piece + 1) * size, out_row, 0, unroll=size)
-        at = pl.ds(piece * size, size)
-        copies.append(pltpu.make_async_copy(result_v.at[at], sens.at[at], sems.at[3 + piece]))
-        copies[-1].start()
+    for start, stop in ((0, low_end), (high_start, rows)):
+        for row in range(start, stop):
+            for block in range(cols // 8):
+                result_v[row, 8 * block : 8 * block + 8, :] = filter_row(near, row, block, lane) * scale
+        send(start, stop - start)
     for copy in copies:
         copy.wait()
 
@@ -808,17 +799,17 @@
     )
 
     early = cols - HALO
-    waves, far, inner, scaled, sums = call(
+    waves, tail, inner, scaled, sums = call(
         functools.partial(early_elements, rows, cols),
         [
             f32(6, rows, wide + HALO, depth),
-            f32(6, rows, wide, depth),
+            f32(6, rows, HALO, depth),
             f32(3, rows * cols, depth),
             f32(rows, wide + HALO, depth),
             f32(2, 8, depth),
         ],
         [disp, dens, kind, inverse, applied],
-        scratch=[vmem(6, rows, HALO, depth)],
+        scratch=[vmem(6, rows, HALO, depth)] * (cols // HALO - 2),
         flops=250 * rows * early * depth,
     )
 
@@ -831,13 +822,15 @@
     got_a = lax.ppermute(send_a, "gx", pairs_xa)
     got_b = lax.ppermute(send_b, BOTH, pairs_xb)
 
-    waves, far, inner, scaled, sums = call(
+    waves, inner, scaled, sums, resid, near, filtered = call(
         functools.partial(late_elements, rows, cols),
-        [f32(*v.shape) for v in (waves, far, inner, scaled, sums)],
-        [waves, far, inner, scaled, dens, kind, edge_u, edge_f, edge_s, applied, inverse, sums],
-        scratch=[vmem(6, rows, HALO, depth), vmem(6 * rows * HALO, depth)],
+        [f32(*v.shape) for v in (waves, inner, scaled, sums)]
+        + [f32(3, rows * cols, depth), f32(RADIUS + 1, rows + 2 * RADIUS, cols, depth), f32(rows, cols, depth)],
+        [waves, inner, scaled, tail, dens, kind, edge_u, edge_f, edge_s, applied, inverse, sums],
+        scratch=[vmem(6 * rows * HALO, depth), pltpu.SemaphoreType.DMA],
+        out_places={4: pltpu.HBM},
         flops=250 * rows * 2 * HALO * depth,
-        aliases={0: 0, 1: 1, 2: 2, 3: 3},
+        aliases={0: 0, 1: 1, 2: 2},
     )
     outer, final, send_a, send_b, parts = call(
         functools.partial(outer_elements, rows, cols, count_x, devices),
@@ -850,18 +843,15 @@
     got_b = lax.ppermute(send_b, BOTH, pairs_xb)
     parts = lax.all_to_all(parts, BOTH, 0, 0, tiled=True)
 
-    sens, resid, comp, volume = call(
-        functools.partial(filter_rows, rows, cols, count_x, cells),
-        [f32(rows, cols, depth), f32(3, rows * cols, depth), f32(1, 1), f32(1, 1)],
-        [scaled, final, got_a, got_b, parts, inner, outer],
-        scratch=[
-            vmem(RADIUS + 1, rows + 2 * RADIUS, cols, depth),
-            vmem(2 * RADIUS, wide + HALO, depth),
-            vmem(rows, cols, depth),
-            pltpu.SemaphoreType.DMA((7,)),
-        ],
+    sens, resid, comp, volume, _ = call(
+        functools.partial(filter_rest, rows, cols, count_x, cells),
+        [f32(rows, cols, depth), f32(3, rows * cols, depth), f32(1, 1), f32(1, 1), f32(*near.shape)],
+        [near, filtered, final, got_a, got_b, parts, outer, resid],
+        scratch=[vmem(2 * RADIUS, wide + HALO, depth), vmem(rows, cols, depth), pltpu.SemaphoreType.DMA((5,))],
+        places={7: pltpu.HBM},
         out_places={0: pltpu.HBM, 1: pltpu.HBM, 2: pltpu.SMEM, 3: pltpu.SMEM},
-        flops=60 * rows * cols * depth,
+        flops=20 * rows * cols * depth,
+        aliases={0: 4, 7: 1},
     )
     return (
         sens,

time: 33.7 us -> 32.4 us (0.961)
  Pallas kernels: 12.6 us -> 11.8 us
  blocking collectives: 12.3 us -> 11.7 us
    ppermute x2, starting transfers between devices: 3.47 us -> 4.72 us  [on_device(): got_a = lax.ppermute(send_a, 'gx', pairs_xa)]
    ppermute x2, starting transfers between devices: 0.92 us -> 0.01 us  [on_device(): got_b = lax.ppermute(send_b, BOTH, pairs_xb)]
    pallas_call x7, Pallas kernels: 12.6 us -> 11.8 us  [call(): pl.pallas_call(body, out_shape=[FULL(v.shape, v.dtype) for v in shapes],...]
    all_to_all x1, blocking collectives: 12.3 us -> 11.7 us  [on_device(): parts = lax.all_to_all(parts, BOTH, 0, 0, tiled=True)]
  transfers between devices with their start and end apart: 6 -> 6, of which waited for: 1 -> 0; matrix products, arithmetic and copies ran while one was open for 0% -> 0% of each run, Pallas kernels for 25% -> 26%
where the time goes in v4:
time: 32.4 us; the launch traced here: 32.2 us
  Pallas kernels  11.8 us (36%)
  blocking collectives  11.7 us (36%)
  starting transfers between devices  7.83 us (24%)
  between operations  0.79 us (2%)
    pallas_call x7, Pallas kernels, call(): pl.pallas_call(body, out_shape=[FULL(v.shape, v.dtype) for v in shapes],...  11.8 us
    all_to_all x1, blocking collectives, on_device(): parts = lax.all_to_all(parts, BOTH, 0, 0, tiled=True)  11.7 us
    ppermute x2, starting transfers between devices, on_device(): got_a = lax.ppermute(send_a, 'gx', pairs_xa)  4.72 us
    ppermute x1, starting transfers between devices, on_device(): got_b = lax.ppermute(send_b, BOTH, pairs_yb)  2.59 us
  transfers between devices with their start and end apart: 6, of which 0 were waited for; matrix products, arithmetic and copies ran while one was open for 0% of the time, Pallas kernels for 26%

profile of v4, /device:TPU:0, one launch (start us, length us, event | category | flops | bytes accessed | tf_op | source)
XLA Modules:
  0.0 32.2 jit_solution(17668799251005768350)
XLA Ops:
  0.6 0.0 copy-start.7
  0.7 1.3 %shard_map.111 = (f32[480,128]{1,0:T(8,128)S(1)}, f32[480,128]{1,0:T(8,128)S(1)}, f32[8,128]{1,0:T(8,128)S(1)}) custom-call(f32[3,32,24,128]{3,2,1,0:T(8,128)} %disp.1, f32[32,24,128]{2,1,0:T(8,128)} %dens.1, s32[32,24,128]{2,1,0:T(8,128)} %kind.1), custom_call_target="tpu_custom_call" | custom-call | bytes 2461696 | tf_op jit(solution)/shard_map/pallas_call | solution.py:729
  2.0 0.5 %collective-permute-start = (f32[480,128]{1,0:T(8,128)S(1)}, f32[480,128]{1,0:T(8,128)S(1)}, u32[]{:S(2)}, u32[]{:S(2)}) collective-permute-start(f32[480,128]{1,0:T(8,128)S(1)} %get-tuple-element.43), channel_id=1, source_target_pairs={{0,1},{1,0},{2,3},{3,2},{4,5},{5,4},{6,7},{7,6},{8,9},{9,8},{10,11... | collective-permute-start | bytes 737288 | tf_op jit(solution)/shard_map/ppermute | solution.py:783
  2.5 2.6 %collective-permute-start.1 = (f32[480,128]{1,0:T(8,128)S(1)}, f32[480,128]{1,0:T(8,128)S(1)}, u32[]{:S(2)}, u32[]{:S(2)}) collective-permute-start(f32[480,128]{1,0:T(8,128)S(1)} %get-tuple-element.44), channel_id=1, source_target_pairs={{0,4},{1,2},{2,1},{3,7},{4,0},{5,6},{6,5},{7,3},{8,12},{9,10},{10,... | collective-permute-start | bytes 737288 | tf_op jit(solution)/shard_map/ppermute | solution.py:784
  5.2 0.0 copy-start
  5.2 0.0 copy-start.1
  5.2 0.0 copy-start.2
  5.2 1.9 %shard_map.112 = (f32[3,768,128]{2,1,0:T(8,128)S(1)}, f32[7,32,128]{2,1,0:T(8,128)S(1)}) custom-call(f32[8,128]{1,0:T(8,128)S(1)} %get-tuple-element.35.after, s32[1,1024]{1,0:T(1,128)S(1)} %bitcast.25, s32[1,1024]{1,0:T(1,128)S(1)} %bitcast.26, s32[1,1024]{1,0:T(1,128)S(1)} %bitcast.27, f32[3,1024]{1,0:T(4,128)S(1)} %copy-done.3, f32[8,128]{1,0:T(8,128)S(1)} %copy-done.7), custom_call_target="tpu_custom_call" | custom-call | flops 1207959552 | bytes 1327104 | tf_op jit(solution)/shard_map/pallas_call | solution.py:729
  7.2 2.6 %shard_map.113 = (f32[6,32,40,128]{3,2,1,0:T(8,128)S(1)}, f32[6,32,8,128]{3,2,1,0:T(8,128)S(1)}, f32[3,768,128]{2,1,0:T(8,128)S(1)}, f32[32,40,128]{2,1,0:T(8,128)S(1)}, f32[2,8,128]{2,1,0:T(8,128)S(1)}) custom-call(f32[2304,128]{1,0:T(8,128)S(1)} %bitcast.13, f32[768,128]{1,0:T(8,128)S(1)} %bitcast.15, s32[768,128]{1,0:T(8,128)S(1)} %bitcast.19, ...), custom_call_target="tpu_custom_call" | custom-call | flops 16384000 | bytes 9822208 | tf_op jit(solution)/shard_map/pallas_call | solution.py:729
  9.8 0.0 collective-permute-done.got_a
  9.8 0.0 collective-permute-done.1.got_b
  9.8 0.1 shard_map.114
  9.9 1.6 %collective-permute-start.2 = (f32[4,32,128]{2,1,0:T(8,128)S(1)}, f32[4,32,128]{2,1,0:T(8,128)S(1)}, u32[]{:S(2)}, u32[]{:S(2)}) collective-permute-start(f32[4,32,128]{2,1,0:T(8,128)S(1)} %get-tuple-element.51), channel_id=1, source_target_pairs={{0,4},{4,0},{8,12},{12,8},{16,20},{20,16},{24,28},{28,24},{1,5},{5... | collective-permute-start | bytes 196616 | tf_op jit(solution)/shard_map/ppermute | solution.py:822
  11.5 0.0 collective-permute-start.3
  11.5 3.8 %shard_map.115 = (f32[6,32,40,128]{3,2,1,0:T(8,128)S(1)}, f32[3,768,128]{2,1,0:T(8,128)S(1)}, f32[32,40,128]{2,1,0:T(8,128)S(1)}, f32[2,8,128]{2,1,0:T(8,128)S(1...) custom-call(f32[6,32,40,128]{3,2,1,0:T(8,128)S(1)} %get-tuple-elemen, ...), custom_call_target="tpu_custom_call", output_to_operand_aliasing={{0}: (0, {}), {1}: (1, {}), {2}: (2, {})} | custom-call | flops 16384000 | bytes 18513920 | tf_op jit(solution)/shard_map/pallas_call | solution.py:729
  15.3 0.0 collective-permute-done.2.got_a
  15.4 0.0 collective-permute-done.3.got_b
  15.4 0.4 %shard_map.116 = (f32[2,3,24,128]{3,2,1,0:T(8,128)S(1)}, f32[40,128]{1,0:T(8,128)S(1)}, f32[3,32,128]{2,1,0:T(8,128)S(1)}, f32[3,32,128]{2,1,0:T(8,128)S(1)}, f32[32,128]{1,0:T(8,128)S(1)}) custom-call(f32[6,32,40,128]{3,2,1,0:T(8,128)S(1)} %get-tuple-element.50.waves, f32[768,128]{1,0:T(8,128)S(1)} %bitcast.18, s32[768,128]{1,0:T(8,128)S(1)} %bitcast.22, ...), custom_call_target="tpu_custom_call" | custom-call | flops 2048000 | bytes 7278592 | tf_op jit(solution)/shard_map/pallas_call | solution.py:729
  15.8 3.1 %collective-permute-start.4 = (f32[3,32,128]{2,1,0:T(8,128)S(1)}, f32[3,32,128]{2,1,0:T(8,128)S(1)}, u32[]{:S(2)}, u32[]{:S(2)}) collective-permute-start(f32[3,32,128]{2,1,0:T(8,128)S(1)} %get-tuple-element.57), channel_id=1, source_target_pairs={{0,4},{4,0},{8,12},{12,8},{16,20},{20,16},{24,28},{28,24},{1,5},{5... | collective-permute-start | bytes 147464 | tf_op jit(solution)/shard_map/ppermute | solution.py:842
  18.9 0.0 collective-permute-start.5
  18.9 11.7 %all_to_all.11 = f32[32,1,128]{2,1,0:T(1,128)S(1)} all-to-all(f32[32,1,128]{2,1,0:T(1,128)S(1)} %bitcast.24), channel_id=1, replica_groups=mesh['gx'=8,'gy'=4] {'gx','gy'}, dimensions={0} | all-to-all | bytes 32768 | tf_op jit(solution)/shard_map/all_to_all | solution.py:844
  30.6 0.0 collective-permute-done.4.got_a
  30.6 0.0 collective-permute-done.5.got_b
  30.6 1.6 %shard_map.117 = (f32[32,24,128]{2,1,0:T(8,128)}, f32[3,768,128]{2,1,0:T(8,128)}, f32[1,1]{1,0:T(1,128)}, f32[1,1]{1,0:T(1,128)}, f32[4,38,24,128]{3,2,1,0:T(8,128)S(1)}) custom-call(f32[4,38,24,128]{3,2,1,0:T(8,128)S(1)} %get-tuple-element.48.near_in, f32[32,24,128]{2,1,0:T(8,128)S(1)} %get-tuple-element.49.inner, ...), custom_call_target="tpu_custom_call", output_to_operand_aliasing={{4}: (0, {}), {1}: (7, {})} | custom-call | flops 1966080 | bytes 7090184 | tf_op jit(solution)/shard_map/pallas_call | solution.py:729
  (12 shorter events, 0.0 us)
Async XLA Ops:
  0.6 4.5 %copy-start.7 = (f32[8,128]{1,0:T(8,128)S(1)}, f32[8,128]{1,0:T(8,128)}, u32[]{:S(2)}) copy-start(f32[8,128]{1,0:T(8,128)} %constant.2.clone.sums) | copy-start | bytes 12292
  0.6 4.5 %copy-start.3 = (f32[3,1024]{1,0:T(4,128)S(1)}, f32[3,1024]{1,0:T(4,128)}, u32[]{:S(2)}) copy-start(f32[3,1024]{1,0:T(4,128)} %force.1) | copy-start | bytes 36868
  0.7 4.5 %copy-start.6 = (s32[1024]{0:T(1024)S(1)}, s32[1024]{0:T(1024)}, u32[]{:S(2)}) copy-start(s32[1024]{0:T(1024)} %param.13) | copy-start | bytes 12292
  0.7 4.5 %copy-start.5 = (s32[1024]{0:T(1024)S(1)}, s32[1024]{0:T(1024)}, u32[]{:S(2)}) copy-start(s32[1024]{0:T(1024)} %param.12) | copy-start | bytes 12292
  0.7 4.5 %copy-start.4 = (s32[1024]{0:T(1024)S(1)}, s32[1024]{0:T(1024)}, u32[]{:S(2)}) copy-start(s32[1024]{0:T(1024)} %param.11) | copy-start | bytes 12292
  2.0 7.7 %collective-permute-start = (f32[480,128]{1,0:T(8,128)S(1)}, f32[480,128]{1,0:T(8,128)S(1)}, u32[]{:S(2)}, u32[]{:S(2)}) collective-permute-start(f32[480,128]{1,0:T(8,128)S(1)} %get-tuple-element.43), channel_id=1, source_target_pairs={{0,1},{1,0},{2,3},{3,2},{4,5},{5,4},{6,7},{7,6},{8,9},{9,8},{10,11... | collective-permute-start | bytes 737288 | tf_op jit(solution)/shard_map/ppermute | solution.py:783
  2.5 7.2 %collective-permute-start.1 = (f32[480,128]{1,0:T(8,128)S(1)}, f32[480,128]{1,0:T(8,128)S(1)}, u32[]{:S(2)}, u32[]{:S(2)}) collective-permute-start(f32[480,128]{1,0:T(8,128)S(1)} %get-tuple-element.44), channel_id=1, source_target_pairs={{0,4},{1,2},{2,1},{3,7},{4,0},{5,6},{6,5},{7,3},{8,12},{9,10},{10,... | collective-permute-start | bytes 737288 | tf_op jit(solution)/shard_map/ppermute | solution.py:784
  5.2 2.0 %copy-start = (f32[3,32,24,128]{3,2,1,0:T(8,128)S(1)}, f32[3,32,24,128]{3,2,1,0:T(8,128)}, u32[]{:S(2)}) copy-start(f32[3,32,24,128]{3,2,1,0:T(8,128)} %disp.1) | copy-start | bytes 3538948
  5.2 2.0 %copy-start.1 = (f32[32,24,128]{2,1,0:T(8,128)S(1)}, f32[32,24,128]{2,1,0:T(8,128)}, u32[]{:S(2)}) copy-start(f32[32,24,128]{2,1,0:T(8,128)} %dens.1) | copy-start | bytes 1179652
  5.2 2.0 %copy-start.2 = (s32[32,24,128]{2,1,0:T(8,128)S(1)}, s32[32,24,128]{2,1,0:T(8,128)}, u32[]{:S(2)}) copy-start(s32[32,24,128]{2,1,0:T(8,128)} %kind.1) | copy-start | bytes 1179652
  9.9 5.4 %collective-permute-start.2 = (f32[4,32,128]{2,1,0:T(8,128)S(1)}, f32[4,32,128]{2,1,0:T(8,128)S(1)}, u32[]{:S(2)}, u32[]{:S(2)}) collective-permute-start(f32[4,32,128]{2,1,0:T(8,128)S(1)} %get-tuple-element.51), channel_id=1, source_target_pairs={{0,4},{4,0},{8,12},{12,8},{16,20},{20,16},{24,28},{28,24},{1,5},{5... | collective-permute-start | bytes 196616 | tf_op jit(solution)/shard_map/ppermute | solution.py:822
  11.5 3.8 %collective-permute-start.3 = (f32[4,32,128]{2,1,0:T(8,128)S(1)}, f32[4,32,128]{2,1,0:T(8,128)S(1)}, u32[]{:S(2)}, u32[]{:S(2)}) collective-permute-start(f32[4,32,128]{2,1,0:T(8,128)S(1)} %get-tuple-element.52), channel_id=1, source_target_pairs={{0,1},{1,0},{2,3},{3,2},{4,8},{5,9},{6,10},{7,11},{8,4},{9,5},{10,... | collective-permute-start | bytes 196616 | tf_op jit(solution)/shard_map/ppermute | solution.py:823
  15.8 14.8 %collective-permute-start.4 = (f32[3,32,128]{2,1,0:T(8,128)S(1)}, f32[3,32,128]{2,1,0:T(8,128)S(1)}, u32[]{:S(2)}, u32[]{:S(2)}) collective-permute-start(f32[3,32,128]{2,1,0:T(8,128)S(1)} %get-tuple-element.57), channel_id=1, source_target_pairs={{0,4},{4,0},{8,12},{12,8},{16,20},{20,16},{24,28},{28,24},{1,5},{5... | collective-permute-start | bytes 147464 | tf_op jit(solution)/shard_map/ppermute | solution.py:842
  18.9 11.7 %collective-permute-start.5 = (f32[3,32,128]{2,1,0:T(8,128)S(1)}, f32[3,32,128]{2,1,0:T(8,128)S(1)}, u32[]{:S(2)}, u32[]{:S(2)}) collective-permute-start(f32[3,32,128]{2,1,0:T(8,128)S(1)} %get-tuple-element.58), channel_id=1, source_target_pairs={{0,1},{1,0},{2,3},{3,2},{4,8},{5,9},{6,10},{7,11},{8,4},{9,5},{10,... | collective-permute-start | bytes 147464 | tf_op jit(solution)/shard_map/ppermute | solution.py:843

commit v5 on v4

--- a/solution.py
+++ b/solution.py
@@ -15,6 +15,7 @@
 HALO = 8
 BOTH = ("gx", "gy")
 FULL = jax.ShapeDtypeStruct
+FILTER_ROWS = 12
 
 
 def element_matrix():
@@ -255,14 +256,11 @@
             part.append(jnp.where(hit_z, piece, 0.0).astype(jnp.bfloat16))
     place = lax.broadcasted_iota(jnp.int32, (rows * cols, loads), 0)
     left = jnp.where(place == target, 1.0, 0.0).astype(jnp.bfloat16)
-    product = None
-    for part in right:
-        piece = lax.dot_general(
-            left, jnp.concatenate(part, axis=0), (((1,), (1,)), ((), ())), preferred_element_type=jnp.float32
-        )
-        product = piece if product is None else product + piece
+    product = lax.dot_general(
+        left, jnp.concatenate(right[0] + right[1], axis=0), (((1,), (1,)), ((), ())), preferred_element_type=jnp.float32
+    )
     for c in range(3):
-        applied[c] = product[:, c * depth : (c + 1) * depth]
+        applied[c] = product[:, c * depth : (c + 1) * depth] + product[:, (3 + c) * depth : (4 + c) * depth]
 
     wide = cols + HALO
     total_x, total_y = rows * count_x, cols * count_y
@@ -455,7 +453,7 @@
 def late_elements(
     rows, cols,
     waves_in, resid_in, scaled_in, tail, dens, kind, edge_u, edge_f, edge_s, applied, inverse, sums_a,
-    waves, resid, scaled, sums, resid_out, near, filtered, far_h, sem,
+    waves, resid, scaled, sums, resid_out, near, filtered, far_h, lines, sem,
 ):
     depth = dens.shape[-1]
     del waves_in, resid_in, scaled_in
@@ -508,9 +506,12 @@
         return nothing
 
     lax.fori_loop(0, rows - 1, own, 0, unroll=True)
-    for row in range(RADIUS, rows - RADIUS - 1):
-        for block in range(last + 1):
-            filtered[row, 8 * block : 8 * block + 8, :] = filter_row(near, row, block, lane)
+    band = bands(depth)
+    inside = range(RADIUS + 1, rows - RADIUS - 1)
+    for start in inside[:: FILTER_ROWS]:
+        picks = range(start, min(start + FILTER_ROWS, inside.stop))
+        rest = filter_rows(near, lines, filtered, picks, cols, band)
+        filtered[picks.start : picks.stop] = filtered[picks.start : picks.stop] + rest
     copy.wait()
 
 
@@ -625,38 +626,53 @@
             near[shift, row, 8 * block : 8 * block + 8, :] = load(start + shift) + load(start - shift)
 
 
-def filter_row(near, row, block, lane):
+def bands(depth):
+    row = lax.broadcasted_iota(jnp.int32, (depth, depth), 0)
+    column = lax.broadcasted_iota(jnp.int32, (depth, depth), 1)
+    away = jnp.abs(row - column)
+    return jnp.concatenate(
+        [jnp.where(away == shift, 1.0, 0.0).astype(jnp.bfloat16) for shift in range(1, RADIUS + 1)], axis=0
+    )
+
+
+def filter_rows(near, lines, result, picks, cols, band):
     depth = near.shape[-1]
-    at = pl.ds(block * 8, 8)
-    classes = {}
-    for shift_x in range(RADIUS + 1):
-        for shift_y in range(RADIUS + 1):
-            square = shift_x * shift_x + shift_y * shift_y
-            if square not in CLASSES:
-                continue
-            value = near[shift_y, row + (RADIUS + shift_x), at, :]
-            if shift_x:
-                value = value + near[shift_y, row + (RADIUS - shift_x), at, :]
-            classes[square] = value if square not in classes else classes[square] + value
-    result = None
-    for shift_z in range(RADIUS + 1):
-        line = None
-        for square, value in classes.items():
-            weight = weight_of(square + shift_z * shift_z)
-            if weight > 0.0:
-                line = weight * value if line is None else line + weight * value
-        if shift_z:
-            up = jnp.where(lane < shift_z, 0.0, pltpu.roll(line, shift_z, 1))
-            down = jnp.where(lane >= depth - shift_z, 0.0, pltpu.roll(line, depth - shift_z, 1))
-            line = up + down
-        result = line if result is None else result + line
-    return result
+    for rank, row in enumerate(picks):
+        for block in range(cols // 8):
+            at = pl.ds(block * 8, 8)
+            classes = {}
+            for shift_x in range(RADIUS + 1):
+                for shift_y in range(RADIUS + 1):
+                    square = shift_x * shift_x + shift_y * shift_y
+                    if square not in CLASSES:
+                        continue
+                    value = near[shift_y, row + (RADIUS + shift_x), at, :]
+                    if shift_x:
+                        value = value + near[shift_y, row + (RADIUS - shift_x), at, :]
+                    classes[square] = value if square not in classes else classes[square] + value
+            for shift_z in range(RADIUS + 1):
+                line = None
+                for square, value in classes.items():
+                    weight = weight_of(square + shift_z * shift_z)
+                    if weight > 0.0:
+                        line = weight * value if line is None else line + weight * value
+                if shift_z:
+                    first = rank * cols + 8 * block
+                    lines[first : first + 8, (shift_z - 1) * depth : shift_z * depth] = line
+                else:
+                    result[row, at, :] = line
+    value = lines[: len(picks) * cols, :]
+    coarse = value.astype(jnp.bfloat16)
+    rest = (value - coarse.astype(jnp.float32)).astype(jnp.bfloat16)
+    total = jnp.dot(coarse, band, preferred_element_type=jnp.float32)
+    total = total + jnp.dot(rest, band, preferred_element_type=jnp.float32)
+    return total.reshape(len(picks), cols, depth)
 
 
 def filter_rest(
     rows, cols, count_x, cells,
     near_in, inner, final, got_a, got_b, parts, outer, resid_in,
-    sens, resid, comp, vol, near, ends, result_v, sems,
+    sens, resid, comp, vol, near, ends, result_v, lines, sems,
 ):
     depth = sens.shape[-1]
     del near_in, resid_in
@@ -685,7 +701,7 @@
         copies.append(pltpu.make_async_copy(result_v.at[at], sens.at[at], sems.at[len(copies)]))
         copies[-1].start()
 
-    low_end, high_start = RADIUS, rows - RADIUS - 1
+    low_end, high_start = RADIUS + 1, rows - RADIUS - 1
     for row in range(low_end, high_start):
         for block in range(cols // 8):
             at = pl.ds(block * 8, 8)
@@ -711,12 +727,11 @@
         lines_y(near, index, cols, lambda start, at=index: ends[at, start : start + 8, :])
         lines_y(near, rows + RADIUS + index, cols, lambda start, at=RADIUS + index: ends[at, start : start + 8, :])
     lines_y(near, rows + RADIUS - 1, cols, lambda start: final[start : start + 8, :])
-    lane = lax.broadcasted_iota(jnp.int32, (8, depth), 1)
-    for start, stop in ((0, low_end), (high_start, rows)):
-        for row in range(start, stop):
-            for block in range(cols // 8):
-                result_v[row, 8 * block : 8 * block + 8, :] = filter_row(near, row, block, lane) * scale
-        send(start, stop - start)
+    picks = (*range(low_end), *range(high_start, rows))
+    rest = filter_rows(near, lines, result_v, picks, cols, bands(depth))
+    for start, size, more in ((0, low_end, rest[:low_end]), (high_start, rows - high_start, rest[low_end:])):
+        result_v[start : start + size] = (result_v[start : start + size] + more) * scale[:1]
+        send(start, size)
     for copy in copies:
         copy.wait()
 
@@ -780,8 +795,8 @@
         places={0: pltpu.HBM, 1: pltpu.HBM, 2: pltpu.HBM},
         limit=53.25,
     )
+    got_b = lax.ppermute(send_b, BOTH, pairs_yb)
     got_a = lax.ppermute(send_a, "gy", pairs_ya)
-    got_b = lax.ppermute(send_b, BOTH, pairs_yb)
 
     sums = np.zeros((8, depth), np.float32)
     for rank, square in enumerate(CLASSES):
@@ -819,15 +834,19 @@
         [sums, disp, dens, kind, got_a, got_b],
         places={0: pl.ANY},
     )
+    got_b = lax.ppermute(send_b, BOTH, pairs_xb)
     got_a = lax.ppermute(send_a, "gx", pairs_xa)
-    got_b = lax.ppermute(send_b, BOTH, pairs_xb)
 
     waves, inner, scaled, sums, resid, near, filtered = call(
         functools.partial(late_elements, rows, cols),
         [f32(*v.shape) for v in (waves, inner, scaled, sums)]
         + [f32(3, rows * cols, depth), f32(RADIUS + 1, rows + 2 * RADIUS, cols, depth), f32(rows, cols, depth)],
         [waves, inner, scaled, tail, dens, kind, edge_u, edge_f, edge_s, applied, inverse, sums],
-        scratch=[vmem(6 * rows * HALO, depth), pltpu.SemaphoreType.DMA],
+        scratch=[
+            vmem(6 * rows * HALO, depth),
+            vmem(FILTER_ROWS * cols, RADIUS * depth),
+            pltpu.SemaphoreType.DMA,
+        ],
         out_places={4: pltpu.HBM},
         flops=250 * rows * 2 * HALO * depth,
         aliases={0: 0, 1: 1, 2: 2},
@@ -839,15 +858,20 @@
         scratch=[vmem(2, 6, wide + HALO, depth), vmem(wide, depth), vmem(2, 6, wide + 2 * HALO, depth)],
         flops=500 * wide * depth,
     )
+    got_b = lax.ppermute(send_b, BOTH, pairs_xb)
     got_a = lax.ppermute(send_a, "gx", pairs_xa)
-    got_b = lax.ppermute(send_b, BOTH, pairs_xb)
     parts = lax.all_to_all(parts, BOTH, 0, 0, tiled=True)
 
     sens, resid, comp, volume, _ = call(
         functools.partial(filter_rest, rows, cols, count_x, cells),
         [f32(rows, cols, depth), f32(3, rows * cols, depth), f32(1, 1), f32(1, 1), f32(*near.shape)],
         [near, filtered, final, got_a, got_b, parts, outer, resid],
-        scratch=[vmem(2 * RADIUS, wide + HALO, depth), vmem(rows, cols, depth), pltpu.SemaphoreType.DMA((5,))],
+        scratch=[
+            vmem(2 * RADIUS, wide + HALO, depth),
+            vmem(rows, cols, depth),
+            vmem(2 * (RADIUS + 1) * cols, RADIUS * depth),
+            pltpu.SemaphoreType.DMA((5,)),
+        ],
         places={7: pltpu.HBM},
         out_places={0: pltpu.HBM, 1: pltpu.HBM, 2: pltpu.SMEM, 3: pltpu.SMEM},
         flops=20 * rows * cols * depth,

time: 32.4 us -> 32.7 us (level)
  starting transfers between devices: 7.83 us -> 8.21 us
    ppermute x2, starting transfers between devices: 4.72 us -> 5.1 us  [on_device(): got_a = lax.ppermute(send_a, 'gx', pairs_xa)]
  transfers between devices with their start and end apart: 6 -> 6, of which waited for: 0 -> 0; matrix products, arithmetic and copies ran while one was open for 0% -> 0% of each run, Pallas kernels for 26% -> 25%
where the time goes in v5:
time: 32.7 us; the launch traced here: 32.6 us
  Pallas kernels  11.8 us (36%)
  blocking collectives  11.7 us (36%)
  starting transfers between devices  8.21 us (25%)
  between operations  0.8 us (2%)
    pallas_call x7, Pallas kernels, call(): pl.pallas_call(body, out_shape=[FULL(v.shape, v.dtype) for v in shapes],...  11.8 us
    all_to_all x1, blocking collectives, on_device(): parts = lax.all_to_all(parts, BOTH, 0, 0, tiled=True)  11.7 us
    ppermute x2, starting transfers between devices, on_device(): got_a = lax.ppermute(send_a, 'gx', pairs_xa)  5.1 us
    ppermute x1, starting transfers between devices, on_device(): got_b = lax.ppermute(send_b, BOTH, pairs_yb)  2.59 us
  transfers between devices with their start and end apart: 6, of which 0 were waited for; matrix products, arithmetic and copies ran while one was open for 0% of the time, Pallas kernels for 25%

profile of v5, /device:TPU:0, one launch (start us, length us, event | category | flops | bytes accessed | tf_op | source)
XLA Modules:
  0.0 32.6 jit_solution(4470968398543108841)
XLA Ops:
  0.6 0.0 copy-start.7
  0.7 1.3 %shard_map.111 = (f32[480,128]{1,0:T(8,128)S(1)}, f32[480,128]{1,0:T(8,128)S(1)}, f32[8,128]{1,0:T(8,128)S(1)}) custom-call(f32[3,32,24,128]{3,2,1,0:T(8,128)} %disp.1, f32[32,24,128]{2,1,0:T(8,128)} %dens.1, s32[32,24,128]{2,1,0:T(8,128)} %kind.1), custom_call_target="tpu_custom_call" | custom-call | bytes 2461696 | tf_op jit(solution)/shard_map/pallas_call | solution.py:744
  2.0 0.5 %collective-permute-start = (f32[480,128]{1,0:T(8,128)S(1)}, f32[480,128]{1,0:T(8,128)S(1)}, u32[]{:S(2)}, u32[]{:S(2)}) collective-permute-start(f32[480,128]{1,0:T(8,128)S(1)} %get-tuple-element.43), channel_id=1, source_target_pairs={{0,1},{1,0},{2,3},{3,2},{4,5},{5,4},{6,7},{7,6},{8,9},{9,8},{10,11... | collective-permute-start | bytes 737288 | tf_op jit(solution)/shard_map/ppermute | solution.py:799
  2.5 2.6 %collective-permute-start.1 = (f32[480,128]{1,0:T(8,128)S(1)}, f32[480,128]{1,0:T(8,128)S(1)}, u32[]{:S(2)}, u32[]{:S(2)}) collective-permute-start(f32[480,128]{1,0:T(8,128)S(1)} %get-tuple-element.44), channel_id=1, source_target_pairs={{0,4},{1,2},{2,1},{3,7},{4,0},{5,6},{6,5},{7,3},{8,12},{9,10},{10,... | collective-permute-start | bytes 737288 | tf_op jit(solution)/shard_map/ppermute | solution.py:798
  5.2 0.0 copy-start
  5.2 0.0 copy-start.1
  5.2 0.0 copy-start.2
  5.2 1.5 %shard_map.112 = (f32[3,768,128]{2,1,0:T(8,128)S(1)}, f32[7,32,128]{2,1,0:T(8,128)S(1)}) custom-call(f32[8,128]{1,0:T(8,128)S(1)} %get-tuple-element.35.after, s32[1,1024]{1,0:T(1,128)S(1)} %bitcast.25, s32[1,1024]{1,0:T(1,128)S(1)} %bitcast.26, s32[1,1024]{1,0:T(1,128)S(1)} %bitcast.27, f32[3,1024]{1,0:T(4,128)S(1)} %copy-done.3, f32[8,128]{1,0:T(8,128)S(1)} %copy-done.7), custom_call_target="tpu_custom_call" | custom-call | flops 1207959552 | bytes 1327104 | tf_op jit(solution)/shard_map/pallas_call | solution.py:744
  6.8 2.6 %shard_map.113 = (f32[6,32,40,128]{3,2,1,0:T(8,128)S(1)}, f32[6,32,8,128]{3,2,1,0:T(8,128)S(1)}, f32[3,768,128]{2,1,0:T(8,128)S(1)}, f32[32,40,128]{2,1,0:T(8,128)S(1)}, f32[2,8,128]{2,1,0:T(8,128)S(1)}) custom-call(f32[2304,128]{1,0:T(8,128)S(1)} %bitcast.13, f32[768,128]{1,0:T(8,128)S(1)} %bitcast.15, s32[768,128]{1,0:T(8,128)S(1)} %bitcast.19, ...), custom_call_target="tpu_custom_call" | custom-call | flops 16384000 | bytes 9822208 | tf_op jit(solution)/shard_map/pallas_call | solution.py:744
  9.4 0.0 collective-permute-done.got_a
  9.4 0.0 collective-permute-done.1.got_b
  9.4 0.1 shard_map.114
  9.6 2.0 %collective-permute-start.2 = (f32[4,32,128]{2,1,0:T(8,128)S(1)}, f32[4,32,128]{2,1,0:T(8,128)S(1)}, u32[]{:S(2)}, u32[]{:S(2)}) collective-permute-start(f32[4,32,128]{2,1,0:T(8,128)S(1)} %get-tuple-element.51), channel_id=1, source_target_pairs={{0,4},{4,0},{8,12},{12,8},{16,20},{20,16},{24,28},{28,24},{1,5},{5... | collective-permute-start | bytes 196616 | tf_op jit(solution)/shard_map/ppermute | solution.py:838
  11.5 0.0 collective-permute-start.3
  11.5 4.0 %shard_map.115 = (f32[6,32,40,128]{3,2,1,0:T(8,128)S(1)}, f32[3,768,128]{2,1,0:T(8,128)S(1)}, f32[32,40,128]{2,1,0:T(8,128)S(1)}, f32[2,8,128]{2,1,0:T(8,128)S(1...) custom-call(f32[6,32,40,128]{3,2,1,0:T(8,128)S(1)} %get-tuple-elemen, ...), custom_call_target="tpu_custom_call", output_to_operand_aliasing={{0}: (0, {}), {1}: (1, {}), {2}: (2, {})} | custom-call | flops 16384000 | bytes 18513920 | tf_op jit(solution)/shard_map/pallas_call | solution.py:744
  15.6 0.0 collective-permute-done.2.got_a
  15.6 0.0 collective-permute-done.3.got_b
  15.6 0.4 %shard_map.116 = (f32[2,3,24,128]{3,2,1,0:T(8,128)S(1)}, f32[40,128]{1,0:T(8,128)S(1)}, f32[3,32,128]{2,1,0:T(8,128)S(1)}, f32[3,32,128]{2,1,0:T(8,128)S(1)}, f32[32,128]{1,0:T(8,128)S(1)}) custom-call(f32[6,32,40,128]{3,2,1,0:T(8,128)S(1)} %get-tuple-element.50.waves, f32[768,128]{1,0:T(8,128)S(1)} %bitcast.18, s32[768,128]{1,0:T(8,128)S(1)} %bitcast.22, ...), custom_call_target="tpu_custom_call" | custom-call | flops 2048000 | bytes 7278592 | tf_op jit(solution)/shard_map/pallas_call | solution.py:744
  16.0 3.1 %collective-permute-start.4 = (f32[3,32,128]{2,1,0:T(8,128)S(1)}, f32[3,32,128]{2,1,0:T(8,128)S(1)}, u32[]{:S(2)}, u32[]{:S(2)}) collective-permute-start(f32[3,32,128]{2,1,0:T(8,128)S(1)} %get-tuple-element.57), channel_id=1, source_target_pairs={{0,4},{4,0},{8,12},{12,8},{16,20},{20,16},{24,28},{28,24},{1,5},{5... | collective-permute-start | bytes 147464 | tf_op jit(solution)/shard_map/ppermute | solution.py:862
  19.1 0.0 collective-permute-start.5
  19.1 11.7 %all_to_all.11 = f32[32,1,128]{2,1,0:T(1,128)S(1)} all-to-all(f32[32,1,128]{2,1,0:T(1,128)S(1)} %bitcast.24), channel_id=1, replica_groups=mesh['gx'=8,'gy'=4] {'gx','gy'}, dimensions={0} | all-to-all | bytes 32768 | tf_op jit(solution)/shard_map/all_to_all | solution.py:863
  30.8 0.0 collective-permute-done.4.got_a
  30.8 0.0 collective-permute-done.5.got_b
  30.8 1.7 %shard_map.117 = (f32[32,24,128]{2,1,0:T(8,128)}, f32[3,768,128]{2,1,0:T(8,128)}, f32[1,1]{1,0:T(1,128)}, f32[1,1]{1,0:T(1,128)}, f32[4,38,24,128]{3,2,1,0:T(8,128)S(1)}) custom-call(f32[4,38,24,128]{3,2,1,0:T(8,128)S(1)} %get-tuple-element.48.near_in, f32[32,24,128]{2,1,0:T(8,128)S(1)} %get-tuple-element.49.inner, ...), custom_call_target="tpu_custom_call", output_to_operand_aliasing={{4}: (0, {}), {1}: (7, {})} | custom-call | flops 1966080 | bytes 7090184 | tf_op jit(solution)/shard_map/pallas_call | solution.py:744
  (12 shorter events, 0.0 us)
Async XLA Ops:
  0.6 4.5 %copy-start.7 = (f32[8,128]{1,0:T(8,128)S(1)}, f32[8,128]{1,0:T(8,128)}, u32[]{:S(2)}) copy-start(f32[8,128]{1,0:T(8,128)} %constant.2.clone.sums) | copy-start | bytes 12292
  0.6 4.5 %copy-start.3 = (f32[3,1024]{1,0:T(4,128)S(1)}, f32[3,1024]{1,0:T(4,128)}, u32[]{:S(2)}) copy-start(f32[3,1024]{1,0:T(4,128)} %force.1) | copy-start | bytes 36868
  0.7 4.5 %copy-start.6 = (s32[1024]{0:T(1024)S(1)}, s32[1024]{0:T(1024)}, u32[]{:S(2)}) copy-start(s32[1024]{0:T(1024)} %param.13) | copy-start | bytes 12292
  0.7 4.5 %copy-start.5 = (s32[1024]{0:T(1024)S(1)}, s32[1024]{0:T(1024)}, u32[]{:S(2)}) copy-start(s32[1024]{0:T(1024)} %param.12) | copy-start | bytes 12292
  0.7 4.5 %copy-start.4 = (s32[1024]{0:T(1024)S(1)}, s32[1024]{0:T(1024)}, u32[]{:S(2)}) copy-start(s32[1024]{0:T(1024)} %param.11) | copy-start | bytes 12292
  2.0 7.4 %collective-permute-start = (f32[480,128]{1,0:T(8,128)S(1)}, f32[480,128]{1,0:T(8,128)S(1)}, u32[]{:S(2)}, u32[]{:S(2)}) collective-permute-start(f32[480,128]{1,0:T(8,128)S(1)} %get-tuple-element.43), channel_id=1, source_target_pairs={{0,1},{1,0},{2,3},{3,2},{4,5},{5,4},{6,7},{7,6},{8,9},{9,8},{10,11... | collective-permute-start | bytes 737288 | tf_op jit(solution)/shard_map/ppermute | solution.py:799
  2.5 6.9 %collective-permute-start.1 = (f32[480,128]{1,0:T(8,128)S(1)}, f32[480,128]{1,0:T(8,128)S(1)}, u32[]{:S(2)}, u32[]{:S(2)}) collective-permute-start(f32[480,128]{1,0:T(8,128)S(1)} %get-tuple-element.44), channel_id=1, source_target_pairs={{0,4},{1,2},{2,1},{3,7},{4,0},{5,6},{6,5},{7,3},{8,12},{9,10},{10,... | collective-permute-start | bytes 737288 | tf_op jit(solution)/shard_map/ppermute | solution.py:798
  5.2 1.6 %copy-start = (f32[3,32,24,128]{3,2,1,0:T(8,128)S(1)}, f32[3,32,24,128]{3,2,1,0:T(8,128)}, u32[]{:S(2)}) copy-start(f32[3,32,24,128]{3,2,1,0:T(8,128)} %disp.1) | copy-start | bytes 3538948
  5.2 1.6 %copy-start.1 = (f32[32,24,128]{2,1,0:T(8,128)S(1)}, f32[32,24,128]{2,1,0:T(8,128)}, u32[]{:S(2)}) copy-start(f32[32,24,128]{2,1,0:T(8,128)} %dens.1) | copy-start | bytes 1179652
  5.2 1.6 %copy-start.2 = (s32[32,24,128]{2,1,0:T(8,128)S(1)}, s32[32,24,128]{2,1,0:T(8,128)}, u32[]{:S(2)}) copy-start(s32[32,24,128]{2,1,0:T(8,128)} %kind.1) | copy-start | bytes 1179652
  9.6 6.0 %collective-permute-start.2 = (f32[4,32,128]{2,1,0:T(8,128)S(1)}, f32[4,32,128]{2,1,0:T(8,128)S(1)}, u32[]{:S(2)}, u32[]{:S(2)}) collective-permute-start(f32[4,32,128]{2,1,0:T(8,128)S(1)} %get-tuple-element.51), channel_id=1, source_target_pairs={{0,4},{4,0},{8,12},{12,8},{16,20},{20,16},{24,28},{28,24},{1,5},{5... | collective-permute-start | bytes 196616 | tf_op jit(solution)/shard_map/ppermute | solution.py:838
  11.5 4.0 %collective-permute-start.3 = (f32[4,32,128]{2,1,0:T(8,128)S(1)}, f32[4,32,128]{2,1,0:T(8,128)S(1)}, u32[]{:S(2)}, u32[]{:S(2)}) collective-permute-start(f32[4,32,128]{2,1,0:T(8,128)S(1)} %get-tuple-element.52), channel_id=1, source_target_pairs={{0,1},{1,0},{2,3},{3,2},{4,8},{5,9},{6,10},{7,11},{8,4},{9,5},{10,... | collective-permute-start | bytes 196616 | tf_op jit(solution)/shard_map/ppermute | solution.py:837
  16.0 14.8 %collective-permute-start.4 = (f32[3,32,128]{2,1,0:T(8,128)S(1)}, f32[3,32,128]{2,1,0:T(8,128)S(1)}, u32[]{:S(2)}, u32[]{:S(2)}) collective-permute-start(f32[3,32,128]{2,1,0:T(8,128)S(1)} %get-tuple-element.57), channel_id=1, source_target_pairs={{0,4},{4,0},{8,12},{12,8},{16,20},{20,16},{24,28},{28,24},{1,5},{5... | collective-permute-start | bytes 147464 | tf_op jit(solution)/shard_map/ppermute | solution.py:862
  19.1 11.7 %collective-permute-start.5 = (f32[3,32,128]{2,1,0:T(8,128)S(1)}, f32[3,32,128]{2,1,0:T(8,128)S(1)}, u32[]{:S(2)}, u32[]{:S(2)}) collective-permute-start(f32[3,32,128]{2,1,0:T(8,128)S(1)} %get-tuple-element.58), channel_id=1, source_target_pairs={{0,1},{1,0},{2,3},{3,2},{4,8},{5,9},{6,10},{7,11},{8,4},{9,5},{10,... | collective-permute-start | bytes 147464 | tf_op jit(solution)/shard_map/ppermute | solution.py:861

commit v6 on v5

--- a/solution.py
+++ b/solution.py
@@ -453,7 +453,7 @@
 def late_elements(
     rows, cols,
     waves_in, resid_in, scaled_in, tail, dens, kind, edge_u, edge_f, edge_s, applied, inverse, sums_a,
-    waves, resid, scaled, sums, resid_out, near, filtered, far_h, lines, sem,
+    waves, resid, scaled, sums, resid_out, near, filtered, far_h, lines, sems,
 ):
     depth = dens.shape[-1]
     del waves_in, resid_in, scaled_in
@@ -481,25 +481,33 @@
         for k in range(6):
             far_h[pl.ds(pl.multiple_of((k * rows + row) * HALO, 8), HALO), :] = high[k]
 
+    last = cols // 8 - 1
+    source = resid.reshape(3, rows, cols, depth)
+    copies = []
+
+    def send(block):
+        at = (slice(None), pl.ds(1, rows - 2), pl.ds(8 * block, 8), slice(None))
+        copies.append(pltpu.make_async_copy(source.at[at], resid_out.at[at], sems.at[block]))
+        copies[-1].start()
+
+    for block in range(1, last):
+        send(block)
     march(rows, cols // 8, waves, edge_state, inverse, emit_edge, put_edge, False)
-    last = cols // 8 - 1
-
-    def put(row, value):
-        scaled[row, cols:wide, :] = value
-
-    emit = joiner(cols, last, tail, None, applied, resid)
-    state = own_state(dens, kind, cols, 8 * last)
-    total, filled = march(rows, last, waves, state, inverse, emit, put, True)
-    sums[0] = sums_a[0] + total
-    sums[1] = sums_a[1] + filled
-
     parts = [far_h[pl.ds(k * rows * HALO + HALO - 1, rows, stride=HALO), :] for k in range(6)]
     at = pl.ds(0, rows, stride=cols)
     for c, value in enumerate(along_z(parts, lax.broadcasted_iota(jnp.int32, (rows, depth), 1))):
         resid[c, at, :] = resid[c, at, :] - value
-    middle = pl.ds(cols, (rows - 2) * cols)
-    copy = pltpu.make_async_copy(resid.at[:, middle, :], resid_out.at[:, middle, :], sem)
-    copy.start()
+    send(0)
+
+    def put(row, value):
+        scaled[row, cols:wide, :] = value
+
+    emit = joiner(cols, last, tail, None, applied, resid)
+    state = own_state(dens, kind, cols, 8 * last)
+    total, filled = march(rows, last, waves, state, inverse, emit, put, True)
+    send(last)
+    sums[0] = sums_a[0] + total
+    sums[1] = sums_a[1] + filled
 
     def own(row, nothing):
         lines_y(near, row + RADIUS, cols, lambda start: scaled[row, start : start + 8, :])
@@ -512,7 +520,8 @@
         picks = range(start, min(start + FILTER_ROWS, inside.stop))
         rest = filter_rows(near, lines, filtered, picks, cols, band)
         filtered[picks.start : picks.stop] = filtered[picks.start : picks.stop] + rest
-    copy.wait()
+    for copy in copies:
+        copy.wait()
 
 
 def outer_elements(
@@ -626,6 +635,34 @@
             near[shift, row, 8 * block : 8 * block + 8, :] = load(start + shift) + load(start - shift)
 
 
+def filter_row(near, row, block, lane):
+    depth = near.shape[-1]
+    at = pl.ds(block * 8, 8)
+    classes = {}
+    for shift_x in range(RADIUS + 1):
+        for shift_y in range(RADIUS + 1):
+            square = shift_x * shift_x + shift_y * shift_y
+            if square not in CLASSES:
+                continue
+            value = near[shift_y, row + (RADIUS + shift_x), at, :]
+            if shift_x:
+                value = value + near[shift_y, row + (RADIUS - shift_x), at, :]
+            classes[square] = value if square not in classes else classes[square] + value
+    result = None
+    for shift_z in range(RADIUS + 1):
+        line = None
+        for square, value in classes.items():
+            weight = weight_of(square + shift_z * shift_z)
+            if weight > 0.0:
+                line = weight * value if line is None else line + weight * value
+        if shift_z:
+            up = jnp.where(lane < shift_z, 0.0, pltpu.roll(line, shift_z, 1))
+            down = jnp.where(lane >= depth - shift_z, 0.0, pltpu.roll(line, depth - shift_z, 1))
+            line = up + down
+        result = line if result is None else result + line
+    return result
+
+
 def bands(depth):
     row = lax.broadcasted_iota(jnp.int32, (depth, depth), 0)
     column = lax.broadcasted_iota(jnp.int32, (depth, depth), 1)
@@ -672,13 +709,13 @@
 def filter_rest(
     rows, cols, count_x, cells,
     near_in, inner, final, got_a, got_b, parts, outer, resid_in,
-    sens, resid, comp, vol, near, ends, result_v, lines, sems,
+    sens, resid, comp, vol, near, ends, result_v, sems,
 ):
     depth = sens.shape[-1]
     del near_in, resid_in
     wide = cols + HALO
     copies = [
-        pltpu.make_async_copy(outer.at[index], resid.at[:, pl.ds(row * cols, cols), :], sems.at[index])
+        pltpu.make_async_copy(outer.at[index], resid.at[:, row], sems.at[index])
         for index, row in enumerate((0, rows - 1))
     ]
     for copy in copies:
@@ -727,11 +764,12 @@
         lines_y(near, index, cols, lambda start, at=index: ends[at, start : start + 8, :])
         lines_y(near, rows + RADIUS + index, cols, lambda start, at=RADIUS + index: ends[at, start : start + 8, :])
     lines_y(near, rows + RADIUS - 1, cols, lambda start: final[start : start + 8, :])
-    picks = (*range(low_end), *range(high_start, rows))
-    rest = filter_rows(near, lines, result_v, picks, cols, bands(depth))
-    for start, size, more in ((0, low_end, rest[:low_end]), (high_start, rows - high_start, rest[low_end:])):
-        result_v[start : start + size] = (result_v[start : start + size] + more) * scale[:1]
-        send(start, size)
+    lane = lax.broadcasted_iota(jnp.int32, (8, depth), 1)
+    for start, stop in ((0, low_end), (high_start, rows)):
+        for row in range(start, stop):
+            for block in range(cols // 8):
+                result_v[row, 8 * block : 8 * block + 8, :] = filter_row(near, row, block, lane) * scale
+        send(start, stop - start)
     for copy in copies:
         copy.wait()
 
@@ -840,12 +878,12 @@
     waves, inner, scaled, sums, resid, near, filtered = call(
         functools.partial(late_elements, rows, cols),
         [f32(*v.shape) for v in (waves, inner, scaled, sums)]
-        + [f32(3, rows * cols, depth), f32(RADIUS + 1, rows + 2 * RADIUS, cols, depth), f32(rows, cols, depth)],
+        + [f32(3, rows, cols, depth), f32(RADIUS + 1, rows + 2 * RADIUS, cols, depth), f32(rows, cols, depth)],
         [waves, inner, scaled, tail, dens, kind, edge_u, edge_f, edge_s, applied, inverse, sums],
         scratch=[
             vmem(6 * rows * HALO, depth),
             vmem(FILTER_ROWS * cols, RADIUS * depth),
-            pltpu.SemaphoreType.DMA,
+            pltpu.SemaphoreType.DMA((cols // HALO,)),
         ],
         out_places={4: pltpu.HBM},
         flops=250 * rows * 2 * HALO * depth,
@@ -864,12 +902,11 @@
 
     sens, resid, comp, volume, _ = call(
         functools.partial(filter_rest, rows, cols, count_x, cells),
-        [f32(rows, cols, depth), f32(3, rows * cols, depth), f32(1, 1), f32(1, 1), f32(*near.shape)],
+        [f32(rows, cols, depth), f32(3, rows, cols, depth), f32(1, 1), f32(1, 1), f32(*near.shape)],
         [near, filtered, final, got_a, got_b, parts, outer, resid],
         scratch=[
             vmem(2 * RADIUS, wide + HALO, depth),
             vmem(rows, cols, depth),
-            vmem(2 * (RADIUS + 1) * cols, RADIUS * depth),
             pltpu.SemaphoreType.DMA((5,)),
         ],
         places={7: pltpu.HBM},
@@ -879,7 +916,7 @@
     )
     return (
         sens,
-        resid.reshape(3, rows, cols, depth),
+        resid,
         comp.reshape(()),
         volume.reshape(()),
     )

time: 32.7 us -> 32.2 us (0.985)
  Pallas kernels: 11.8 us -> 10.7 us
  blocking collectives: 11.7 us -> 12.2 us
    pallas_call x7, Pallas kernels: 11.8 us -> 10.7 us  [call(): pl.pallas_call(body, out_shape=[FULL(v.shape, v.dtype) for v in shapes],...]
    all_to_all x1, blocking collectives: 11.7 us -> 12.2 us  [on_device(): parts = lax.all_to_all(parts, BOTH, 0, 0, tiled=True)]
  transfers between devices with their start and end apart: 6 -> 6, of which waited for: 0 -> 1; matrix products, arithmetic and copies ran while one was open for 0% -> 0% of each run, Pallas kernels for 25% -> 22%
where the time goes in v6:
time: 32.2 us; the launch traced here: 32 us
  blocking collectives  12.2 us (38%)
  Pallas kernels  10.7 us (33%)
  starting transfers between devices  8.05 us (25%)
  between operations  0.78 us (2%)
    all_to_all x1, blocking collectives, on_device(): parts = lax.all_to_all(parts, BOTH, 0, 0, tiled=True)  12.2 us
    pallas_call x7, Pallas kernels, call(): pl.pallas_call(body, out_shape=[FULL(v.shape, v.dtype) for v in shapes],...  10.7 us
    ppermute x2, starting transfers between devices, on_device(): got_a = lax.ppermute(send_a, 'gx', pairs_xa)  4.93 us
    ppermute x1, starting transfers between devices, on_device(): got_b = lax.ppermute(send_b, BOTH, pairs_yb)  2.59 us
  transfers between devices with their start and end apart: 6, of which 1 were waited for; matrix products, arithmetic and copies ran while one was open for 0% of the time, Pallas kernels for 22%

profile of v6, /device:TPU:0, one launch (start us, length us, event | category | flops | bytes accessed | tf_op | source)
XLA Modules:
  0.0 32.0 jit_solution(15038945132725235422)
XLA Ops:
  0.6 0.0 copy-start.7
  0.7 1.3 %shard_map.111 = (f32[480,128]{1,0:T(8,128)S(1)}, f32[480,128]{1,0:T(8,128)S(1)}, f32[8,128]{1,0:T(8,128)S(1)}) custom-call(f32[3,32,24,128]{3,2,1,0:T(8,128)} %disp.1, f32[32,24,128]{2,1,0:T(8,128)} %dens.1, s32[32,24,128]{2,1,0:T(8,128)} %kind.1), custom_call_target="tpu_custom_call" | custom-call | bytes 2461696 | tf_op jit(solution)/shard_map/pallas_call | solution.py:782
  2.0 0.5 %collective-permute-start = (f32[480,128]{1,0:T(8,128)S(1)}, f32[480,128]{1,0:T(8,128)S(1)}, u32[]{:S(2)}, u32[]{:S(2)}) collective-permute-start(f32[480,128]{1,0:T(8,128)S(1)} %get-tuple-element.43), channel_id=1, source_target_pairs={{0,1},{1,0},{2,3},{3,2},{4,5},{5,4},{6,7},{7,6},{8,9},{9,8},{10,11... | collective-permute-start | bytes 737288 | tf_op jit(solution)/shard_map/ppermute | solution.py:837
  2.5 2.6 %collective-permute-start.1 = (f32[480,128]{1,0:T(8,128)S(1)}, f32[480,128]{1,0:T(8,128)S(1)}, u32[]{:S(2)}, u32[]{:S(2)}) collective-permute-start(f32[480,128]{1,0:T(8,128)S(1)} %get-tuple-element.44), channel_id=1, source_target_pairs={{0,4},{1,2},{2,1},{3,7},{4,0},{5,6},{6,5},{7,3},{8,12},{9,10},{10,... | collective-permute-start | bytes 737288 | tf_op jit(solution)/shard_map/ppermute | solution.py:836
  5.2 0.0 copy-start
  5.2 0.0 copy-start.1
  5.2 0.0 copy-start.2
  5.2 1.5 %shard_map.112 = (f32[3,768,128]{2,1,0:T(8,128)S(1)}, f32[7,32,128]{2,1,0:T(8,128)S(1)}) custom-call(f32[8,128]{1,0:T(8,128)S(1)} %get-tuple-element.35.after, s32[1,1024]{1,0:T(1,128)S(1)} %bitcast.24, s32[1,1024]{1,0:T(1,128)S(1)} %bitcast.25, s32[1,1024]{1,0:T(1,128)S(1)} %bitcast.26, f32[3,1024]{1,0:T(4,128)S(1)} %copy-done.3, f32[8,128]{1,0:T(8,128)S(1)} %copy-done.7), custom_call_target="tpu_custom_call" | custom-call | flops 1207959552 | bytes 1327104 | tf_op jit(solution)/shard_map/pallas_call | solution.py:782
  6.8 2.6 %shard_map.113 = (f32[6,32,40,128]{3,2,1,0:T(8,128)S(1)}, f32[6,32,8,128]{3,2,1,0:T(8,128)S(1)}, f32[3,768,128]{2,1,0:T(8,128)S(1)}, f32[32,40,128]{2,1,0:T(8,128)S(1)}, f32[2,8,128]{2,1,0:T(8,128)S(1)}) custom-call(f32[2304,128]{1,0:T(8,128)S(1)} %bitcast.12, f32[768,128]{1,0:T(8,128)S(1)} %bitcast.14, s32[768,128]{1,0:T(8,128)S(1)} %bitcast.18, ...), custom_call_target="tpu_custom_call" | custom-call | flops 16384000 | bytes 9822208 | tf_op jit(solution)/shard_map/pallas_call | solution.py:782
  9.4 0.0 collective-permute-done.got_a
  9.4 0.0 collective-permute-done.1.got_b
  9.4 0.1 shard_map.114
  9.6 2.0 %collective-permute-start.2 = (f32[4,32,128]{2,1,0:T(8,128)S(1)}, f32[4,32,128]{2,1,0:T(8,128)S(1)}, u32[]{:S(2)}, u32[]{:S(2)}) collective-permute-start(f32[4,32,128]{2,1,0:T(8,128)S(1)} %get-tuple-element.51), channel_id=1, source_target_pairs={{0,4},{4,0},{8,12},{12,8},{16,20},{20,16},{24,28},{28,24},{1,5},{5... | collective-permute-start | bytes 196616 | tf_op jit(solution)/shard_map/ppermute | solution.py:876
  11.5 0.0 collective-permute-start.3
  11.5 3.0 %shard_map.115 = (f32[6,32,40,128]{3,2,1,0:T(8,128)S(1)}, f32[3,768,128]{2,1,0:T(8,128)S(1)}, f32[32,40,128]{2,1,0:T(8,128)S(1)}, f32[2,8,128]{2,1,0:T(8,128)S(1...) custom-call(f32[6,32,40,128]{3,2,1,0:T(8,128)S(1)} %get-tuple-elemen, ...), custom_call_target="tpu_custom_call", output_to_operand_aliasing={{0}: (0, {}), {1}: (1, {}), {2}: (2, {})} | custom-call | flops 16384000 | bytes 18513920 | tf_op jit(solution)/shard_map/pallas_call | solution.py:782
  14.6 0.2 collective-permute-done.2.got_a
  14.8 0.0 collective-permute-done.3.got_b
  14.8 0.4 %shard_map.116 = (f32[2,3,24,128]{3,2,1,0:T(8,128)S(1)}, f32[40,128]{1,0:T(8,128)S(1)}, f32[3,32,128]{2,1,0:T(8,128)S(1)}, f32[3,32,128]{2,1,0:T(8,128)S(1)}, f32[32,128]{1,0:T(8,128)S(1)}) custom-call(f32[6,32,40,128]{3,2,1,0:T(8,128)S(1)} %get-tuple-element.50.waves, f32[768,128]{1,0:T(8,128)S(1)} %bitcast.17, s32[768,128]{1,0:T(8,128)S(1)} %bitcast.21, ...), custom_call_target="tpu_custom_call" | custom-call | flops 2048000 | bytes 7278592 | tf_op jit(solution)/shard_map/pallas_call | solution.py:782
  15.2 3.0 %collective-permute-start.4 = (f32[3,32,128]{2,1,0:T(8,128)S(1)}, f32[3,32,128]{2,1,0:T(8,128)S(1)}, u32[]{:S(2)}, u32[]{:S(2)}) collective-permute-start(f32[3,32,128]{2,1,0:T(8,128)S(1)} %get-tuple-element.57), channel_id=1, source_target_pairs={{0,4},{4,0},{8,12},{12,8},{16,20},{20,16},{24,28},{28,24},{1,5},{5... | collective-permute-start | bytes 147464 | tf_op jit(solution)/shard_map/ppermute | solution.py:900
  18.1 0.0 collective-permute-start.5
  18.1 12.2 %all_to_all.11 = f32[32,1,128]{2,1,0:T(1,128)S(1)} all-to-all(f32[32,1,128]{2,1,0:T(1,128)S(1)} %bitcast.23), channel_id=1, replica_groups=mesh['gx'=8,'gy'=4] {'gx','gy'}, dimensions={0} | all-to-all | bytes 32768 | tf_op jit(solution)/shard_map/all_to_all | solution.py:901
  30.3 0.0 collective-permute-done.4.got_a
  30.3 0.0 collective-permute-done.5.got_b
  30.3 1.6 %shard_map.117 = (f32[32,24,128]{2,1,0:T(8,128)}, f32[3,32,24,128]{3,2,1,0:T(8,128)}, f32[1,1]{1,0:T(1,128)}, f32[1,1]{1,0:T(1,128)}, f32[4,38,24,128]{3,2,1,0:T(8,128)S(1)}) custom-call(f32[4,38,24,128]{3,2,1,0:T(8,128)S(1)} %get-tuple-element.48.near_in, f32[32,24,128]{2,1,0:T(8,128)S(1)} %get-tuple-element.49.inner, ...), custom_call_target="tpu_custom_call", output_to_operand_aliasing={{4}: (0, {}), {1}: (7, {})} | custom-call | flops 1966080 | bytes 7090184 | tf_op jit(solution)/shard_map/pallas_call | solution.py:782
  (12 shorter events, 0.0 us)
Async XLA Ops:
  0.6 4.5 %copy-start.7 = (f32[8,128]{1,0:T(8,128)S(1)}, f32[8,128]{1,0:T(8,128)}, u32[]{:S(2)}) copy-start(f32[8,128]{1,0:T(8,128)} %constant.2.clone.sums) | copy-start | bytes 12292
  0.6 4.5 %copy-start.3 = (f32[3,1024]{1,0:T(4,128)S(1)}, f32[3,1024]{1,0:T(4,128)}, u32[]{:S(2)}) copy-start(f32[3,1024]{1,0:T(4,128)} %force.1) | copy-start | bytes 36868
  0.7 4.5 %copy-start.6 = (s32[1024]{0:T(1024)S(1)}, s32[1024]{0:T(1024)}, u32[]{:S(2)}) copy-start(s32[1024]{0:T(1024)} %param.13) | copy-start | bytes 12292
  0.7 4.5 %copy-start.5 = (s32[1024]{0:T(1024)S(1)}, s32[1024]{0:T(1024)}, u32[]{:S(2)}) copy-start(s32[1024]{0:T(1024)} %param.12) | copy-start | bytes 12292
  0.7 4.5 %copy-start.4 = (s32[1024]{0:T(1024)S(1)}, s32[1024]{0:T(1024)}, u32[]{:S(2)}) copy-start(s32[1024]{0:T(1024)} %param.11) | copy-start | bytes 12292
  2.0 7.4 %collective-permute-start = (f32[480,128]{1,0:T(8,128)S(1)}, f32[480,128]{1,0:T(8,128)S(1)}, u32[]{:S(2)}, u32[]{:S(2)}) collective-permute-start(f32[480,128]{1,0:T(8,128)S(1)} %get-tuple-element.43), channel_id=1, source_target_pairs={{0,1},{1,0},{2,3},{3,2},{4,5},{5,4},{6,7},{7,6},{8,9},{9,8},{10,11... | collective-permute-start | bytes 737288 | tf_op jit(solution)/shard_map/ppermute | solution.py:837
  2.5 6.9 %collective-permute-start.1 = (f32[480,128]{1,0:T(8,128)S(1)}, f32[480,128]{1,0:T(8,128)S(1)}, u32[]{:S(2)}, u32[]{:S(2)}) collective-permute-start(f32[480,128]{1,0:T(8,128)S(1)} %get-tuple-element.44), channel_id=1, source_target_pairs={{0,4},{1,2},{2,1},{3,7},{4,0},{5,6},{6,5},{7,3},{8,12},{9,10},{10,... | collective-permute-start | bytes 737288 | tf_op jit(solution)/shard_map/ppermute | solution.py:836
  5.2 1.6 %copy-start = (f32[3,32,24,128]{3,2,1,0:T(8,128)S(1)}, f32[3,32,24,128]{3,2,1,0:T(8,128)}, u32[]{:S(2)}) copy-start(f32[3,32,24,128]{3,2,1,0:T(8,128)} %disp.1) | copy-start | bytes 3538948
  5.2 1.6 %copy-start.1 = (f32[32,24,128]{2,1,0:T(8,128)S(1)}, f32[32,24,128]{2,1,0:T(8,128)}, u32[]{:S(2)}) copy-start(f32[32,24,128]{2,1,0:T(8,128)} %dens.1) | copy-start | bytes 1179652
  5.2 1.6 %copy-start.2 = (s32[32,24,128]{2,1,0:T(8,128)S(1)}, s32[32,24,128]{2,1,0:T(8,128)}, u32[]{:S(2)}) copy-start(s32[32,24,128]{2,1,0:T(8,128)} %kind.1) | copy-start | bytes 1179652
  9.6 5.2 %collective-permute-start.2 = (f32[4,32,128]{2,1,0:T(8,128)S(1)}, f32[4,32,128]{2,1,0:T(8,128)S(1)}, u32[]{:S(2)}, u32[]{:S(2)}) collective-permute-start(f32[4,32,128]{2,1,0:T(8,128)S(1)} %get-tuple-element.51), channel_id=1, source_target_pairs={{0,4},{4,0},{8,12},{12,8},{16,20},{20,16},{24,28},{28,24},{1,5},{5... | collective-permute-start | bytes 196616 | tf_op jit(solution)/shard_map/ppermute | solution.py:876
  11.5 3.2 %collective-permute-start.3 = (f32[4,32,128]{2,1,0:T(8,128)S(1)}, f32[4,32,128]{2,1,0:T(8,128)S(1)}, u32[]{:S(2)}, u32[]{:S(2)}) collective-permute-start(f32[4,32,128]{2,1,0:T(8,128)S(1)} %get-tuple-element.52), channel_id=1, source_target_pairs={{0,1},{1,0},{2,3},{3,2},{4,8},{5,9},{6,10},{7,11},{8,4},{9,5},{10,... | collective-permute-start | bytes 196616 | tf_op jit(solution)/shard_map/ppermute | solution.py:875
  15.2 15.2 %collective-permute-start.4 = (f32[3,32,128]{2,1,0:T(8,128)S(1)}, f32[3,32,128]{2,1,0:T(8,128)S(1)}, u32[]{:S(2)}, u32[]{:S(2)}) collective-permute-start(f32[3,32,128]{2,1,0:T(8,128)S(1)} %get-tuple-element.57), channel_id=1, source_target_pairs={{0,4},{4,0},{8,12},{12,8},{16,20},{20,16},{24,28},{28,24},{1,5},{5... | collective-permute-start | bytes 147464 | tf_op jit(solution)/shard_map/ppermute | solution.py:900
  18.1 12.2 %collective-permute-start.5 = (f32[3,32,128]{2,1,0:T(8,128)S(1)}, f32[3,32,128]{2,1,0:T(8,128)S(1)}, u32[]{:S(2)}, u32[]{:S(2)}) collective-permute-start(f32[3,32,128]{2,1,0:T(8,128)S(1)} %get-tuple-element.58), channel_id=1, source_target_pairs={{0,1},{1,0},{2,3},{3,2},{4,8},{5,9},{6,10},{7,11},{8,4},{9,5},{10,... | collective-permute-start | bytes 147464 | tf_op jit(solution)/shard_map/ppermute | solution.py:899

commit v7 on v6

--- a/solution.py
+++ b/solution.py
@@ -453,7 +453,7 @@
 def late_elements(
     rows, cols,
     waves_in, resid_in, scaled_in, tail, dens, kind, edge_u, edge_f, edge_s, applied, inverse, sums_a,
-    waves, resid, scaled, sums, resid_out, near, filtered, far_h, lines, sems,
+    waves, resid, scaled, sums, resid_out, near, filtered, out_a, out_b, far_h, lines, sems,
 ):
     depth = dens.shape[-1]
     del waves_in, resid_in, scaled_in
@@ -508,6 +508,26 @@
     send(last)
     sums[0] = sums_a[0] + total
     sums[1] = sums_a[1] + filled
+
+    def out(up, down):
+        for index in range(RADIUS - 1):
+            up[index] = scaled[rows - RADIUS + index, :wide, :]
+        at = pl.ds((rows - 1) * cols, cols)
+        code = kind[at, :]
+        up[RADIUS - 1, HALO:, :] = factor_of(physical_of(dens[at, :], code), code)
+        up[RADIUS - 1, :HALO, :] = edge_f[pl.ds((rows - 1) * HALO, HALO), :]
+        for index in range(RADIUS):
+            down[index] = scaled[index, :wide, :]
+
+    odd = lax.axis_index("gx") % 2
+
+    @pl.when(odd == 0)
+    def _():
+        out(out_a, out_b)
+
+    @pl.when(odd == 1)
+    def _():
+        out(out_b, out_a)
 
     def own(row, nothing):
         lines_y(near, row + RADIUS, cols, lambda start: scaled[row, start : start + 8, :])
@@ -526,8 +546,8 @@
 
 def outer_elements(
     rows, cols, count_x, devices,
-    waves, dens, kind, edge_f, edge_s, got_a, got_b, inner, scaled, sums, inverse,
-    resid, final, out_a, out_b, parts, ring, stiff_low, carry_y,
+    waves, dens, kind, edge_f, edge_s, got_a, got_b, inner, sums, inverse,
+    resid, final, before, parts, ring, stiff_low, carry_y,
 ):
     depth = dens.shape[-1]
     constants = modal_constants()
@@ -576,7 +596,9 @@
             nodes(lambda k: waves.at[k, rows - 1]),
             nodes(lambda k: ring.at[1, k]),
         ]
-        _, f_low = modal(line[0], line[1], stiff_low[first : first + 8, :], constants)
+        energy, f_low = modal(line[0], line[1], stiff_low[first : first + 8, :], constants)
+        place = first + 8 if own else 0
+        before[place : place + 8, :] = energy * inverse[RADIUS, first : first + 8, :]
         if own:
             _, stiff, factor = own_state(dens, kind, cols, first)(rows - 1)
         else:
@@ -610,21 +632,6 @@
         pieces.append(line + pltpu.roll(line, half, 1))
     line = jnp.where(lax.broadcasted_iota(jnp.int32, (1, depth), 1) < half, pieces[0], pieces[1])
     parts[...] = jnp.broadcast_to(line, (devices, depth))
-
-    def send(up, down):
-        for index in range(RADIUS - 1):
-            up[index] = scaled[rows - RADIUS + index, :wide, :]
-        up[RADIUS - 1] = final[:wide, :]
-        for index in range(RADIUS):
-            down[index] = scaled[index, :wide, :]
-
-    @pl.when(odd == 0)
-    def _():
-        send(out_a, out_b)
-
-    @pl.when(odd == 1)
-    def _():
-        send(out_b, out_a)
 
 
 def lines_y(near, row, cols, load):
@@ -708,7 +715,7 @@
 
 def filter_rest(
     rows, cols, count_x, cells,
-    near_in, inner, final, got_a, got_b, parts, outer, resid_in,
+    near_in, inner, final, before, got_a, got_b, parts, outer, resid_in,
     sens, resid, comp, vol, near, ends, result_v, sems,
 ):
     depth = sens.shape[-1]
@@ -748,7 +755,10 @@
     def take(low, high):
         for index in range(RADIUS):
             for source, has, at in ((low, has_low, index), (high, has_high, RADIUS + index)):
-                value = jnp.where(has, source[index], 0.0)
+                value = source[index]
+                if source is low and index == RADIUS - 1:
+                    value = value * before[...]
+                value = jnp.where(has, value, 0.0)
                 ends[at, :wide, :] = value
                 ends[at, wide:, :] = value[:HALO]
 
@@ -875,10 +885,11 @@
     got_b = lax.ppermute(send_b, BOTH, pairs_xb)
     got_a = lax.ppermute(send_a, "gx", pairs_xa)
 
-    waves, inner, scaled, sums, resid, near, filtered = call(
+    waves, inner, scaled, sums, resid, near, filtered, send_a, send_b = call(
         functools.partial(late_elements, rows, cols),
         [f32(*v.shape) for v in (waves, inner, scaled, sums)]
-        + [f32(3, rows, cols, depth), f32(RADIUS + 1, rows + 2 * RADIUS, cols, depth), f32(rows, cols, depth)],
+        + [f32(3, rows, cols, depth), f32(RADIUS + 1, rows + 2 * RADIUS, cols, depth), f32(rows, cols, depth)]
+        + [f32(RADIUS, wide, depth)] * 2,
         [waves, inner, scaled, tail, dens, kind, edge_u, edge_f, edge_s, applied, inverse, sums],
         scratch=[
             vmem(6 * rows * HALO, depth),
@@ -889,30 +900,30 @@
         flops=250 * rows * 2 * HALO * depth,
         aliases={0: 0, 1: 1, 2: 2},
     )
-    outer, final, send_a, send_b, parts = call(
+    more_b = lax.ppermute(send_b, BOTH, pairs_xb)
+    more_a = lax.ppermute(send_a, "gx", pairs_xa)
+    outer, final, before, parts = call(
         functools.partial(outer_elements, rows, cols, count_x, devices),
-        [f32(2, 3, cols, depth), f32(wide + HALO, depth)] + [f32(RADIUS, wide, depth)] * 2 + [f32(devices, depth)],
-        [waves, dens, kind, edge_f, edge_s, got_a, got_b, inner, scaled, sums, inverse],
+        [f32(2, 3, cols, depth), f32(wide + HALO, depth), f32(wide, depth), f32(devices, depth)],
+        [waves, dens, kind, edge_f, edge_s, got_a, got_b, inner, sums, inverse],
         scratch=[vmem(2, 6, wide + HALO, depth), vmem(wide, depth), vmem(2, 6, wide + 2 * HALO, depth)],
         flops=500 * wide * depth,
     )
-    got_b = lax.ppermute(send_b, BOTH, pairs_xb)
-    got_a = lax.ppermute(send_a, "gx", pairs_xa)
     parts = lax.all_to_all(parts, BOTH, 0, 0, tiled=True)
 
     sens, resid, comp, volume, _ = call(
         functools.partial(filter_rest, rows, cols, count_x, cells),
         [f32(rows, cols, depth), f32(3, rows, cols, depth), f32(1, 1), f32(1, 1), f32(*near.shape)],
-        [near, filtered, final, got_a, got_b, parts, outer, resid],
+        [near, filtered, final, before, more_a, more_b, parts, outer, resid],
         scratch=[
             vmem(2 * RADIUS, wide + HALO, depth),
             vmem(rows, cols, depth),
             pltpu.SemaphoreType.DMA((5,)),
         ],
-        places={7: pltpu.HBM},
+        places={8: pltpu.HBM},
         out_places={0: pltpu.HBM, 1: pltpu.HBM, 2: pltpu.SMEM, 3: pltpu.SMEM},
         flops=20 * rows * cols * depth,
-        aliases={0: 4, 7: 1},
+        aliases={0: 4, 8: 1},
     )
     return (
         sens,

time: 32.2 us -> 32.4 us (level)
  blocking collectives: 12.2 us -> 0 us
  waiting for transfers between devices: 0.21 us -> 7.07 us
  starting transfers between devices: 8.05 us -> 13 us
  Pallas kernels: 10.7 us -> 11.3 us
    all_to_all x1 -> x0, blocking collectives: 12.2 us -> none  [on_device(): parts = lax.all_to_all(parts, BOTH, 0, 0, tiled=True)]
    all_to_all x0 -> x1, waiting for transfers between devices: none -> 7.05 us  [on_device(): parts = lax.all_to_all(parts, BOTH, 0, 0, tiled=True)]
    all_to_all x0 -> x1, starting transfers between devices: none -> 4.76 us  [on_device(): parts = lax.all_to_all(parts, BOTH, 0, 0, tiled=True)]
    ppermute x0 -> x2, starting transfers between devices: none -> 3.1 us  [the longest x1 3.1 us: on_device(): more_a = lax.ppermute(send_a, 'gx', pairs_xa)]
    ppermute x2 -> x1, starting transfers between devices: 4.93 us -> 1.98 us  [on_device(): got_a = lax.ppermute(send_a, 'gx', pairs_xa)]
    pallas_call x7, Pallas kernels: 10.7 us -> 11.3 us  [call(): pl.pallas_call(body, out_shape=[FULL(v.shape, v.dtype) for v in shapes],...]
  transfers between devices with their start and end apart: 6 -> 7, of which waited for: 1 -> 1; matrix products, arithmetic and copies ran while one was open for 0% -> 0% of each run, Pallas kernels for 22% -> 25%
where the time goes in v7:
time: 32.4 us; the launch traced here: 32.2 us
  starting transfers between devices  13 us (40%)
  Pallas kernels  11.3 us (35%)
  waiting for transfers between devices  7.07 us (22%)
  between operations  0.81 us (2%)
    pallas_call x7, Pallas kernels, call(): pl.pallas_call(body, out_shape=[FULL(v.shape, v.dtype) for v in shapes],...  11.3 us
    all_to_all x1, waiting for transfers between devices, on_device(): parts = lax.all_to_all(parts, BOTH, 0, 0, tiled=True)  7.05 us
    all_to_all x1, starting transfers between devices, on_device(): parts = lax.all_to_all(parts, BOTH, 0, 0, tiled=True)  4.76 us
    ppermute x1, starting transfers between devices, on_device(): more_a = lax.ppermute(send_a, 'gx', pairs_xa)  3.1 us
    ppermute x1, starting transfers between devices, on_device(): got_b = lax.ppermute(send_b, BOTH, pairs_yb)  2.59 us
    ppermute x1, starting transfers between devices, on_device(): got_a = lax.ppermute(send_a, 'gx', pairs_xa)  1.98 us
  transfers between devices with their start and end apart: 7, of which 1 were waited for; matrix products, arithmetic and copies ran while one was open for 0% of the time, Pallas kernels for 25%

profile of v7, /device:TPU:0, one launch (start us, length us, event | category | flops | bytes accessed | tf_op | source)
XLA Modules:
  0.0 32.2 jit_solution(15313516428297951757)
XLA Ops:
  0.6 0.0 copy-start.7
  0.7 1.3 %shard_map.111 = (f32[480,128]{1,0:T(8,128)S(1)}, f32[480,128]{1,0:T(8,128)S(1)}, f32[8,128]{1,0:T(8,128)S(1)}) custom-call(f32[3,32,24,128]{3,2,1,0:T(8,128)} %disp.1, f32[32,24,128]{2,1,0:T(8,128)} %dens.1, s32[32,24,128]{2,1,0:T(8,128)} %kind.1), custom_call_target="tpu_custom_call" | custom-call | bytes 2461696 | tf_op jit(solution)/shard_map/pallas_call | solution.py:792
  2.0 0.5 %collective-permute-start = (f32[480,128]{1,0:T(8,128)S(1)}, f32[480,128]{1,0:T(8,128)S(1)}, u32[]{:S(2)}, u32[]{:S(2)}) collective-permute-start(f32[480,128]{1,0:T(8,128)S(1)} %get-tuple-element.43), channel_id=1, source_target_pairs={{0,1},{1,0},{2,3},{3,2},{4,5},{5,4},{6,7},{7,6},{8,9},{9,8},{10,11... | collective-permute-start | bytes 737288 | tf_op jit(solution)/shard_map/ppermute | solution.py:847
  2.5 2.6 %collective-permute-start.1 = (f32[480,128]{1,0:T(8,128)S(1)}, f32[480,128]{1,0:T(8,128)S(1)}, u32[]{:S(2)}, u32[]{:S(2)}) collective-permute-start(f32[480,128]{1,0:T(8,128)S(1)} %get-tuple-element.44), channel_id=1, source_target_pairs={{0,4},{1,2},{2,1},{3,7},{4,0},{5,6},{6,5},{7,3},{8,12},{9,10},{10,... | collective-permute-start | bytes 737288 | tf_op jit(solution)/shard_map/ppermute | solution.py:846
  5.2 0.0 copy-start
  5.2 0.0 copy-start.1
  5.2 0.0 copy-start.2
  5.2 1.5 %shard_map.112 = (f32[3,768,128]{2,1,0:T(8,128)S(1)}, f32[7,32,128]{2,1,0:T(8,128)S(1)}) custom-call(f32[8,128]{1,0:T(8,128)S(1)} %get-tuple-element.35.after, s32[1,1024]{1,0:T(1,128)S(1)} %bitcast.23, s32[1,1024]{1,0:T(1,128)S(1)} %bitcast.24, s32[1,1024]{1,0:T(1,128)S(1)} %bitcast.25, f32[3,1024]{1,0:T(4,128)S(1)} %copy-done.3, f32[8,128]{1,0:T(8,128)S(1)} %copy-done.7), custom_call_target="tpu_custom_call" | custom-call | flops 1207959552 | bytes 1327104 | tf_op jit(solution)/shard_map/pallas_call | solution.py:792
  6.8 2.6 %shard_map.113 = (f32[6,32,40,128]{3,2,1,0:T(8,128)S(1)}, f32[6,32,8,128]{3,2,1,0:T(8,128)S(1)}, f32[3,768,128]{2,1,0:T(8,128)S(1)}, f32[32,40,128]{2,1,0:T(8,128)S(1)}, f32[2,8,128]{2,1,0:T(8,128)S(1)}) custom-call(f32[2304,128]{1,0:T(8,128)S(1)} %bitcast.12, f32[768,128]{1,0:T(8,128)S(1)} %bitcast.14, s32[768,128]{1,0:T(8,128)S(1)} %bitcast.18, ...), custom_call_target="tpu_custom_call" | custom-call | flops 16384000 | bytes 9822208 | tf_op jit(solution)/shard_map/pallas_call | solution.py:792
  9.4 0.0 collective-permute-done.got_a
  9.4 0.0 collective-permute-done.1.got_b
  9.4 0.1 shard_map.114
  9.6 2.0 %collective-permute-start.2 = (f32[4,32,128]{2,1,0:T(8,128)S(1)}, f32[4,32,128]{2,1,0:T(8,128)S(1)}, u32[]{:S(2)}, u32[]{:S(2)}) collective-permute-start(f32[4,32,128]{2,1,0:T(8,128)S(1)} %get-tuple-element.51), channel_id=1, source_target_pairs={{0,4},{4,0},{8,12},{12,8},{16,20},{20,16},{24,28},{28,24},{1,5},{5... | collective-permute-start | bytes 196616 | tf_op jit(solution)/shard_map/ppermute | solution.py:886
  11.5 0.0 collective-permute-start.3
  11.5 3.0 %shard_map.115 = (f32[6,32,40,128]{3,2,1,0:T(8,128)S(1)}, f32[3,768,128]{2,1,0:T(8,128)S(1)}, f32[32,40,128]{2,1,0:T(8,128)S(1)}, f32[2,8,128]{2,1,0:T(8,128)S(1...) custom-call(f32[6,32,40,128]{3,2,1,0:T(8,128)S(1)} %get-tuple-elemen, ...), custom_call_target="tpu_custom_call", output_to_operand_aliasing={{0}: (0, {}), {1}: (1, {}), {2}: (2, {})} | custom-call | flops 16384000 | bytes 18612224 | tf_op jit(solution)/shard_map/pallas_call | solution.py:792
  14.6 3.1 %collective-permute-start.4 = (f32[3,32,128]{2,1,0:T(8,128)S(1)}, f32[3,32,128]{2,1,0:T(8,128)S(1)}, u32[]{:S(2)}, u32[]{:S(2)}) collective-permute-start(f32[3,32,128]{2,1,0:T(8,128)S(1)} %get-tuple-element.57), channel_id=1, source_target_pairs={{0,4},{4,0},{8,12},{12,8},{16,20},{20,16},{24,28},{28,24},{1,5},{5... | collective-permute-start | bytes 147464 | tf_op jit(solution)/shard_map/ppermute | solution.py:904
  17.7 0.0 collective-permute-start.5
  17.7 0.0 collective-permute-done.2.got_a
  17.7 0.0 collective-permute-done.3.got_b
  17.7 1.0 %shard_map.116 = (f32[2,3,24,128]{3,2,1,0:T(8,128)S(1)}, f32[40,128]{1,0:T(8,128)S(1)}, f32[32,128]{1,0:T(8,128)S(1)}, f32[32,128]{1,0:T(8,128)}) custom-call(f32[6,32,40,128]{3,2,1,0:T(8,128)S(1)} %get-tuple-element.50.waves, f32[768,128]{1,0:T(8,128)S(1)} %bitcast.17, s32[768,128]{1,0:T(8,128)S(1)} %bitcast.21, f32[256,128]{1,0:T(8,128)S(1)} %get-tuple-element.46.edge_f, ...), custom_call_target="tpu_custom_call" | custom-call | flops 2048000 | bytes 6541312 | tf_op jit(solution)/shard_map/pallas_call | solution.py:792
  18.7 4.8 %all-to-all-start = ((f32[32,1,128]{2,1,0:T(1,128)}), f32[32,1,128]{2,1,0:T(1,128)S(1)}, u32[]{:S(2)}, u32[]{:S(2)}) async-start(f32[32,1,128]{2,1,0:T(1,128)} %bitcast.7), calls=%async_computation | async-start | bytes 32768 | tf_op jit(solution)/shard_map/all_to_all | solution.py:912
  23.5 0.0 collective-permute-done.5.got_b
  23.5 7.1 %all-to-all-done = f32[32,1,128]{2,1,0:T(1,128)S(1)} async-done(((f32[32,1,128]{2,1,0:T(1,128)}), f32[32,1,128]{2,1,0:T(1,128)S(1)}, u32[]{:S(2)}, u32[]{:S(2)}) %all-to-all-start) | async-done | bytes 16416 | tf_op jit(solution)/shard_map/all_to_all | solution.py:912
  30.6 1.6 %shard_map.117 = (f32[32,24,128]{2,1,0:T(8,128)}, f32[3,32,24,128]{3,2,1,0:T(8,128)}, f32[1,1]{1,0:T(1,128)}, f32[1,1]{1,0:T(1,128)}, f32[4,38,24,128]{3,2,1,0:T(8,128)S(1)}) custom-call(f32[4,38,24,128]{3,2,1,0:T(8,128)S(1)} %get-tuple-element.48.near_in, f32[32,24,128]{2,1,0:T(8,128)S(1)} %get-tuple-element.49.inner, ...), custom_call_target="tpu_custom_call", output_to_operand_aliasing={{4}: (0, {}), {1}: (8, {})} | custom-call | flops 1966080 | bytes 7106568 | tf_op jit(solution)/shard_map/pallas_call | solution.py:792
  (13 shorter events, 0.0 us)
Async XLA Ops:
  0.6 4.5 %copy-start.7 = (f32[8,128]{1,0:T(8,128)S(1)}, f32[8,128]{1,0:T(8,128)}, u32[]{:S(2)}) copy-start(f32[8,128]{1,0:T(8,128)} %constant.2.clone.sums) | copy-start | bytes 12292
  0.6 4.5 %copy-start.3 = (f32[3,1024]{1,0:T(4,128)S(1)}, f32[3,1024]{1,0:T(4,128)}, u32[]{:S(2)}) copy-start(f32[3,1024]{1,0:T(4,128)} %force.1) | copy-start | bytes 36868
  0.7 4.5 %copy-start.6 = (s32[1024]{0:T(1024)S(1)}, s32[1024]{0:T(1024)}, u32[]{:S(2)}) copy-start(s32[1024]{0:T(1024)} %param.13) | copy-start | bytes 12292
  0.7 4.5 %copy-start.5 = (s32[1024]{0:T(1024)S(1)}, s32[1024]{0:T(1024)}, u32[]{:S(2)}) copy-start(s32[1024]{0:T(1024)} %param.12) | copy-start | bytes 12292
  0.7 4.5 %copy-start.4 = (s32[1024]{0:T(1024)S(1)}, s32[1024]{0:T(1024)}, u32[]{:S(2)}) copy-start(s32[1024]{0:T(1024)} %param.11) | copy-start | bytes 12292
  2.0 7.4 %collective-permute-start = (f32[480,128]{1,0:T(8,128)S(1)}, f32[480,128]{1,0:T(8,128)S(1)}, u32[]{:S(2)}, u32[]{:S(2)}) collective-permute-start(f32[480,128]{1,0:T(8,128)S(1)} %get-tuple-element.43), channel_id=1, source_target_pairs={{0,1},{1,0},{2,3},{3,2},{4,5},{5,4},{6,7},{7,6},{8,9},{9,8},{10,11... | collective-permute-start | bytes 737288 | tf_op jit(solution)/shard_map/ppermute | solution.py:847
  2.5 6.9 %collective-permute-start.1 = (f32[480,128]{1,0:T(8,128)S(1)}, f32[480,128]{1,0:T(8,128)S(1)}, u32[]{:S(2)}, u32[]{:S(2)}) collective-permute-start(f32[480,128]{1,0:T(8,128)S(1)} %get-tuple-element.44), channel_id=1, source_target_pairs={{0,4},{1,2},{2,1},{3,7},{4,0},{5,6},{6,5},{7,3},{8,12},{9,10},{10,... | collective-permute-start | bytes 737288 | tf_op jit(solution)/shard_map/ppermute | solution.py:846
  5.2 1.6 %copy-start = (f32[3,32,24,128]{3,2,1,0:T(8,128)S(1)}, f32[3,32,24,128]{3,2,1,0:T(8,128)}, u32[]{:S(2)}) copy-start(f32[3,32,24,128]{3,2,1,0:T(8,128)} %disp.1) | copy-start | bytes 3538948
  5.2 1.6 %copy-start.1 = (f32[32,24,128]{2,1,0:T(8,128)S(1)}, f32[32,24,128]{2,1,0:T(8,128)}, u32[]{:S(2)}) copy-start(f32[32,24,128]{2,1,0:T(8,128)} %dens.1) | copy-start | bytes 1179652
  5.2 1.6 %copy-start.2 = (s32[32,24,128]{2,1,0:T(8,128)S(1)}, s32[32,24,128]{2,1,0:T(8,128)}, u32[]{:S(2)}) copy-start(s32[32,24,128]{2,1,0:T(8,128)} %kind.1) | copy-start | bytes 1179652
  9.6 8.1 %collective-permute-start.2 = (f32[4,32,128]{2,1,0:T(8,128)S(1)}, f32[4,32,128]{2,1,0:T(8,128)S(1)}, u32[]{:S(2)}, u32[]{:S(2)}) collective-permute-start(f32[4,32,128]{2,1,0:T(8,128)S(1)} %get-tuple-element.51), channel_id=1, source_target_pairs={{0,4},{4,0},{8,12},{12,8},{16,20},{20,16},{24,28},{28,24},{1,5},{5... | collective-permute-start | bytes 196616 | tf_op jit(solution)/shard_map/ppermute | solution.py:886
  11.5 6.1 %collective-permute-start.3 = (f32[4,32,128]{2,1,0:T(8,128)S(1)}, f32[4,32,128]{2,1,0:T(8,128)S(1)}, u32[]{:S(2)}, u32[]{:S(2)}) collective-permute-start(f32[4,32,128]{2,1,0:T(8,128)S(1)} %get-tuple-element.52), channel_id=1, source_target_pairs={{0,1},{1,0},{2,3},{3,2},{4,8},{5,9},{6,10},{7,11},{8,4},{9,5},{10,... | collective-permute-start | bytes 196616 | tf_op jit(solution)/shard_map/ppermute | solution.py:885
  14.6 8.9 %collective-permute-start.4 = (f32[3,32,128]{2,1,0:T(8,128)S(1)}, f32[3,32,128]{2,1,0:T(8,128)S(1)}, u32[]{:S(2)}, u32[]{:S(2)}) collective-permute-start(f32[3,32,128]{2,1,0:T(8,128)S(1)} %get-tuple-element.57), channel_id=1, source_target_pairs={{0,4},{4,0},{8,12},{12,8},{16,20},{20,16},{24,28},{28,24},{1,5},{5... | collective-permute-start | bytes 147464 | tf_op jit(solution)/shard_map/ppermute | solution.py:904
  17.7 5.8 %collective-permute-start.5 = (f32[3,32,128]{2,1,0:T(8,128)S(1)}, f32[3,32,128]{2,1,0:T(8,128)S(1)}, u32[]{:S(2)}, u32[]{:S(2)}) collective-permute-start(f32[3,32,128]{2,1,0:T(8,128)S(1)} %get-tuple-element.58), channel_id=1, source_target_pairs={{0,1},{1,0},{2,3},{3,2},{4,8},{5,9},{6,10},{7,11},{8,4},{9,5},{10,... | collective-permute-start | bytes 147464 | tf_op jit(solution)/shard_map/ppermute | solution.py:903
  18.7 11.8 %all-to-all-start = ((f32[32,1,128]{2,1,0:T(1,128)}), f32[32,1,128]{2,1,0:T(1,128)S(1)}, u32[]{:S(2)}, u32[]{:S(2)}) async-start(f32[32,1,128]{2,1,0:T(1,128)} %bitcast.7), calls=%async_computation | async-start | bytes 32768 | tf_op jit(solution)/shard_map/all_to_all | solution.py:912

commit v8 on v7

--- a/solution.py
+++ b/solution.py
@@ -453,7 +453,7 @@
 def late_elements(
     rows, cols,
     waves_in, resid_in, scaled_in, tail, dens, kind, edge_u, edge_f, edge_s, applied, inverse, sums_a,
-    waves, resid, scaled, sums, resid_out, near, filtered, out_a, out_b, far_h, lines, sems,
+    waves, resid, scaled, sums, resid_out, out_a, out_b, far_h, sems,
 ):
     depth = dens.shape[-1]
     del waves_in, resid_in, scaled_in
@@ -528,18 +528,6 @@
     @pl.when(odd == 1)
     def _():
         out(out_b, out_a)
-
-    def own(row, nothing):
-        lines_y(near, row + RADIUS, cols, lambda start: scaled[row, start : start + 8, :])
-        return nothing
-
-    lax.fori_loop(0, rows - 1, own, 0, unroll=True)
-    band = bands(depth)
-    inside = range(RADIUS + 1, rows - RADIUS - 1)
-    for start in inside[:: FILTER_ROWS]:
-        picks = range(start, min(start + FILTER_ROWS, inside.stop))
-        rest = filter_rows(near, lines, filtered, picks, cols, band)
-        filtered[picks.start : picks.stop] = filtered[picks.start : picks.stop] + rest
     for copy in copies:
         copy.wait()
 
@@ -642,34 +630,6 @@
             near[shift, row, 8 * block : 8 * block + 8, :] = load(start + shift) + load(start - shift)
 
 
-def filter_row(near, row, block, lane):
-    depth = near.shape[-1]
-    at = pl.ds(block * 8, 8)
-    classes = {}
-    for shift_x in range(RADIUS + 1):
-        for shift_y in range(RADIUS + 1):
-            square = shift_x * shift_x + shift_y * shift_y
-            if square not in CLASSES:
-                continue
-            value = near[shift_y, row + (RADIUS + shift_x), at, :]
-            if shift_x:
-                value = value + near[shift_y, row + (RADIUS - shift_x), at, :]
-            classes[square] = value if square not in classes else classes[square] + value
-    result = None
-    for shift_z in range(RADIUS + 1):
-        line = None
-        for square, value in classes.items():
-            weight = weight_of(square + shift_z * shift_z)
-            if weight > 0.0:
-                line = weight * value if line is None else line + weight * value
-        if shift_z:
-            up = jnp.where(lane < shift_z, 0.0, pltpu.roll(line, shift_z, 1))
-            down = jnp.where(lane >= depth - shift_z, 0.0, pltpu.roll(line, depth - shift_z, 1))
-            line = up + down
-        result = line if result is None else result + line
-    return result
-
-
 def bands(depth):
     row = lax.broadcasted_iota(jnp.int32, (depth, depth), 0)
     column = lax.broadcasted_iota(jnp.int32, (depth, depth), 1)
@@ -713,44 +673,13 @@
     return total.reshape(len(picks), cols, depth)
 
 
-def filter_rest(
-    rows, cols, count_x, cells,
-    near_in, inner, final, before, got_a, got_b, parts, outer, resid_in,
-    sens, resid, comp, vol, near, ends, result_v, sems,
-):
-    depth = sens.shape[-1]
-    del near_in, resid_in
+def filter_all(rows, cols, count_x, scaled, final, before, got_a, got_b, result, near, ends, lines):
+    depth = result.shape[-1]
     wide = cols + HALO
-    copies = [
-        pltpu.make_async_copy(outer.at[index], resid.at[:, row], sems.at[index])
-        for index, row in enumerate((0, rows - 1))
-    ]
-    for copy in copies:
-        copy.start()
     here = lax.axis_index("gx")
     has_low = here > 0
     has_high = here < count_x - 1
     odd = here % 2
-    half = depth // 2
-    line = jnp.sum(parts[...], axis=0, keepdims=True)
-    first = lax.broadcasted_iota(jnp.int32, (1, depth), 1) < half
-    compliance = jnp.sum(jnp.where(first, line, 0.0))
-    volume = jnp.sum(jnp.where(first, 0.0, line))
-    comp[0, 0] = compliance
-    vol[0, 0] = volume / cells
-    scale = cells / jnp.broadcast_to(compliance, (8, depth))
-
-    def send(start, size):
-        at = pl.ds(start, size)
-        copies.append(pltpu.make_async_copy(result_v.at[at], sens.at[at], sems.at[len(copies)]))
-        copies[-1].start()
-
-    low_end, high_start = RADIUS + 1, rows - RADIUS - 1
-    for row in range(low_end, high_start):
-        for block in range(cols // 8):
-            at = pl.ds(block * 8, 8)
-            result_v[row, at, :] = inner[row, at, :] * scale
-    send(low_end, high_start - low_end)
 
     def take(low, high):
         for index in range(RADIUS):
@@ -774,12 +703,41 @@
         lines_y(near, index, cols, lambda start, at=index: ends[at, start : start + 8, :])
         lines_y(near, rows + RADIUS + index, cols, lambda start, at=RADIUS + index: ends[at, start : start + 8, :])
     lines_y(near, rows + RADIUS - 1, cols, lambda start: final[start : start + 8, :])
-    lane = lax.broadcasted_iota(jnp.int32, (8, depth), 1)
-    for start, stop in ((0, low_end), (high_start, rows)):
-        for row in range(start, stop):
+    for row in range(rows - 1):
+        lines_y(near, row + RADIUS, cols, lambda start, row=row: scaled[row, start : start + 8, :])
+    band = bands(depth)
+    for start in range(0, rows, FILTER_ROWS):
+        picks = range(start, min(start + FILTER_ROWS, rows))
+        rest = filter_rows(near, lines, result, picks, cols, band)
+        result[picks.start : picks.stop] = result[picks.start : picks.stop] + rest
+
+
+def finish(rows, cols, cells, inner, parts, outer, resid_in, sens, resid, comp, vol, result_v, sems):
+    depth = sens.shape[-1]
+    del resid_in
+    copies = [
+        pltpu.make_async_copy(outer.at[index], resid.at[:, row], sems.at[index])
+        for index, row in enumerate((0, rows - 1))
+    ]
+    for copy in copies:
+        copy.start()
+    half = depth // 2
+    line = jnp.sum(parts[...], axis=0, keepdims=True)
+    first = lax.broadcasted_iota(jnp.int32, (1, depth), 1) < half
+    compliance = jnp.sum(jnp.where(first, line, 0.0))
+    volume = jnp.sum(jnp.where(first, 0.0, line))
+    comp[0, 0] = compliance
+    vol[0, 0] = volume / cells
+    scale = cells / jnp.broadcast_to(compliance, (8, depth))
+    size = rows // 2
+    for start in range(0, rows, size):
+        for row in range(start, start + size):
             for block in range(cols // 8):
-                result_v[row, 8 * block : 8 * block + 8, :] = filter_row(near, row, block, lane) * scale
-        send(start, stop - start)
+                at = pl.ds(block * 8, 8)
+                result_v[row, at, :] = inner[row, at, :] * scale
+        at = pl.ds(start, size)
+        copies.append(pltpu.make_async_copy(result_v.at[at], sens.at[at], sems.at[len(copies)]))
+        copies[-1].start()
     for copy in copies:
         copy.wait()
 
@@ -885,15 +843,14 @@
     got_b = lax.ppermute(send_b, BOTH, pairs_xb)
     got_a = lax.ppermute(send_a, "gx", pairs_xa)
 
-    waves, inner, scaled, sums, resid, near, filtered, send_a, send_b = call(
+    waves, inner, scaled, sums, resid, send_a, send_b = call(
         functools.partial(late_elements, rows, cols),
         [f32(*v.shape) for v in (waves, inner, scaled, sums)]
-        + [f32(3, rows, cols, depth), f32(RADIUS + 1, rows + 2 * RADIUS, cols, depth), f32(rows, cols, depth)]
+        + [f32(3, rows, cols, depth)]
         + [f32(RADIUS, wide, depth)] * 2,
         [waves, inner, scaled, tail, dens, kind, edge_u, edge_f, edge_s, applied, inverse, sums],
         scratch=[
             vmem(6 * rows * HALO, depth),
-            vmem(FILTER_ROWS * cols, RADIUS * depth),
             pltpu.SemaphoreType.DMA((cols // HALO,)),
         ],
         out_places={4: pltpu.HBM},
@@ -911,19 +868,26 @@
     )
     parts = lax.all_to_all(parts, BOTH, 0, 0, tiled=True)
 
-    sens, resid, comp, volume, _ = call(
-        functools.partial(filter_rest, rows, cols, count_x, cells),
-        [f32(rows, cols, depth), f32(3, rows, cols, depth), f32(1, 1), f32(1, 1), f32(*near.shape)],
-        [near, filtered, final, before, more_a, more_b, parts, outer, resid],
+    filtered, = call(
+        functools.partial(filter_all, rows, cols, count_x),
+        [f32(rows, cols, depth)],
+        [scaled, final, before, more_a, more_b],
         scratch=[
+            vmem(RADIUS + 1, rows + 2 * RADIUS, cols, depth),
             vmem(2 * RADIUS, wide + HALO, depth),
-            vmem(rows, cols, depth),
-            pltpu.SemaphoreType.DMA((5,)),
+            vmem(FILTER_ROWS * cols, RADIUS * depth),
         ],
-        places={8: pltpu.HBM},
+        flops=80 * rows * cols * depth,
+    )
+    sens, resid, comp, volume = call(
+        functools.partial(finish, rows, cols, cells),
+        [f32(rows, cols, depth), f32(3, rows, cols, depth), f32(1, 1), f32(1, 1)],
+        [filtered, parts, outer, resid],
+        scratch=[vmem(rows, cols, depth), pltpu.SemaphoreType.DMA((4,))],
+        places={3: pltpu.HBM},
         out_places={0: pltpu.HBM, 1: pltpu.HBM, 2: pltpu.SMEM, 3: pltpu.SMEM},
-        flops=20 * rows * cols * depth,
-        aliases={0: 4, 8: 1},
+        flops=rows * cols * depth,
+        aliases={3: 1},
     )
     return (
         sens,

time: 32.4 us -> 32.1 us (level)
  waiting for transfers between devices: 7.07 us -> 5.98 us
  Pallas kernels: 11.3 us -> 12.2 us
    all_to_all x1, waiting for transfers between devices: 7.05 us -> 5.97 us  [on_device(): parts = lax.all_to_all(parts, BOTH, 0, 0, tiled=True)]
    pallas_call x7 -> x8, Pallas kernels: 11.3 us -> 12.2 us  [call(): pl.pallas_call(body, out_shape=[FULL(v.shape, v.dtype) for v in shapes],...]
  transfers between devices with their start and end apart: 7 -> 7, of which waited for: 1 -> 1; matrix products, arithmetic and copies ran while one was open for 0% -> 0% of each run, Pallas kernels for 25% -> 29%
where the time goes in v8:
time: 32.1 us; the launch traced here: 31.9 us
  starting transfers between devices  12.9 us (40%)
  Pallas kernels  12.2 us (38%)
  waiting for transfers between devices  5.98 us (19%)
  between operations  0.81 us (3%)
    pallas_call x8, Pallas kernels, call(): pl.pallas_call(body, out_shape=[FULL(v.shape, v.dtype) for v in shapes],...  12.2 us
    all_to_all x1, waiting for transfers between devices, on_device(): parts = lax.all_to_all(parts, BOTH, 0, 0, tiled=True)  5.97 us
    all_to_all x1, starting transfers between devices, on_device(): parts = lax.all_to_all(parts, BOTH, 0, 0, tiled=True)  4.76 us
    ppermute x1, starting transfers between devices, on_device(): more_a = lax.ppermute(send_a, 'gx', pairs_xa)  3.1 us
    ppermute x1, starting transfers between devices, on_device(): got_b = lax.ppermute(send_b, BOTH, pairs_yb)  2.59 us
    ppermute x1, starting transfers between devices, on_device(): got_a = lax.ppermute(send_a, 'gx', pairs_xa)  1.92 us
  transfers between devices with their start and end apart: 7, of which 1 were waited for; matrix products, arithmetic and copies ran while one was open for 0% of the time, Pallas kernels for 29%

profile of v8, /device:TPU:0, one launch (start us, length us, event | category | flops | bytes accessed | tf_op | source)
XLA Modules:
  0.0 31.9 jit_solution(11036787120841849891)
XLA Ops:
  0.6 0.0 copy-start.7
  0.7 1.3 %shard_map.111 = (f32[480,128]{1,0:T(8,128)S(1)}, f32[480,128]{1,0:T(8,128)S(1)}, f32[8,128]{1,0:T(8,128)S(1)}) custom-call(f32[3,32,24,128]{3,2,1,0:T(8,128)} %disp.1, f32[32,24,128]{2,1,0:T(8,128)} %dens.1, s32[32,24,128]{2,1,0:T(8,128)} %kind.1), custom_call_target="tpu_custom_call" | custom-call | bytes 2461696 | tf_op jit(solution)/shard_map/pallas_call | solution.py:750
  2.0 0.5 %collective-permute-start = (f32[480,128]{1,0:T(8,128)S(1)}, f32[480,128]{1,0:T(8,128)S(1)}, u32[]{:S(2)}, u32[]{:S(2)}) collective-permute-start(f32[480,128]{1,0:T(8,128)S(1)} %get-tuple-element.42), channel_id=1, source_target_pairs={{0,1},{1,0},{2,3},{3,2},{4,5},{5,4},{6,7},{7,6},{8,9},{9,8},{10,11... | collective-permute-start | bytes 737288 | tf_op jit(solution)/shard_map/ppermute | solution.py:805
  2.5 2.6 %collective-permute-start.1 = (f32[480,128]{1,0:T(8,128)S(1)}, f32[480,128]{1,0:T(8,128)S(1)}, u32[]{:S(2)}, u32[]{:S(2)}) collective-permute-start(f32[480,128]{1,0:T(8,128)S(1)} %get-tuple-element.43), channel_id=1, source_target_pairs={{0,4},{1,2},{2,1},{3,7},{4,0},{5,6},{6,5},{7,3},{8,12},{9,10},{10,... | collective-permute-start | bytes 737288 | tf_op jit(solution)/shard_map/ppermute | solution.py:804
  5.2 0.0 copy-start
  5.2 0.0 copy-start.1
  5.2 0.0 copy-start.2
  5.2 1.5 %shard_map.112 = (f32[3,768,128]{2,1,0:T(8,128)S(1)}, f32[7,32,128]{2,1,0:T(8,128)S(1)}) custom-call(f32[8,128]{1,0:T(8,128)S(1)} %get-tuple-element.34.after, s32[1,1024]{1,0:T(1,128)S(1)} %bitcast.23, s32[1,1024]{1,0:T(1,128)S(1)} %bitcast.24, s32[1,1024]{1,0:T(1,128)S(1)} %bitcast.25, f32[3,1024]{1,0:T(4,128)S(1)} %copy-done.3, f32[8,128]{1,0:T(8,128)S(1)} %copy-done.7), custom_call_target="tpu_custom_call" | custom-call | flops 1207959552 | bytes 1327104 | tf_op jit(solution)/shard_map/pallas_call | solution.py:750
  6.8 2.7 %shard_map.113 = (f32[6,32,40,128]{3,2,1,0:T(8,128)S(1)}, f32[6,32,8,128]{3,2,1,0:T(8,128)S(1)}, f32[3,768,128]{2,1,0:T(8,128)S(1)}, f32[32,40,128]{2,1,0:T(8,128)S(1)}, f32[2,8,128]{2,1,0:T(8,128)S(1)}) custom-call(f32[2304,128]{1,0:T(8,128)S(1)} %bitcast.12, f32[768,128]{1,0:T(8,128)S(1)} %bitcast.14, s32[768,128]{1,0:T(8,128)S(1)} %bitcast.18, ...), custom_call_target="tpu_custom_call" | custom-call | flops 16384000 | bytes 9822208 | tf_op jit(solution)/shard_map/pallas_call | solution.py:750
  9.4 0.0 collective-permute-done.got_a
  9.5 0.0 collective-permute-done.1.got_b
  9.5 0.1 shard_map.114
  9.6 1.9 %collective-permute-start.2 = (f32[4,32,128]{2,1,0:T(8,128)S(1)}, f32[4,32,128]{2,1,0:T(8,128)S(1)}, u32[]{:S(2)}, u32[]{:S(2)}) collective-permute-start(f32[4,32,128]{2,1,0:T(8,128)S(1)} %get-tuple-element.49), channel_id=1, source_target_pairs={{0,4},{4,0},{8,12},{12,8},{16,20},{20,16},{24,28},{28,24},{1,5},{5... | collective-permute-start | bytes 196616 | tf_op jit(solution)/shard_map/ppermute | solution.py:844
  11.5 0.0 collective-permute-start.3
  11.5 2.9 %shard_map.115 = (f32[6,32,40,128]{3,2,1,0:T(8,128)S(1)}, f32[3,768,128]{2,1,0:T(8,128)S(1)}, f32[32,40,128]{2,1,0:T(8,128)S(1)}, f32[2,8,128]{2,1,0:T(8,128)S(1...) custom-call(f32[6,32,40,128]{3,2,1,0:T(8,128)S(1)} %get-tuple-elemen, ...), custom_call_target="tpu_custom_call", output_to_operand_aliasing={{0}: (0, {}), {1}: (1, {}), {2}: (2, {})} | custom-call | flops 16384000 | bytes 16351232 | tf_op jit(solution)/shard_map/pallas_call | solution.py:750
  14.5 3.1 %collective-permute-start.4 = (f32[3,32,128]{2,1,0:T(8,128)S(1)}, f32[3,32,128]{2,1,0:T(8,128)S(1)}, u32[]{:S(2)}, u32[]{:S(2)}) collective-permute-start(f32[3,32,128]{2,1,0:T(8,128)S(1)} %get-tuple-element.55), channel_id=1, source_target_pairs={{0,4},{4,0},{8,12},{12,8},{16,20},{20,16},{24,28},{28,24},{1,5},{5... | collective-permute-start | bytes 147464 | tf_op jit(solution)/shard_map/ppermute | solution.py:861
  17.6 0.0 collective-permute-start.5
  17.6 0.0 collective-permute-done.2.got_a
  17.6 1.0 %shard_map.116 = (f32[2,3,24,128]{3,2,1,0:T(8,128)S(1)}, f32[40,128]{1,0:T(8,128)S(1)}, f32[32,128]{1,0:T(8,128)S(1)}, f32[32,128]{1,0:T(8,128)}) custom-call(f32[6,32,40,128]{3,2,1,0:T(8,128)S(1)} %get-tuple-element.48.waves, f32[768,128]{1,0:T(8,128)S(1)} %bitcast.17, s32[768,128]{1,0:T(8,128)S(1)} %bitcast.21, f32[256,128]{1,0:T(8,128)S(1)} %get-tuple-element.45.edge_f, ...), custom_call_target="tpu_custom_call" | custom-call | flops 2048000 | bytes 6541312 | tf_op jit(solution)/shard_map/pallas_call | solution.py:750
  18.6 4.8 %all-to-all-start = ((f32[32,1,128]{2,1,0:T(1,128)}), f32[32,1,128]{2,1,0:T(1,128)S(1)}, u32[]{:S(2)}, u32[]{:S(2)}) async-start(f32[32,1,128]{2,1,0:T(1,128)} %bitcast.7), calls=%async_computation | async-start | bytes 32768 | tf_op jit(solution)/shard_map/all_to_all | solution.py:869
  23.4 0.0 collective-permute-done.5.got_b
  23.4 1.1 %shard_map.117.inner = f32[32,24,128]{2,1,0:T(8,128)S(1)} custom-call(f32[32,40,128]{2,1,0:T(8,128)S(1)} %get-tuple-element.47.scaled, f32[40,128]{1,0:T(8,128)S(1)} %get-tuple-element.53.final, f32[32,128]{1,0:T(8,128)S(1)} %get-tuple-element.54.before, f32[3,32,128]{2,1,0:T(8,128)S(1)} %collective-permute-done.4.got_a, ...), custom_call_target="tpu_custom_call" | custom-call | flops 7864320 | bytes 1183744 | tf_op jit(solution)/shard_map/pallas_call | solution.py:750
  24.5 6.0 %all-to-all-done = f32[32,1,128]{2,1,0:T(1,128)S(1)} async-done(((f32[32,1,128]{2,1,0:T(1,128)}), f32[32,1,128]{2,1,0:T(1,128)S(1)}, u32[]{:S(2)}, u32[]{:S(2)}) %all-to-all-start) | async-done | bytes 16416 | tf_op jit(solution)/shard_map/all_to_all | solution.py:869
  30.5 1.4 %shard_map.118 = (f32[32,24,128]{2,1,0:T(8,128)}, f32[3,32,24,128]{3,2,1,0:T(8,128)}, f32[1,1]{1,0:T(1,128)}, f32[1,1]{1,0:T(1,128)}) custom-call(f32[32,24,128]{2,1,0:T(8,128)S(1)} %shard_map.117.inner, f32[32,128]{1,0:T(8,128)S(1)} %bitcast.22, f32[2,3,24,128]{3,2,1,0:T(8,128)S(1)} %get-tuple-element.58.outer, ...), custom_call_target="tpu_custom_call", output_to_operand_aliasing={{1}: (3, {})} | custom-call | flops 98304 | bytes 3235848 | tf_op jit(solution)/shard_map/pallas_call | solution.py:750
  (14 shorter events, 0.0 us)
Async XLA Ops:
  0.6 4.5 %copy-start.7 = (f32[8,128]{1,0:T(8,128)S(1)}, f32[8,128]{1,0:T(8,128)}, u32[]{:S(2)}) copy-start(f32[8,128]{1,0:T(8,128)} %constant.2.clone.sums) | copy-start | bytes 12292
  0.6 4.5 %copy-start.3 = (f32[3,1024]{1,0:T(4,128)S(1)}, f32[3,1024]{1,0:T(4,128)}, u32[]{:S(2)}) copy-start(f32[3,1024]{1,0:T(4,128)} %force.1) | copy-start | bytes 36868
  0.7 4.5 %copy-start.6 = (s32[1024]{0:T(1024)S(1)}, s32[1024]{0:T(1024)}, u32[]{:S(2)}) copy-start(s32[1024]{0:T(1024)} %param.13) | copy-start | bytes 12292
  0.7 4.5 %copy-start.5 = (s32[1024]{0:T(1024)S(1)}, s32[1024]{0:T(1024)}, u32[]{:S(2)}) copy-start(s32[1024]{0:T(1024)} %param.12) | copy-start | bytes 12292
  0.7 4.5 %copy-start.4 = (s32[1024]{0:T(1024)S(1)}, s32[1024]{0:T(1024)}, u32[]{:S(2)}) copy-start(s32[1024]{0:T(1024)} %param.11) | copy-start | bytes 12292
  2.0 7.4 %collective-permute-start = (f32[480,128]{1,0:T(8,128)S(1)}, f32[480,128]{1,0:T(8,128)S(1)}, u32[]{:S(2)}, u32[]{:S(2)}) collective-permute-start(f32[480,128]{1,0:T(8,128)S(1)} %get-tuple-element.42), channel_id=1, source_target_pairs={{0,1},{1,0},{2,3},{3,2},{4,5},{5,4},{6,7},{7,6},{8,9},{9,8},{10,11... | collective-permute-start | bytes 737288 | tf_op jit(solution)/shard_map/ppermute | solution.py:805
  2.5 6.9 %collective-permute-start.1 = (f32[480,128]{1,0:T(8,128)S(1)}, f32[480,128]{1,0:T(8,128)S(1)}, u32[]{:S(2)}, u32[]{:S(2)}) collective-permute-start(f32[480,128]{1,0:T(8,128)S(1)} %get-tuple-element.43), channel_id=1, source_target_pairs={{0,4},{1,2},{2,1},{3,7},{4,0},{5,6},{6,5},{7,3},{8,12},{9,10},{10,... | collective-permute-start | bytes 737288 | tf_op jit(solution)/shard_map/ppermute | solution.py:804
  5.2 1.6 %copy-start = (f32[3,32,24,128]{3,2,1,0:T(8,128)S(1)}, f32[3,32,24,128]{3,2,1,0:T(8,128)}, u32[]{:S(2)}) copy-start(f32[3,32,24,128]{3,2,1,0:T(8,128)} %disp.1) | copy-start | bytes 3538948
  5.2 1.6 %copy-start.1 = (f32[32,24,128]{2,1,0:T(8,128)S(1)}, f32[32,24,128]{2,1,0:T(8,128)}, u32[]{:S(2)}) copy-start(f32[32,24,128]{2,1,0:T(8,128)} %dens.1) | copy-start | bytes 1179652
  5.2 1.6 %copy-start.2 = (s32[32,24,128]{2,1,0:T(8,128)S(1)}, s32[32,24,128]{2,1,0:T(8,128)}, u32[]{:S(2)}) copy-start(s32[32,24,128]{2,1,0:T(8,128)} %kind.1) | copy-start | bytes 1179652
  9.6 8.0 %collective-permute-start.2 = (f32[4,32,128]{2,1,0:T(8,128)S(1)}, f32[4,32,128]{2,1,0:T(8,128)S(1)}, u32[]{:S(2)}, u32[]{:S(2)}) collective-permute-start(f32[4,32,128]{2,1,0:T(8,128)S(1)} %get-tuple-element.49), channel_id=1, source_target_pairs={{0,4},{4,0},{8,12},{12,8},{16,20},{20,16},{24,28},{28,24},{1,5},{5... | collective-permute-start | bytes 196616 | tf_op jit(solution)/shard_map/ppermute | solution.py:844
  11.5 6.0 %collective-permute-start.3 = (f32[4,32,128]{2,1,0:T(8,128)S(1)}, f32[4,32,128]{2,1,0:T(8,128)S(1)}, u32[]{:S(2)}, u32[]{:S(2)}) collective-permute-start(f32[4,32,128]{2,1,0:T(8,128)S(1)} %get-tuple-element.50), channel_id=1, source_target_pairs={{0,1},{1,0},{2,3},{3,2},{4,8},{5,9},{6,10},{7,11},{8,4},{9,5},{10,... | collective-permute-start | bytes 196616 | tf_op jit(solution)/shard_map/ppermute | solution.py:843
  14.5 8.9 %collective-permute-start.4 = (f32[3,32,128]{2,1,0:T(8,128)S(1)}, f32[3,32,128]{2,1,0:T(8,128)S(1)}, u32[]{:S(2)}, u32[]{:S(2)}) collective-permute-start(f32[3,32,128]{2,1,0:T(8,128)S(1)} %get-tuple-element.55), channel_id=1, source_target_pairs={{0,4},{4,0},{8,12},{12,8},{16,20},{20,16},{24,28},{28,24},{1,5},{5... | collective-permute-start | bytes 147464 | tf_op jit(solution)/shard_map/ppermute | solution.py:861
  17.6 5.8 %collective-permute-start.5 = (f32[3,32,128]{2,1,0:T(8,128)S(1)}, f32[3,32,128]{2,1,0:T(8,128)S(1)}, u32[]{:S(2)}, u32[]{:S(2)}) collective-permute-start(f32[3,32,128]{2,1,0:T(8,128)S(1)} %get-tuple-element.56), channel_id=1, source_target_pairs={{0,1},{1,0},{2,3},{3,2},{4,8},{5,9},{6,10},{7,11},{8,4},{9,5},{10,... | collective-permute-start | bytes 147464 | tf_op jit(solution)/shard_map/ppermute | solution.py:860
  18.6 11.8 %all-to-all-start = ((f32[32,1,128]{2,1,0:T(1,128)}), f32[32,1,128]{2,1,0:T(1,128)S(1)}, u32[]{:S(2)}, u32[]{:S(2)}) async-start(f32[32,1,128]{2,1,0:T(1,128)} %bitcast.7), calls=%async_computation | async-start | bytes 32768 | tf_op jit(solution)/shard_map/all_to_all | solution.py:869

commit v9 on v8

--- a/solution.py
+++ b/solution.py
@@ -453,7 +453,7 @@
 def late_elements(
     rows, cols,
     waves_in, resid_in, scaled_in, tail, dens, kind, edge_u, edge_f, edge_s, applied, inverse, sums_a,
-    waves, resid, scaled, sums, resid_out, out_a, out_b, far_h, sems,
+    waves, resid, scaled, sums, out_a, out_b, far_h,
 ):
     depth = dens.shape[-1]
     del waves_in, resid_in, scaled_in
@@ -482,22 +482,11 @@
             far_h[pl.ds(pl.multiple_of((k * rows + row) * HALO, 8), HALO), :] = high[k]
 
     last = cols // 8 - 1
-    source = resid.reshape(3, rows, cols, depth)
-    copies = []
-
-    def send(block):
-        at = (slice(None), pl.ds(1, rows - 2), pl.ds(8 * block, 8), slice(None))
-        copies.append(pltpu.make_async_copy(source.at[at], resid_out.at[at], sems.at[block]))
-        copies[-1].start()
-
-    for block in range(1, last):
-        send(block)
     march(rows, cols // 8, waves, edge_state, inverse, emit_edge, put_edge, False)
     parts = [far_h[pl.ds(k * rows * HALO + HALO - 1, rows, stride=HALO), :] for k in range(6)]
     at = pl.ds(0, rows, stride=cols)
     for c, value in enumerate(along_z(parts, lax.broadcasted_iota(jnp.int32, (rows, depth), 1))):
         resid[c, at, :] = resid[c, at, :] - value
-    send(0)
 
     def put(row, value):
         scaled[row, cols:wide, :] = value
@@ -505,7 +494,6 @@
     emit = joiner(cols, last, tail, None, applied, resid)
     state = own_state(dens, kind, cols, 8 * last)
     total, filled = march(rows, last, waves, state, inverse, emit, put, True)
-    send(last)
     sums[0] = sums_a[0] + total
     sums[1] = sums_a[1] + filled
 
@@ -528,8 +516,6 @@
     @pl.when(odd == 1)
     def _():
         out(out_b, out_a)
-    for copy in copies:
-        copy.wait()
 
 
 def outer_elements(
@@ -673,9 +659,17 @@
     return total.reshape(len(picks), cols, depth)
 
 
-def filter_all(rows, cols, count_x, scaled, final, before, got_a, got_b, result, near, ends, lines):
+def filter_all(rows, cols, count_x, scaled, final, before, got_a, got_b, inner, outer, result, resid, near, ends, lines, sems):
     depth = result.shape[-1]
     wide = cols + HALO
+    middle = pl.ds(1, rows - 2)
+    copies = [
+        pltpu.make_async_copy(inner.reshape(3, rows, cols, depth).at[:, middle], resid.at[:, middle], sems.at[0]),
+        pltpu.make_async_copy(outer.at[0], resid.at[:, 0], sems.at[1]),
+        pltpu.make_async_copy(outer.at[1], resid.at[:, rows - 1], sems.at[2]),
+    ]
+    for copy in copies:
+        copy.start()
     here = lax.axis_index("gx")
     has_low = here > 0
     has_high = here < count_x - 1
@@ -710,17 +704,13 @@
         picks = range(start, min(start + FILTER_ROWS, rows))
         rest = filter_rows(near, lines, result, picks, cols, band)
         result[picks.start : picks.stop] = result[picks.start : picks.stop] + rest
-
-
-def finish(rows, cols, cells, inner, parts, outer, resid_in, sens, resid, comp, vol, result_v, sems):
+    for copy in copies:
+        copy.wait()
+
+
+def finish(rows, cols, cells, inner, parts, sens, comp, vol, result_v, sems):
     depth = sens.shape[-1]
-    del resid_in
-    copies = [
-        pltpu.make_async_copy(outer.at[index], resid.at[:, row], sems.at[index])
-        for index, row in enumerate((0, rows - 1))
-    ]
-    for copy in copies:
-        copy.start()
+    copies = []
     half = depth // 2
     line = jnp.sum(parts[...], axis=0, keepdims=True)
     first = lax.broadcasted_iota(jnp.int32, (1, depth), 1) < half
@@ -843,17 +833,12 @@
     got_b = lax.ppermute(send_b, BOTH, pairs_xb)
     got_a = lax.ppermute(send_a, "gx", pairs_xa)
 
-    waves, inner, scaled, sums, resid, send_a, send_b = call(
+    waves, inner, scaled, sums, send_a, send_b = call(
         functools.partial(late_elements, rows, cols),
         [f32(*v.shape) for v in (waves, inner, scaled, sums)]
-        + [f32(3, rows, cols, depth)]
         + [f32(RADIUS, wide, depth)] * 2,
         [waves, inner, scaled, tail, dens, kind, edge_u, edge_f, edge_s, applied, inverse, sums],
-        scratch=[
-            vmem(6 * rows * HALO, depth),
-            pltpu.SemaphoreType.DMA((cols // HALO,)),
-        ],
-        out_places={4: pltpu.HBM},
+        scratch=[vmem(6 * rows * HALO, depth)],
         flops=250 * rows * 2 * HALO * depth,
         aliases={0: 0, 1: 1, 2: 2},
     )
@@ -868,26 +853,26 @@
     )
     parts = lax.all_to_all(parts, BOTH, 0, 0, tiled=True)
 
-    filtered, = call(
+    filtered, resid = call(
         functools.partial(filter_all, rows, cols, count_x),
-        [f32(rows, cols, depth)],
-        [scaled, final, before, more_a, more_b],
+        [f32(rows, cols, depth), f32(3, rows, cols, depth)],
+        [scaled, final, before, more_a, more_b, inner, outer],
         scratch=[
             vmem(RADIUS + 1, rows + 2 * RADIUS, cols, depth),
             vmem(2 * RADIUS, wide + HALO, depth),
             vmem(FILTER_ROWS * cols, RADIUS * depth),
+            pltpu.SemaphoreType.DMA((3,)),
         ],
+        out_places={1: pltpu.HBM},
         flops=80 * rows * cols * depth,
     )
-    sens, resid, comp, volume = call(
+    sens, comp, volume = call(
         functools.partial(finish, rows, cols, cells),
-        [f32(rows, cols, depth), f32(3, rows, cols, depth), f32(1, 1), f32(1, 1)],
-        [filtered, parts, outer, resid],
-        scratch=[vmem(rows, cols, depth), pltpu.SemaphoreType.DMA((4,))],
-        places={3: pltpu.HBM},
-        out_places={0: pltpu.HBM, 1: pltpu.HBM, 2: pltpu.SMEM, 3: pltpu.SMEM},
+        [f32(rows, cols, depth), f32(1, 1), f32(1, 1)],
+        [filtered, parts],
+        scratch=[vmem(rows, cols, depth), pltpu.SemaphoreType.DMA((2,))],
+        out_places={0: pltpu.HBM, 1: pltpu.SMEM, 2: pltpu.SMEM},
         flops=rows * cols * depth,
-        aliases={3: 1},
     )
     return (
         sens,

time: 32.1 us -> 31.3 us (0.975)
  Pallas kernels: 12.2 us -> 11.5 us
    pallas_call x8, Pallas kernels: 12.2 us -> 11.5 us  [call(): pl.pallas_call(body, out_shape=[FULL(v.shape, v.dtype) for v in shapes],...]
  transfers between devices with their start and end apart: 7 -> 7, of which waited for: 1 -> 1; matrix products, arithmetic and copies ran while one was open for 0% -> 0% of each run, Pallas kernels for 29% -> 27%
where the time goes in v9:
time: 31.3 us; the launch traced here: 31.1 us
  starting transfers between devices  12.9 us (41%)
  Pallas kernels  11.5 us (37%)
  waiting for transfers between devices  5.94 us (19%)
  between operations  0.82 us (3%)
    pallas_call x8, Pallas kernels, call(): pl.pallas_call(body, out_shape=[FULL(v.shape, v.dtype) for v in shapes],...  11.5 us
    all_to_all x1, waiting for transfers between devices, on_device(): parts = lax.all_to_all(parts, BOTH, 0, 0, tiled=True)  5.92 us
    all_to_all x1, starting transfers between devices, on_device(): parts = lax.all_to_all(parts, BOTH, 0, 0, tiled=True)  4.76 us
    ppermute x1, starting transfers between devices, on_device(): more_a = lax.ppermute(send_a, 'gx', pairs_xa)  3.1 us
    ppermute x1, starting transfers between devices, on_device(): got_b = lax.ppermute(send_b, BOTH, pairs_yb)  2.59 us
    ppermute x1, starting transfers between devices, on_device(): got_a = lax.ppermute(send_a, 'gx', pairs_xa)  1.92 us
  transfers between devices with their start and end apart: 7, of which 1 were waited for; matrix products, arithmetic and copies ran while one was open for 0% of the time, Pallas kernels for 27%

profile of v9, /device:TPU:0, one launch (start us, length us, event | category | flops | bytes accessed | tf_op | source)
XLA Modules:
  0.0 31.1 jit_solution(17005799209425120650)
XLA Ops:
  0.6 0.0 copy-start.7
  0.7 1.3 %shard_map.111 = (f32[480,128]{1,0:T(8,128)S(1)}, f32[480,128]{1,0:T(8,128)S(1)}, f32[8,128]{1,0:T(8,128)S(1)}) custom-call(f32[3,32,24,128]{3,2,1,0:T(8,128)} %disp.1, f32[32,24,128]{2,1,0:T(8,128)} %dens.1, s32[32,24,128]{2,1,0:T(8,128)} %kind.1), custom_call_target="tpu_custom_call" | custom-call | bytes 2461696 | tf_op jit(solution)/shard_map/pallas_call | solution.py:740
  2.0 0.5 %collective-permute-start = (f32[480,128]{1,0:T(8,128)S(1)}, f32[480,128]{1,0:T(8,128)S(1)}, u32[]{:S(2)}, u32[]{:S(2)}) collective-permute-start(f32[480,128]{1,0:T(8,128)S(1)} %get-tuple-element.42), channel_id=1, source_target_pairs={{0,1},{1,0},{2,3},{3,2},{4,5},{5,4},{6,7},{7,6},{8,9},{9,8},{10,11... | collective-permute-start | bytes 737288 | tf_op jit(solution)/shard_map/ppermute | solution.py:795
  2.5 2.6 %collective-permute-start.1 = (f32[480,128]{1,0:T(8,128)S(1)}, f32[480,128]{1,0:T(8,128)S(1)}, u32[]{:S(2)}, u32[]{:S(2)}) collective-permute-start(f32[480,128]{1,0:T(8,128)S(1)} %get-tuple-element.43), channel_id=1, source_target_pairs={{0,4},{1,2},{2,1},{3,7},{4,0},{5,6},{6,5},{7,3},{8,12},{9,10},{10,... | collective-permute-start | bytes 737288 | tf_op jit(solution)/shard_map/ppermute | solution.py:794
  5.2 0.0 copy-start
  5.2 0.0 copy-start.1
  5.2 0.0 copy-start.2
  5.2 1.5 %shard_map.112 = (f32[3,768,128]{2,1,0:T(8,128)S(1)}, f32[7,32,128]{2,1,0:T(8,128)S(1)}) custom-call(f32[8,128]{1,0:T(8,128)S(1)} %get-tuple-element.34.after, s32[1,1024]{1,0:T(1,128)S(1)} %bitcast.23, s32[1,1024]{1,0:T(1,128)S(1)} %bitcast.24, s32[1,1024]{1,0:T(1,128)S(1)} %bitcast.25, f32[3,1024]{1,0:T(4,128)S(1)} %copy-done.3, f32[8,128]{1,0:T(8,128)S(1)} %copy-done.7), custom_call_target="tpu_custom_call" | custom-call | flops 1207959552 | bytes 1327104 | tf_op jit(solution)/shard_map/pallas_call | solution.py:740
  6.8 2.7 %shard_map.113 = (f32[6,32,40,128]{3,2,1,0:T(8,128)S(1)}, f32[6,32,8,128]{3,2,1,0:T(8,128)S(1)}, f32[3,768,128]{2,1,0:T(8,128)S(1)}, f32[32,40,128]{2,1,0:T(8,128)S(1)}, f32[2,8,128]{2,1,0:T(8,128)S(1)}) custom-call(f32[2304,128]{1,0:T(8,128)S(1)} %bitcast.12, f32[768,128]{1,0:T(8,128)S(1)} %bitcast.14, s32[768,128]{1,0:T(8,128)S(1)} %bitcast.18, ...), custom_call_target="tpu_custom_call" | custom-call | flops 16384000 | bytes 9822208 | tf_op jit(solution)/shard_map/pallas_call | solution.py:740
  9.4 0.0 collective-permute-done.got_a
  9.5 0.0 collective-permute-done.1.got_b
  9.5 0.1 shard_map.114
  9.6 1.9 %collective-permute-start.2 = (f32[4,32,128]{2,1,0:T(8,128)S(1)}, f32[4,32,128]{2,1,0:T(8,128)S(1)}, u32[]{:S(2)}, u32[]{:S(2)}) collective-permute-start(f32[4,32,128]{2,1,0:T(8,128)S(1)} %get-tuple-element.49), channel_id=1, source_target_pairs={{0,4},{4,0},{8,12},{12,8},{16,20},{20,16},{24,28},{28,24},{1,5},{5... | collective-permute-start | bytes 196616 | tf_op jit(solution)/shard_map/ppermute | solution.py:834
  11.5 0.0 collective-permute-start.3
  11.5 2.2 %shard_map.115 = (f32[6,32,40,128]{3,2,1,0:T(8,128)S(1)}, f32[3,768,128]{2,1,0:T(8,128)S(1)}, f32[32,40,128]{2,1,0:T(8,128)S(1)}, f32[2,8,128]{2,1,0:T(8,128)S(1...) custom-call(f32[6,32,40,128]{3,2,1,0:T(8,128)S(1)} %get-tuple-elemen, ...), custom_call_target="tpu_custom_call", output_to_operand_aliasing={{0}: (0, {}), {1}: (1, {}), {2}: (2, {})} | custom-call | flops 16384000 | bytes 15171584 | tf_op jit(solution)/shard_map/pallas_call | solution.py:740
  13.7 3.1 %collective-permute-start.4 = (f32[3,32,128]{2,1,0:T(8,128)S(1)}, f32[3,32,128]{2,1,0:T(8,128)S(1)}, u32[]{:S(2)}, u32[]{:S(2)}) collective-permute-start(f32[3,32,128]{2,1,0:T(8,128)S(1)} %get-tuple-element.55), channel_id=1, source_target_pairs={{0,4},{4,0},{8,12},{12,8},{16,20},{20,16},{24,28},{28,24},{1,5},{5... | collective-permute-start | bytes 147464 | tf_op jit(solution)/shard_map/ppermute | solution.py:846
  16.8 0.0 collective-permute-start.5
  16.8 0.0 collective-permute-done.2.got_a
  16.8 1.0 %shard_map.116 = (f32[2,3,24,128]{3,2,1,0:T(8,128)S(1)}, f32[40,128]{1,0:T(8,128)S(1)}, f32[32,128]{1,0:T(8,128)S(1)}, f32[32,128]{1,0:T(8,128)}) custom-call(f32[6,32,40,128]{3,2,1,0:T(8,128)S(1)} %get-tuple-element.48.waves, f32[768,128]{1,0:T(8,128)S(1)} %bitcast.17, s32[768,128]{1,0:T(8,128)S(1)} %bitcast.21, f32[256,128]{1,0:T(8,128)S(1)} %get-tuple-element.45.edge_f, ...), custom_call_target="tpu_custom_call" | custom-call | flops 2048000 | bytes 6541312 | tf_op jit(solution)/shard_map/pallas_call | solution.py:740
  17.9 4.8 %all-to-all-start = ((f32[32,1,128]{2,1,0:T(1,128)}), f32[32,1,128]{2,1,0:T(1,128)S(1)}, u32[]{:S(2)}, u32[]{:S(2)}) async-start(f32[32,1,128]{2,1,0:T(1,128)} %bitcast.7), calls=%async_computation | async-start | bytes 32768 | tf_op jit(solution)/shard_map/all_to_all | solution.py:854
  22.7 0.0 collective-permute-done.5.got_b
  22.7 1.1 %shard_map.117 = (f32[32,24,128]{2,1,0:T(8,128)S(1)}, f32[3,32,24,128]{3,2,1,0:T(8,128)}) custom-call(f32[32,40,128]{2,1,0:T(8,128)S(1)} %get-tuple-element.47.scaled, f32[40,128]{1,0:T(8,128)S(1)} %get-tuple-element.53.final, f32[32,128]{1,0:T(8,128)S(1)} %get-tuple-element.54.before, f32[3,32,128]{2,1,0:T(8,128)S(1)} %collective-permute-done.4.got_a, ...), custom_call_target="tpu_custom_call" | custom-call | flops 7864320 | bytes 3616768 | tf_op jit(solution)/shard_map/pallas_call | solution.py:740
  23.8 5.9 %all-to-all-done = f32[32,1,128]{2,1,0:T(1,128)S(1)} async-done(((f32[32,1,128]{2,1,0:T(1,128)}), f32[32,1,128]{2,1,0:T(1,128)S(1)}, u32[]{:S(2)}, u32[]{:S(2)}) %all-to-all-start) | async-done | bytes 16416 | tf_op jit(solution)/shard_map/all_to_all | solution.py:854
  29.7 1.4 %shard_map.118 = (f32[32,24,128]{2,1,0:T(8,128)}, f32[1,1]{1,0:T(1,128)}, f32[1,1]{1,0:T(1,128)}) custom-call(f32[32,24,128]{2,1,0:T(8,128)S(1)} %get-tuple-element.58.inner, f32[32,128]{1,0:T(8,128)S(1)} %bitcast.22), custom_call_target="tpu_custom_call" | custom-call | flops 98304 | bytes 802824 | tf_op jit(solution)/shard_map/pallas_call | solution.py:740
  (14 shorter events, 0.0 us)
Async XLA Ops:
  0.6 4.5 %copy-start.7 = (f32[8,128]{1,0:T(8,128)S(1)}, f32[8,128]{1,0:T(8,128)}, u32[]{:S(2)}) copy-start(f32[8,128]{1,0:T(8,128)} %constant.2.clone.sums) | copy-start | bytes 12292
  0.6 4.5 %copy-start.3 = (f32[3,1024]{1,0:T(4,128)S(1)}, f32[3,1024]{1,0:T(4,128)}, u32[]{:S(2)}) copy-start(f32[3,1024]{1,0:T(4,128)} %force.1) | copy-start | bytes 36868
  0.7 4.5 %copy-start.6 = (s32[1024]{0:T(1024)S(1)}, s32[1024]{0:T(1024)}, u32[]{:S(2)}) copy-start(s32[1024]{0:T(1024)} %param.13) | copy-start | bytes 12292
  0.7 4.5 %copy-start.5 = (s32[1024]{0:T(1024)S(1)}, s32[1024]{0:T(1024)}, u32[]{:S(2)}) copy-start(s32[1024]{0:T(1024)} %param.12) | copy-start | bytes 12292
  0.7 4.5 %copy-start.4 = (s32[1024]{0:T(1024)S(1)}, s32[1024]{0:T(1024)}, u32[]{:S(2)}) copy-start(s32[1024]{0:T(1024)} %param.11) | copy-start | bytes 12292
  2.0 7.4 %collective-permute-start = (f32[480,128]{1,0:T(8,128)S(1)}, f32[480,128]{1,0:T(8,128)S(1)}, u32[]{:S(2)}, u32[]{:S(2)}) collective-permute-start(f32[480,128]{1,0:T(8,128)S(1)} %get-tuple-element.42), channel_id=1, source_target_pairs={{0,1},{1,0},{2,3},{3,2},{4,5},{5,4},{6,7},{7,6},{8,9},{9,8},{10,11... | collective-permute-start | bytes 737288 | tf_op jit(solution)/shard_map/ppermute | solution.py:795
  2.5 6.9 %collective-permute-start.1 = (f32[480,128]{1,0:T(8,128)S(1)}, f32[480,128]{1,0:T(8,128)S(1)}, u32[]{:S(2)}, u32[]{:S(2)}) collective-permute-start(f32[480,128]{1,0:T(8,128)S(1)} %get-tuple-element.43), channel_id=1, source_target_pairs={{0,4},{1,2},{2,1},{3,7},{4,0},{5,6},{6,5},{7,3},{8,12},{9,10},{10,... | collective-permute-start | bytes 737288 | tf_op jit(solution)/shard_map/ppermute | solution.py:794
  5.2 1.6 %copy-start = (f32[3,32,24,128]{3,2,1,0:T(8,128)S(1)}, f32[3,32,24,128]{3,2,1,0:T(8,128)}, u32[]{:S(2)}) copy-start(f32[3,32,24,128]{3,2,1,0:T(8,128)} %disp.1) | copy-start | bytes 3538948
  5.2 1.6 %copy-start.1 = (f32[32,24,128]{2,1,0:T(8,128)S(1)}, f32[32,24,128]{2,1,0:T(8,128)}, u32[]{:S(2)}) copy-start(f32[32,24,128]{2,1,0:T(8,128)} %dens.1) | copy-start | bytes 1179652
  5.2 1.6 %copy-start.2 = (s32[32,24,128]{2,1,0:T(8,128)S(1)}, s32[32,24,128]{2,1,0:T(8,128)}, u32[]{:S(2)}) copy-start(s32[32,24,128]{2,1,0:T(8,128)} %kind.1) | copy-start | bytes 1179652
  9.6 7.2 %collective-permute-start.2 = (f32[4,32,128]{2,1,0:T(8,128)S(1)}, f32[4,32,128]{2,1,0:T(8,128)S(1)}, u32[]{:S(2)}, u32[]{:S(2)}) collective-permute-start(f32[4,32,128]{2,1,0:T(8,128)S(1)} %get-tuple-element.49), channel_id=1, source_target_pairs={{0,4},{4,0},{8,12},{12,8},{16,20},{20,16},{24,28},{28,24},{1,5},{5... | collective-permute-start | bytes 196616 | tf_op jit(solution)/shard_map/ppermute | solution.py:834
  11.5 5.3 %collective-permute-start.3 = (f32[4,32,128]{2,1,0:T(8,128)S(1)}, f32[4,32,128]{2,1,0:T(8,128)S(1)}, u32[]{:S(2)}, u32[]{:S(2)}) collective-permute-start(f32[4,32,128]{2,1,0:T(8,128)S(1)} %get-tuple-element.50), channel_id=1, source_target_pairs={{0,1},{1,0},{2,3},{3,2},{4,8},{5,9},{6,10},{7,11},{8,4},{9,5},{10,... | collective-permute-start | bytes 196616 | tf_op jit(solution)/shard_map/ppermute | solution.py:833
  13.7 8.9 %collective-permute-start.4 = (f32[3,32,128]{2,1,0:T(8,128)S(1)}, f32[3,32,128]{2,1,0:T(8,128)S(1)}, u32[]{:S(2)}, u32[]{:S(2)}) collective-permute-start(f32[3,32,128]{2,1,0:T(8,128)S(1)} %get-tuple-element.55), channel_id=1, source_target_pairs={{0,4},{4,0},{8,12},{12,8},{16,20},{20,16},{24,28},{28,24},{1,5},{5... | collective-permute-start | bytes 147464 | tf_op jit(solution)/shard_map/ppermute | solution.py:846
  16.8 5.8 %collective-permute-start.5 = (f32[3,32,128]{2,1,0:T(8,128)S(1)}, f32[3,32,128]{2,1,0:T(8,128)S(1)}, u32[]{:S(2)}, u32[]{:S(2)}) collective-permute-start(f32[3,32,128]{2,1,0:T(8,128)S(1)} %get-tuple-element.56), channel_id=1, source_target_pairs={{0,1},{1,0},{2,3},{3,2},{4,8},{5,9},{6,10},{7,11},{8,4},{9,5},{10,... | collective-permute-start | bytes 147464 | tf_op jit(solution)/shard_map/ppermute | solution.py:845
  17.9 11.8 %all-to-all-start = ((f32[32,1,128]{2,1,0:T(1,128)}), f32[32,1,128]{2,1,0:T(1,128)S(1)}, u32[]{:S(2)}, u32[]{:S(2)}) async-start(f32[32,1,128]{2,1,0:T(1,128)} %bitcast.7), calls=%async_computation | async-start | bytes 32768 | tf_op jit(solution)/shard_map/all_to_all | solution.py:854
